TPU v7x, 512 devices: a whole 4x4x16 slice. The times are simulated.
512 devices in a mesh: pop: 64 (over z, x), segment: 8 (over y, core).
Axes of the slice: x: 4, y: 4, z: 16, core: 2. Of those that a mesh axis runs over, the one named last changes fastest.
Arguments:
- block: bfloat16 [64, 4608], P('pop', 'segment'), may hold values from -6 to 6
- w_in: bfloat16 [3, 36864, 4608], P(None, 'pop', 'segment'), may hold values from -0.09375 to 0.09375
- w_out: bfloat16 [3, 36864, 4608], P(None, 'pop', 'segment'), may hold values from -0.03125 to 0.03125
- gains: float32 [3, 4608], P(None, 'segment'), may hold values from 0.5 to 1.5
- fac_left: bfloat16 [4, 4, 4, 4608], P(None, None, None, 'segment'), may hold values from -0.09375 to 0.09375
- right_perturb_factors: bfloat16 [4, 4, 4, 36864], P(None, None, None, 'pop'), may hold values from -1.796875 to 1.796875
- assign: int32 [3], replicated, may hold values from 0 to 3
Outputs:
- scores: float32 [3, 4], replicated
- final_member_activations: bfloat16 [64, 4, 4608], P('pop', None, 'segment')
All inputs are finite; a program needn't handle non-finite values.
Results may differ from a plain program's by a relative error of at most 0.017.
Values may be sent and summed in bfloat16 or wider, within the bound.
No kernel may reach another device: no remote copies, remote signals or barrier semaphores. Data moves between devices by JAX's collectives and lax.ppermute only.
A program may use at most 64 MiB of HBM per device.

v0:
```python
import math

import jax
import jax.numpy as jnp
from jax import lax
from jax.sharding import PartitionSpec as P

D = 4608


def from_behind(block, axis, distance):
    devices = range(lax.axis_size(axis))
    route = [(i - distance, i) for i in devices if i - distance in devices]
    return lax.ppermute(block, axis, route)


def square_total(values):
    wide = values.astype(jnp.float32)
    return lax.psum(jnp.sum(wide * wide, axis=-1), "segment")


def local(block, w_in, w_out, gains, fac_left, right_perturb_factors, assign):
    tok_local = block.shape[0]
    members = fac_left.shape[0]
    sections = fac_left.shape[1]
    layers = w_in.shape[0]
    total_tok = tok_local * lax.axis_size("pop")
    pop_pos = lax.axis_index("pop")
    following = from_behind(block, "pop", -1)
    target = jnp.concatenate([block[1:], following], axis=0).astype(jnp.float32)
    positions = (pop_pos * tok_local + jnp.arange(tok_local)).astype(jnp.float32)
    weighting = jnp.where(positions < total_tok - 1, 1.0 + 2.0 * positions / (total_tok - 2), 0.0)
    stream = jnp.broadcast_to(block[:, None, :], (tok_local, members, block.shape[1]))
    squared_entries = square_total(stream)
    partials = []
    for layer_pos in range(layers):
        member_picker = (jnp.arange(sections) == assign[layer_pos]).astype(jnp.float32)
        left_fac = jnp.einsum("s,msrd->mrd", member_picker, fac_left.astype(jnp.float32)).astype(
            jnp.bfloat16
        )
        right_factor_rows = jnp.einsum(
            "b,dbao->dao", member_picker, right_perturb_factors.astype(jnp.float32)
        )
        scale_rows = lax.rsqrt(squared_entries / D + 1e-06)
        normal = (stream.astype(jnp.float32) * scale_rows[..., None] * gains[layer_pos]).astype(
            jnp.bfloat16
        )
        low_part = jnp.einsum("tmd,mrd->tmr", normal, left_fac, preferred_element_type=jnp.float32)
        low_all = lax.all_gather(low_part, "pop", axis=0, tiled=True)
        weight_in = w_in[layer_pos]
        weight_out = w_out[layer_pos]
        pre_part = jnp.einsum(
            "tmd,fd->tmf",
            lax.all_gather(normal, "pop", axis=0, tiled=True),
            weight_in,
            preferred_element_type=jnp.float32,
        )
        hidden_preactivation, reduced_dimension = lax.psum((pre_part, low_all), "segment")
        blended_hidden = hidden_preactivation + jnp.einsum(
            "xwa,wan->xwn", reduced_dimension, right_factor_rows, precision=lax.Precision.HIGHEST
        )
        gated = jax.nn.silu(blended_hidden).astype(jnp.bfloat16)
        update = lax.psum_scatter(
            jnp.einsum("tmf,fd->tmd", gated, weight_out, preferred_element_type=jnp.float32),
            "pop",
            scatter_dimension=0,
            tiled=True,
        )
        stream = (stream.astype(jnp.float32) + update).astype(jnp.bfloat16)
        squared_entries = square_total(stream)
        probe = stream.astype(jnp.float32) * lax.rsqrt(squared_entries / D + 1e-06)[..., None]
        partials.append(jnp.einsum("tmd,td,t->m", probe, target, weighting))
    totals = lax.psum(jnp.stack(partials), ("pop", "segment"))
    return (totals / math.sqrt((total_tok - 1) * D), stream)


def solution(mesh):
    return jax.shard_map(
        local,
        mesh=mesh,
        in_specs=(
            P("pop", "segment"),
            P(None, "pop", "segment"),
            P(None, "pop", "segment"),
            P(None, "segment"),
            P(None, None, None, "segment"),
            P(None, None, None, "pop"),
            P(),
        ),
        out_specs=(P(), P("pop", None, "segment")),
        check_vma=False,
    )
```

profile of v0, /device:TPU:1, one launch (start us, length us, event | category | flops | bytes accessed | tf_op | source)
XLA Modules:
  0.0 1591.0 jit_solution(16435126958383159992)
XLA Ops:
  10.0 18.7 %psum.77 = f32[1,4]{1,0:T(1,128)S(1)} all-reduce(f32[1,4]{1,0:T(1,128)S(1)} %reduce_sum.45), channel_id=1, replica_groups=mesh['pop'=64,'segment'=8] {'segment'}, use_global_device_ids=true, to_apply=%region_1.2 | all-reduce | flops 4 | bytes 32 | tf_op jit(solution)/shard_map/psum | solution.py:19
  28.8 70.5 %all_gather.18 = bf16[64,4,576]{2,1,0:T(4,128)(2,1)S(1)} all-gather(bf16[1,4,576]{2,1,0:T(4,128)(2,1)S(1)} %multiply_convert_fusion.4), channel_id=1, replica_groups=mesh['pop'=64,'segment'=8] {'pop'}, dimensions={0}, use_global_device_ids=true | all-gather | bytes 299520 | tf_op jit(solution)/shard_map/all_gather | solution.py:54
  99.2 2.4 fusion.19
  103.4 73.9 %all-gather.3 = f32[64,4,4]{2,1,0:T(4,128)S(1)} all-gather(f32[1,4,4]{2,1,0:T(4,128)S(1)} %bitcast.162), channel_id=2, replica_groups=mesh['pop'=64,'segment'=8] {'pop'}, dimensions={0}, use_global_device_ids=true | all-gather | bytes 4160 | tf_op jit(solution)/shard_map/all_gather | solution.py:49
  177.4 63.2 %psum.79 = f32[64,4,4]{0,2,1:T(4,128)S(1)} all-reduce(f32[64,4,4]{0,2,1:T(4,128)S(1)} %copy.18), channel_id=1, replica_groups=mesh['pop'=64,'segment'=8] {'segment'}, use_global_device_ids=true, to_apply=%region_3.4 | all-reduce | flops 1024 | bytes 8192 | tf_op jit(solution)/shard_map/psum | solution.py:58
  241.4 1.9 multiply_convert_fusion.2
  243.4 1.7 fusion.17
  249.3 246.8 %all-reduce.16.cloned.1.call-done = f32[64,4,576]{2,1,0:T(4,128)} async-done(((f32[64,4,576]{2,1,0:T(4,128)}), f32[64,4,576]{2,1,0:T(4,128)}) %all-reduce.16.cloned.1.call-update) | async-done | bytes 589840
  497.6 22.4 %psum.80 = f32[1,4]{1,0:T(1,128)S(1)} all-reduce(f32[1,4]{1,0:T(1,128)S(1)} %bitcast.166), channel_id=1, replica_groups=mesh['pop'=64,'segment'=8] {'segment'}, use_global_device_ids=true, to_apply=%region_6.7 | all-reduce | flops 4 | bytes 32 | tf_op jit(solution)/shard_map/psum | solution.py:19
  520.1 67.8 %all_gather.20 = bf16[64,4,576]{2,1,0:T(4,128)(2,1)S(1)} all-gather(bf16[1,4,576]{2,1,0:T(4,128)(2,1)S(1)} %fusion.58), channel_id=1, replica_groups=mesh['pop'=64,'segment'=8] {'pop'}, dimensions={0}, use_global_device_ids=true | all-gather | bytes 299520 | tf_op jit(solution)/shard_map/all_gather | solution.py:54
  589.5 72.0 %all-gather.4 = f32[64,4,4]{2,1,0:T(4,128)S(1)} all-gather(f32[1,4,4]{2,1,0:T(4,128)S(1)} %bitcast.163), channel_id=3, replica_groups=mesh['pop'=64,'segment'=8] {'pop'}, dimensions={0}, use_global_device_ids=true | all-gather | bytes 4160 | tf_op jit(solution)/shard_map/all_gather | solution.py:49
  661.6 62.7 %psum.82 = f32[64,4,4]{0,2,1:T(4,128)S(1)} all-reduce(f32[64,4,4]{0,2,1:T(4,128)S(1)} %copy.21), channel_id=1, replica_groups=mesh['pop'=64,'segment'=8] {'segment'}, use_global_device_ids=true, to_apply=%region_8.9 | all-reduce | flops 1024 | bytes 8192 | tf_op jit(solution)/shard_map/psum | solution.py:58
  724.3 1.9 multiply_convert_fusion.1
  726.3 1.6 fusion.13
  730.9 247.1 %all-reduce.18.cloned.1.call-done = f32[64,4,576]{2,1,0:T(4,128)} async-done(((f32[64,4,576]{2,1,0:T(4,128)}), f32[64,4,576]{2,1,0:T(4,128)}) %all-reduce.18.cloned.1.call-update) | async-done | bytes 589840
  979.4 22.4 %psum.83 = f32[1,4]{1,0:T(1,128)S(1)} all-reduce(f32[1,4]{1,0:T(1,128)S(1)} %bitcast.167), channel_id=1, replica_groups=mesh['pop'=64,'segment'=8] {'segment'}, use_global_device_ids=true, to_apply=%region_11.12 | all-reduce | flops 4 | bytes 32 | tf_op jit(solution)/shard_map/psum | solution.py:19
  1001.9 67.8 %all_gather.22 = bf16[64,4,576]{2,1,0:T(4,128)(2,1)S(1)} all-gather(bf16[1,4,576]{2,1,0:T(4,128)(2,1)S(1)} %fusion.56), channel_id=1, replica_groups=mesh['pop'=64,'segment'=8] {'pop'}, dimensions={0}, use_global_device_ids=true | all-gather | bytes 299520 | tf_op jit(solution)/shard_map/all_gather | solution.py:54
  1071.3 71.5 %all-gather.5 = f32[64,4,4]{2,1,0:T(4,128)S(1)} all-gather(f32[1,4,4]{2,1,0:T(4,128)S(1)} %bitcast.164), channel_id=4, replica_groups=mesh['pop'=64,'segment'=8] {'pop'}, dimensions={0}, use_global_device_ids=true | all-gather | bytes 4160 | tf_op jit(solution)/shard_map/all_gather | solution.py:49
  1142.9 63.4 %psum.85 = f32[64,4,4]{0,2,1:T(4,128)S(1)} all-reduce(f32[64,4,4]{0,2,1:T(4,128)S(1)} %copy.24), channel_id=1, replica_groups=mesh['pop'=64,'segment'=8] {'segment'}, use_global_device_ids=true, to_apply=%region_13.14 | all-reduce | flops 1024 | bytes 8192 | tf_op jit(solution)/shard_map/psum | solution.py:58
  1206.3 1.9 multiply_convert_fusion
  1212.5 3.0 collective-permute-done
  1215.9 244.2 %all-reduce.20.cloned.1.call-done = f32[64,4,576]{2,1,0:T(4,128)} async-done(((f32[64,4,576]{2,1,0:T(4,128)}), f32[64,4,576]{2,1,0:T(4,128)}) %all-reduce.20.cloned.1.call-update) | async-done | bytes 589840
  1461.6 22.4 %psum.86 = f32[1,4]{1,0:T(1,128)S(1)} all-reduce(f32[1,4]{1,0:T(1,128)S(1)} %bitcast.165), channel_id=1, replica_groups=mesh['pop'=64,'segment'=8] {'segment'}, use_global_device_ids=true, to_apply=%region_16.17 | all-reduce | flops 4 | bytes 32 | tf_op jit(solution)/shard_map/psum | solution.py:19
  1484.2 99.4 %psum.87 = f32[3,4]{1,0:T(4,128)S(1)} all-reduce(f32[3,4]{1,0:T(4,128)S(1)} %pad_maximum_fusion), channel_id=1, replica_groups=mesh['pop'=64,'segment'=8] {'pop','segment'}, use_global_device_ids=true, to_apply=%region_17.18 | all-reduce | flops 12 | bytes 96 | tf_op jit(solution)/shard_map/psum | solution.py:73
  (70 shorter events, 26.1 us)
Async XLA Ops:
  7.2 95.3 %copy-start = (bf16[4,4,4,576]{3,2,1,0:T(4,128)(2,1)S(1)}, bf16[4,4,4,576]{3,2,1,0:T(4,128)(2,1)}, u32[]{:S(2)}) copy-start(bf16[4,4,4,576]{3,2,1,0:T(4,128)(2,1)} %param.11) | copy-start | bytes 221188
  7.2 94.6 %copy-start.3 = (s32[3]{0:T(128)S(1)}, s32[3]{0:T(128)}, u32[]{:S(2)}) copy-start(s32[3]{0:T(128)} %param.13) | copy-start | bytes 40
  7.2 233.4 %copy-start.5 = (bf16[4,4,4,576]{3,2,1,0:T(4,128)(2,1)S(1)}, bf16[4,4,4,576]{3,2,1,0:T(4,128)(2,1)}, u32[]{:S(2)}) copy-start(bf16[4,4,4,576]{3,2,1,0:T(4,128)(2,1)} %param.12) | copy-start | bytes 221188
  7.2 234.2 %all-reduce.10.cloned.1.call-start = ((), (), s32[]{:S(2)}) async-start(), calls=%async_computation | async-start | bytes 1310720 | tf_op jit(solution)/shard_map/psum | solution.py:58
  101.7 394.5 %all-reduce.16.cloned.1.call-start = ((), (), s32[]{:S(2)}) async-start(), calls=%async_computation.3 | async-start | bytes 1310720
  243.3 344.6 %copy-start.1 = (bf16[3,576,576]{2,1,0:T(8,128)(2,1)S(1)}, bf16[3,576,576]{2,1,0:T(8,128)(2,1)}, u32[]{:S(2)}) copy-start(bf16[3,576,576]{2,1,0:T(8,128)(2,1)} %param.8) | copy-start | bytes 5971972
  246.4 477.9 %all-reduce.12.cloned.1.call-start = ((), (), s32[]{:S(2)}) async-start(), calls=%async_computation.1 | async-start | bytes 1310720 | tf_op jit(solution)/shard_map/psum | solution.py:58
  589.3 388.7 %all-reduce.18.cloned.1.call-start = ((), (), s32[]{:S(2)}) async-start(), calls=%async_computation.4 | async-start | bytes 1310720
  729.2 477.2 %all-reduce.14.cloned.1.call-start = ((), (), s32[]{:S(2)}) async-start(), calls=%async_computation.2 | async-start | bytes 1310720 | tf_op jit(solution)/shard_map/psum | solution.py:58
  1071.1 389.0 %all-reduce.20.cloned.1.call-start = ((), (), s32[]{:S(2)}) async-start(), calls=%async_computation.5 | async-start | bytes 1310720
  1208.3 2.9 copy-start.4
  1211.2 4.3 collective-permute-start
  1461.6 122.6 %copy-start.2 = (bf16[1,4,576]{2,1,0:T(4,128)(2,1)}, bf16[1,4,576]{2,1,0:T(4,128)(2,1)S(1)}, u32[]{:S(2)}) copy-start(bf16[1,4,576]{2,1,0:T(4,128)(2,1)S(1)} %get-tuple-element.10) | copy-start | bytes 13828
Sparse Core Ops, SparseCore 0:
  101.8 95.7 all-reduce.9
  246.5 249.6 all-reduce.15
  589.4 92.4 all-reduce.11
  729.3 248.6 all-reduce.17
  1071.2 92.4 all-reduce.13
  1211.3 248.7 all-reduce.19
where the time goes:
time: 1590 us
  blocking collectives  798 us (50%)
  waiting for transfers between devices  741 us (47%)
  matrix products  21.5 us (1%)
    unnamed x9, waiting for transfers between devices  738 us
    all_gather x3, blocking collectives, local(): low_all = lax.all_gather(low_part, 'pop', axis=0, tiled=True)  217 us
    all_gather x3, blocking collectives, local(): lax.all_gather(normal, 'pop', axis=0, tiled=True)  206 us
    psum x3, blocking collectives, local(): lax.psum((pre_part, low_all), 'segment')  189 us
    psum x1, blocking collectives, local(): totals = lax.psum(jnp.stack(partials), ('pop', 'segment'))  99.4 us
    psum x4, blocking collectives, square_total(): return lax.psum(jnp.sum(wide * wide, axis=-1), 'segment')  85.8 us
  transfers between devices with their start and end apart: 7, of which 4 were waited for; matrix products, arithmetic and copies ran while one was open for 1% of the time, Pallas kernels for 0%

commit v1 on v0

v1 whole, which is shorter than its diff:
```python
import math

import jax
import jax.numpy as jnp
from jax import lax
from jax.sharding import Mesh, PartitionSpec as P

D = 4608
BF = jnp.bfloat16
F32 = jnp.float32
SEG = ("y", "c")
EPS = 1e-06


def swap(chunks, axes):
    return lax.all_to_all(chunks, axes, 0, 0, tiled=True)


def share(value, axes, count):
    return swap(jnp.broadcast_to(value[None], (count, *value.shape)), axes)


def split_pair(value):
    high = value.astype(BF)
    low = (value - high.astype(F32)).astype(BF)
    return high, low


def dot_t(a, b, precision=None):
    return lax.dot_general(
        a, b, (((1,), (1,)), ((), ())), preferred_element_type=F32, precision=precision
    )


def packed(hidden, *extras):
    high, low = split_pair(jnp.concatenate(extras, axis=1))
    pad = 64 - 2 * high.shape[1]
    return jnp.concatenate(
        [hidden.astype(BF), high, low, jnp.zeros((hidden.shape[0], pad), BF)], axis=1
    )


def unpacked(total, width, count):
    hidden = total[:, :width]
    extras = total[:, width : width + count] + total[:, width + count : width + 2 * count]
    return hidden, extras


def local(block, w_in, w_out, gains, fac_left, right_perturb_factors, assign):
    nz, nx = lax.axis_size("z"), lax.axis_size("x")
    ns = lax.axis_size("y") * lax.axis_size("c")
    width = block.shape[1]
    hid = w_in.shape[1]
    layers = w_in.shape[0]
    members, _, rank, _ = fac_left.shape
    tok = nz * nx
    rows = tok * members
    z, x = lax.axis_index("z"), lax.axis_index("x")
    seg = lax.axis_index("y") * lax.axis_size("c") + lax.axis_index("c")

    lefts = [
        jnp.take(fac_left, assign[i], axis=1).reshape(members * rank, width) for i in range(layers)
    ]
    rights = [
        jnp.take(right_perturb_factors, assign[i], axis=1).reshape(members * rank, hid).astype(F32)
        for i in range(layers)
    ]

    base = share(block[0], ("x", "z"), tok)
    natural = jnp.swapaxes(base.reshape(nx, nz, width), 0, 1).reshape(tok, width)
    after = jnp.concatenate([natural[1:], jnp.zeros((1, width), BF)], axis=0)
    after = jnp.swapaxes(after.reshape(nz, nx, width), 0, 1).reshape(tok, width)
    place = jnp.arange(tok)
    token = (place % nz) * nx + place // nz
    weighting = jnp.where(token < tok - 1, 1.0 + 2.0 * token.astype(F32) / (tok - 2), 0.0)
    target = jnp.repeat(after, members, axis=0).astype(F32)
    row_weight = jnp.repeat(weighting, members)
    row_member = jnp.arange(rows) % members
    pick = (row_member[:, None] == (jnp.arange(members * rank) // rank)[None]).astype(F32)
    chunk = rows // ns
    own_member = jnp.arange(chunk) % members
    own_weight = lax.dynamic_slice(row_weight, (seg * chunk,), (chunk,))
    to_member = (own_member[None] == jnp.arange(members)[:, None]).astype(F32)

    my_row = x * nz + z
    mine = jnp.broadcast_to(block, (members, width))
    scores = []
    stream = None
    for layer in range(layers):
        gain = gains[layer]
        if layer == 0:
            wide = base.astype(F32)
            scaled = (wide * gain).astype(BF)
            part = packed(
                dot_t(scaled, w_in[0]),
                dot_t(scaled, lefts[0]),
                jnp.sum(wide * wide, axis=1, keepdims=True),
            )
            parts = share(part, SEG, ns).reshape(ns, tok, -1)
            total = jnp.sum(parts.astype(F32), axis=0)
            hidden, extras = unpacked(total, hid, members * rank + 1)
            scale = lax.rsqrt(extras[:, -1:] / D + EPS)
            low = extras[:, :-1].reshape(tok, members, rank)
            mixed = scale[:, None] * (
                hidden[:, None]
                + jnp.einsum(
                    "tmr,mrf->tmf",
                    low,
                    rights[0].reshape(members, rank, hid),
                    precision=lax.Precision.HIGHEST,
                )
            )
            gated = jax.nn.silu(mixed).astype(BF).reshape(rows, hid)
        else:
            wide = stream.astype(F32)
            scaled = (wide * gain).astype(BF)
            part = packed(
                dot_t(scaled, w_in[layer]),
                dot_t(scaled, lefts[layer]) * pick,
                jnp.sum(wide * wide, axis=1, keepdims=True),
                jnp.sum(wide * target, axis=1, keepdims=True),
            )
            parts = swap(part, SEG).reshape(ns, chunk, -1)
            total = jnp.sum(parts.astype(F32), axis=0)
            hidden, extras = unpacked(total, hid, members * rank + 2)
            scale = lax.rsqrt(extras[:, -2:-1] / D + EPS)
            scores.append(jnp.sum(to_member * (extras[:, -1] * scale[:, 0] * own_weight), axis=1))
            low = jnp.dot(extras[:, :-2], rights[layer], precision=lax.Precision.HIGHEST)
            gated = jax.nn.silu(scale * (hidden + low)).astype(BF)
            gated = share(gated, SEG, ns).reshape(rows, hid)
        update = jnp.dot(gated, w_out[layer], preferred_element_type=F32).astype(BF)
        part = swap(update.reshape(nx, rows // nx, width), "x")
        part = jnp.sum(part.astype(F32), axis=0).astype(BF)
        part = swap(part.reshape(nz, members, width), "z")
        mine = (mine.astype(F32) + jnp.sum(part.astype(F32), axis=0)).astype(BF)
        if layer < layers - 1:
            stream = share(mine, "z", nz).reshape(nz * members, width)
            stream = share(stream, "x", nx).reshape(rows, width)

    wide = mine.astype(F32)
    my_target = lax.dynamic_slice(after, (my_row, 0), (1, width)).astype(F32)
    first = jnp.where((z == 0) & (x == 0), 1.0, 0.0)
    sums = jnp.concatenate(
        [
            jnp.sum(wide * wide, axis=1),
            jnp.sum(wide * my_target, axis=1),
            *[first * s for s in scores],
        ]
    )
    count = nx * ns
    got = share(sums, ("x", *SEG), count).reshape(nx, ns, -1)
    got = jnp.sum(got, axis=1)
    weights_x = lax.dynamic_slice(weighting.reshape(nx, nz), (0, z), (nx, 1))
    square, along = got[:, :members], got[:, members : 2 * members]
    last = jnp.sum(along * lax.rsqrt(square / D + EPS) * weights_x, axis=0)
    earlier = jnp.sum(got[:, 2 * members :], axis=0)
    both = jnp.concatenate([earlier, last])
    both = jnp.sum(share(both, "z", nz).reshape(nz, -1), axis=0)
    return both.reshape(layers, members) / math.sqrt((tok - 1) * D), mine[None]


def solution(mesh):
    split = Mesh(mesh.devices.reshape(16, 4, 4, 2), ("z", "x", "y", "c"))
    pop = ("z", "x")
    return jax.shard_map(
        local,
        mesh=split,
        in_specs=(
            P(pop, SEG),
            P(None, pop, SEG),
            P(None, pop, SEG),
            P(None, SEG),
            P(None, None, None, SEG),
            P(None, None, None, pop),
            P(),
        ),
        out_specs=(P(), P(pop, None, SEG)),
        check_vma=False,
    )
```

time: 1590 us -> 289 us (0.18)
  blocking collectives: 798 us -> 75.8 us
  waiting for transfers between devices: 741 us -> 95.6 us
  starting transfers between devices: 1.54 us -> 75.7 us
    unnamed x9 -> x0, waiting for transfers between devices: 738 us -> none
    all_gather x6 -> x0, blocking collectives: 423 us -> none  [the longest x3 217 us: local(): low_all = lax.all_gather(low_part, 'pop', axis=0, tiled=True)]
    psum x8 -> x0, blocking collectives: 374 us -> none  [the longest x3 189 us: local(): lax.psum((pre_part, low_all), 'segment')]
    all_to_all x0 -> x12, waiting for transfers between devices: none -> 95.6 us  [swap(): return lax.all_to_all(chunks, axes, 0, 0, tiled=True)]
    all_to_all x0 -> x6, blocking collectives: none -> 75.8 us  [swap(): return lax.all_to_all(chunks, axes, 0, 0, tiled=True)]
    all_to_all x0 -> x12, starting transfers between devices: none -> 75.7 us  [swap(): return lax.all_to_all(chunks, axes, 0, 0, tiled=True)]
  transfers between devices with their start and end apart: 7 -> 12, of which waited for: 4 -> 12; matrix products, arithmetic and copies ran while one was open for 1% -> 2% of each run, Pallas kernels for 0% -> 0%
where the time goes in v1:
time: 289 us; the launch traced here: 287 us
  waiting for transfers between devices  95.6 us (33%)
  blocking collectives  75.8 us (26%)
  starting transfers between devices  75.7 us (26%)
  local copies, waits for them, and re-layouts  15 us (5%)
  matrix products  11.5 us (4%)
  between operations  6.68 us (2%)
  other arithmetic  6.65 us (2%)
    all_to_all x12, waiting for transfers between devices, swap(): return lax.all_to_all(chunks, axes, 0, 0, tiled=True)  95.6 us
    all_to_all x6, blocking collectives, swap(): return lax.all_to_all(chunks, axes, 0, 0, tiled=True)  75.8 us
    all_to_all x12, starting transfers between devices, swap(): return lax.all_to_all(chunks, axes, 0, 0, tiled=True)  75.7 us
  transfers between devices with their start and end apart: 12, of which 12 were waited for; matrix products, arithmetic and copies ran while one was open for 2% of the time, Pallas kernels for 0%

profile of v1, /device:TPU:1, one launch (start us, length us, event | category | flops | bytes accessed | tf_op | source)
XLA Modules:
  0.0 286.9 jit_solution(11656243243673477249)
XLA Ops:
  3.8 19.1 %all-to-all-start = ((bf16[64,2,288]{2,1,0:T(2,128)(2,1)}), bf16[64,2,288]{2,1,0:T(2,128)(2,1)S(1)}, u32[]{:S(2)}, u32[]{:S(2)}) async-start(bf16[64,2,288]{2,1,0:T(2,128)(2,1)} %reshape.460), calls=%async_computation | async-start | bytes 196608 | tf_op jit(solution)/shard_map/all_to_all | solution.py:16
  31.7 5.1 %all-to-all-done = bf16[64,2,288]{2,1,0:T(2,128)(2,1)S(1)} async-done(((bf16[64,2,288]{2,1,0:T(2,128)(2,1)}), bf16[64,2,288]{2,1,0:T(2,128)(2,1)S(1)}, u32[]{:S(2)}, u32[]{:S(2)}) %all-to-all-start) | async-done | bytes 73760 | tf_op jit(solution)/shard_map/all_to_all | solution.py:16
  39.1 17.8 %all_to_all.101 = bf16[8,64,640]{2,1,0:T(8,128)(2,1)S(1)} all-to-all(bf16[8,64,640]{2,1,0:T(8,128)(2,1)S(1)} %broadcast_in_dim.124), channel_id=1, replica_groups=mesh['z'=16,'x'=4,'y'=4,'c'=2] {'y','c'}, dimensions={0} | all-to-all | bytes 1310720 | tf_op jit(solution)/shard_map/all_to_all | solution.py:16
  60.9 8.8 %all_to_all.102 = bf16[4,64,576]{2,1,0:T(8,128)(2,1)S(1)} all-to-all(bf16[4,64,576]{2,1,0:T(8,128)(2,1)S(1)} %bitcast.110), channel_id=1, replica_groups=mesh['z'=16,'x'=4,'y'=4,'c'=2] {'x'}, dimensions={0} | all-to-all | bytes 589824 | tf_op jit(solution)/shard_map/all_to_all | solution.py:16
  70.3 5.8 %all-to-all-start.3 = ((bf16[16,4,576]{2,1,0:T(4,128)(2,1)}), bf16[16,4,576]{2,1,0:T(4,128)(2,1)S(1)}, u32[]{:S(2)}, u32[]{:S(2)}) async-start(bf16[16,4,576]{2,1,0:T(4,128)(2,1)} %reshape.297), calls=%async_computation.3 | async-start | bytes 163840 | tf_op jit(solution)/shard_map/all_to_all | solution.py:16
  76.1 11.8 %all-to-all-done.3 = bf16[16,4,576]{2,1,0:T(4,128)(2,1)S(1)} async-done(((bf16[16,4,576]{2,1,0:T(4,128)(2,1)}), bf16[16,4,576]{2,1,0:T(4,128)(2,1)S(1)}, u32[]{:S(2)}, u32[]{:S(2)}) %all-to-all-start.3) | async-done | bytes 73760 | tf_op jit(solution)/shard_map/all_to_all | solution.py:16
  92.4 11.3 %all-to-all-done.4 = bf16[16,4,576]{2,1,0:T(4,128)(2,1)S(1)} async-done(((bf16[16,4,576]{2,1,0:T(4,128)(2,1)}), bf16[16,4,576]{2,1,0:T(4,128)(2,1)S(1)}, u32[]{:S(2)}, u32[]{:S(2)}) %all-to-all-start.4) | async-done | bytes 73760 | tf_op jit(solution)/shard_map/all_to_all | solution.py:16
  108.4 5.5 %all-to-all-done.5 = bf16[4,64,576]{2,1,0:T(8,128)(2,1)S(1)} async-done(((bf16[4,64,576]{2,1,0:T(8,128)(2,1)}), bf16[4,64,576]{2,1,0:T(8,128)(2,1)S(1)}, u32[]{:S(2)}, u32[]{:S(2)}) %all-to-all-start.5) | async-done | bytes 294944 | tf_op jit(solution)/shard_map/all_to_all | solution.py:16
  117.1 9.6 %all-to-all-start.6 = ((bf16[8,32,640]{2,1,0:T(8,128)(2,1)}), bf16[8,32,640]{2,1,0:T(8,128)(2,1)S(1)}, u32[]{:S(2)}, u32[]{:S(2)}) async-start(bf16[8,32,640]{2,1,0:T(8,128)(2,1)} %bitcast.17), calls=%async_computation.6 | async-start | bytes 655360 | tf_op jit(solution)/shard_map/all_to_all | solution.py:16
  126.8 7.1 %all-to-all-done.6 = bf16[8,32,640]{2,1,0:T(8,128)(2,1)S(1)} async-done(((bf16[8,32,640]{2,1,0:T(8,128)(2,1)}), bf16[8,32,640]{2,1,0:T(8,128)(2,1)S(1)}, u32[]{:S(2)}, u32[]{:S(2)}) %all-to-all-start.6) | async-done | bytes 327712 | tf_op jit(solution)/shard_map/all_to_all | solution.py:16
  134.4 11.0 %all_to_all.103 = bf16[8,32,576]{2,1,0:T(8,128)(2,1)S(1)} all-to-all(bf16[8,32,576]{2,1,0:T(8,128)(2,1)S(1)} %broadcast_in_dim.131), channel_id=1, replica_groups=mesh['z'=16,'x'=4,'y'=4,'c'=2] {'y','c'}, dimensions={0} | all-to-all | bytes 589824 | tf_op jit(solution)/shard_map/all_to_all | solution.py:16
  147.2 9.1 %all_to_all.104 = bf16[4,64,576]{2,1,0:T(8,128)(2,1)S(1)} all-to-all(bf16[4,64,576]{2,1,0:T(8,128)(2,1)S(1)} %bitcast.111), channel_id=1, replica_groups=mesh['z'=16,'x'=4,'y'=4,'c'=2] {'x'}, dimensions={0} | all-to-all | bytes 589824 | tf_op jit(solution)/shard_map/all_to_all | solution.py:16
  156.4 14.4 %all_to_all.105 = bf16[16,4,576]{2,1,0:T(4,128)(2,1)S(1)} all-to-all(bf16[16,4,576]{2,1,0:T(4,128)(2,1)S(1)} %reshape.306), channel_id=1, replica_groups=mesh['z'=16,'x'=4,'y'=4,'c'=2] {'z'}, dimensions={0} | all-to-all | bytes 147456 | tf_op jit(solution)/shard_map/all_to_all | solution.py:16
  170.9 14.8 %all_to_all.106 = bf16[16,4,576]{2,1,0:T(4,128)(2,1)S(1)} all-to-all(bf16[16,4,576]{2,1,0:T(4,128)(2,1)S(1)} %broadcast_in_dim.132), channel_id=1, replica_groups=mesh['z'=16,'x'=4,'y'=4,'c'=2] {'z'}, dimensions={0} | all-to-all | bytes 147456 | tf_op jit(solution)/shard_map/all_to_all | solution.py:16
  189.9 5.8 %all-to-all-done.11 = bf16[4,64,576]{2,1,0:T(8,128)(2,1)S(1)} async-done(((bf16[4,64,576]{2,1,0:T(8,128)(2,1)}), bf16[4,64,576]{2,1,0:T(8,128)(2,1)S(1)}, u32[]{:S(2)}, u32[]{:S(2)}) %all-to-all-start.11) | async-done | bytes 294944 | tf_op jit(solution)/shard_map/all_to_all | solution.py:16
  199.0 8.7 %all-to-all-start.12 = ((bf16[8,32,640]{2,1,0:T(8,128)(2,1)}), bf16[8,32,640]{2,1,0:T(8,128)(2,1)S(1)}, u32[]{:S(2)}, u32[]{:S(2)}) async-start(bf16[8,32,640]{2,1,0:T(8,128)(2,1)} %bitcast.26), calls=%async_computation.12 | async-start | bytes 655360 | tf_op jit(solution)/shard_map/all_to_all | solution.py:16
  207.7 7.1 %all-to-all-done.12 = bf16[8,32,640]{2,1,0:T(8,128)(2,1)S(1)} async-done(((bf16[8,32,640]{2,1,0:T(8,128)(2,1)}), bf16[8,32,640]{2,1,0:T(8,128)(2,1)S(1)}, u32[]{:S(2)}, u32[]{:S(2)}) %all-to-all-start.12) | async-done | bytes 327712 | tf_op jit(solution)/shard_map/all_to_all | solution.py:16
  216.0 4.5 %all-to-all-start.13 = ((bf16[8,32,576]{2,1,0:T(8,128)(2,1)}), bf16[8,32,576]{2,1,0:T(8,128)(2,1)S(1)}, u32[]{:S(2)}, u32[]{:S(2)}) async-start(bf16[8,32,576]{2,1,0:T(8,128)(2,1)} %broadcast_in_dim.137), calls=%async_computation.13 | async-start | bytes 655360 | tf_op jit(solution)/shard_map/all_to_all | solution.py:16
  220.8 6.9 %all-to-all-done.13 = bf16[8,32,576]{2,1,0:T(8,128)(2,1)S(1)} async-done(((bf16[8,32,576]{2,1,0:T(8,128)(2,1)}), bf16[8,32,576]{2,1,0:T(8,128)(2,1)S(1)}, u32[]{:S(2)}, u32[]{:S(2)}) %all-to-all-start.13) | async-done | bytes 294944 | tf_op jit(solution)/shard_map/all_to_all | solution.py:16
  233.8 5.7 %all-to-all-done.14 = bf16[4,64,576]{2,1,0:T(8,128)(2,1)S(1)} async-done(((bf16[4,64,576]{2,1,0:T(8,128)(2,1)}), bf16[4,64,576]{2,1,0:T(8,128)(2,1)S(1)}, u32[]{:S(2)}, u32[]{:S(2)}) %all-to-all-start.14) | async-done | bytes 294944 | tf_op jit(solution)/shard_map/all_to_all | solution.py:16
  243.8 11.7 %all-to-all-done.15 = bf16[16,4,576]{2,1,0:T(4,128)(2,1)S(1)} async-done(((bf16[16,4,576]{2,1,0:T(4,128)(2,1)}), bf16[16,4,576]{2,1,0:T(4,128)(2,1)S(1)}, u32[]{:S(2)}, u32[]{:S(2)}) %all-to-all-start.15) | async-done | bytes 73760 | tf_op jit(solution)/shard_map/all_to_all | solution.py:16
  256.3 7.2 %all-to-all-start.16 = ((f32[32,1,16]{2,1,0:T(1,128)}), f32[32,1,16]{2,1,0:T(1,128)S(1)}, u32[]{:S(2)}, u32[]{:S(2)}) async-start(f32[32,1,16]{2,1,0:T(1,128)} %broadcast_in_dim.140), calls=%async_computation.16 | async-start | bytes 32768 | tf_op jit(solution)/shard_map/all_to_all | solution.py:16
  263.6 7.0 %all-to-all-done.16 = f32[32,1,16]{2,1,0:T(1,128)S(1)} async-done(((f32[32,1,16]{2,1,0:T(1,128)}), f32[32,1,16]{2,1,0:T(1,128)S(1)}, u32[]{:S(2)}, u32[]{:S(2)}) %all-to-all-start.16) | async-done | bytes 2080 | tf_op jit(solution)/shard_map/all_to_all | solution.py:16
  275.6 10.6 %all-to-all-done.17 = f32[16,1,12]{2,1,0:T(1,128)S(1)} async-done(((f32[16,1,12]{2,1,0:T(1,128)}), f32[16,1,12]{2,1,0:T(1,128)S(1)}, u32[]{:S(2)}, u32[]{:S(2)}) %all-to-all-start.17) | async-done | bytes 800 | tf_op jit(solution)/shard_map/all_to_all | solution.py:16
  (128 shorter events, 54.0 us)
Async XLA Ops:
  3.8 32.9 %all-to-all-start = ((bf16[64,2,288]{2,1,0:T(2,128)(2,1)}), bf16[64,2,288]{2,1,0:T(2,128)(2,1)S(1)}, u32[]{:S(2)}, u32[]{:S(2)}) async-start(bf16[64,2,288]{2,1,0:T(2,128)(2,1)} %reshape.460), calls=%async_computation | async-start | bytes 196608 | tf_op jit(solution)/shard_map/all_to_all | solution.py:16
  70.3 17.6 %all-to-all-start.3 = ((bf16[16,4,576]{2,1,0:T(4,128)(2,1)}), bf16[16,4,576]{2,1,0:T(4,128)(2,1)S(1)}, u32[]{:S(2)}, u32[]{:S(2)}) async-start(bf16[16,4,576]{2,1,0:T(4,128)(2,1)} %reshape.297), calls=%async_computation.3 | async-start | bytes 163840 | tf_op jit(solution)/shard_map/all_to_all | solution.py:16
  88.6 15.1 %all-to-all-start.4 = ((bf16[16,4,576]{2,1,0:T(4,128)(2,1)}), bf16[16,4,576]{2,1,0:T(4,128)(2,1)S(1)}, u32[]{:S(2)}, u32[]{:S(2)}) async-start(bf16[16,4,576]{2,1,0:T(4,128)(2,1)} %broadcast_in_dim.125), calls=%async_computation.4 | async-start | bytes 163840 | tf_op jit(solution)/shard_map/all_to_all | solution.py:16
  104.5 9.3 %all-to-all-start.5 = ((bf16[4,64,576]{2,1,0:T(8,128)(2,1)}), bf16[4,64,576]{2,1,0:T(8,128)(2,1)S(1)}, u32[]{:S(2)}, u32[]{:S(2)}) async-start(bf16[4,64,576]{2,1,0:T(8,128)(2,1)} %broadcast_in_dim.127), calls=%async_computation.5 | async-start | bytes 655360 | tf_op jit(solution)/shard_map/all_to_all | solution.py:16
  117.1 16.8 %all-to-all-start.6 = ((bf16[8,32,640]{2,1,0:T(8,128)(2,1)}), bf16[8,32,640]{2,1,0:T(8,128)(2,1)S(1)}, u32[]{:S(2)}, u32[]{:S(2)}) async-start(bf16[8,32,640]{2,1,0:T(8,128)(2,1)} %bitcast.17), calls=%async_computation.6 | async-start | bytes 655360 | tf_op jit(solution)/shard_map/all_to_all | solution.py:16
  186.4 9.3 %all-to-all-start.11 = ((bf16[4,64,576]{2,1,0:T(8,128)(2,1)}), bf16[4,64,576]{2,1,0:T(8,128)(2,1)S(1)}, u32[]{:S(2)}, u32[]{:S(2)}) async-start(bf16[4,64,576]{2,1,0:T(8,128)(2,1)} %broadcast_in_dim.134), calls=%async_computation.11 | async-start | bytes 655360 | tf_op jit(solution)/shard_map/all_to_all | solution.py:16
  199.0 15.8 %all-to-all-start.12 = ((bf16[8,32,640]{2,1,0:T(8,128)(2,1)}), bf16[8,32,640]{2,1,0:T(8,128)(2,1)S(1)}, u32[]{:S(2)}, u32[]{:S(2)}) async-start(bf16[8,32,640]{2,1,0:T(8,128)(2,1)} %bitcast.26), calls=%async_computation.12 | async-start | bytes 655360 | tf_op jit(solution)/shard_map/all_to_all | solution.py:16
  216.0 11.6 %all-to-all-start.13 = ((bf16[8,32,576]{2,1,0:T(8,128)(2,1)}), bf16[8,32,576]{2,1,0:T(8,128)(2,1)S(1)}, u32[]{:S(2)}, u32[]{:S(2)}) async-start(bf16[8,32,576]{2,1,0:T(8,128)(2,1)} %broadcast_in_dim.137), calls=%async_computation.13 | async-start | bytes 655360 | tf_op jit(solution)/shard_map/all_to_all | solution.py:16
  230.1 9.4 %all-to-all-start.14 = ((bf16[4,64,576]{2,1,0:T(8,128)(2,1)}), bf16[4,64,576]{2,1,0:T(8,128)(2,1)S(1)}, u32[]{:S(2)}, u32[]{:S(2)}) async-start(bf16[4,64,576]{2,1,0:T(8,128)(2,1)} %bitcast.30), calls=%async_computation.14 | async-start | bytes 655360 | tf_op jit(solution)/shard_map/all_to_all | solution.py:16
  240.2 15.2 %all-to-all-start.15 = ((bf16[16,4,576]{2,1,0:T(4,128)(2,1)}), bf16[16,4,576]{2,1,0:T(4,128)(2,1)S(1)}, u32[]{:S(2)}, u32[]{:S(2)}) async-start(bf16[16,4,576]{2,1,0:T(4,128)(2,1)} %reshape.311), calls=%async_computation.15 | async-start | bytes 163840 | tf_op jit(solution)/shard_map/all_to_all | solution.py:16
  256.3 14.3 %all-to-all-start.16 = ((f32[32,1,16]{2,1,0:T(1,128)}), f32[32,1,16]{2,1,0:T(1,128)S(1)}, u32[]{:S(2)}, u32[]{:S(2)}) async-start(f32[32,1,16]{2,1,0:T(1,128)} %broadcast_in_dim.140), calls=%async_computation.16 | async-start | bytes 32768 | tf_op jit(solution)/shard_map/all_to_all | solution.py:16
  271.5 14.7 %all-to-all-start.17 = ((f32[16,1,12]{2,1,0:T(1,128)}), f32[16,1,12]{2,1,0:T(1,128)S(1)}, u32[]{:S(2)}, u32[]{:S(2)}) async-start(f32[16,1,12]{2,1,0:T(1,128)} %broadcast_in_dim.142), calls=%async_computation.17 | async-start | bytes 16384 | tf_op jit(solution)/shard_map/all_to_all | solution.py:16

commit v2 on v1

--- a/solution.py
+++ b/solution.py
@@ -34,7 +34,7 @@
 
 def packed(hidden, *extras):
     high, low = split_pair(jnp.concatenate(extras, axis=1))
-    pad = 64 - 2 * high.shape[1]
+    pad = -(hidden.shape[1] + 2 * high.shape[1]) % 128
     return jnp.concatenate(
         [hidden.astype(BF), high, low, jnp.zeros((hidden.shape[0], pad), BF)], axis=1
     )
@@ -54,35 +54,40 @@
     layers = w_in.shape[0]
     members, _, rank, _ = fac_left.shape
     tok = nz * nx
-    rows = tok * members
     z, x = lax.axis_index("z"), lax.axis_index("x")
     seg = lax.axis_index("y") * lax.axis_size("c") + lax.axis_index("c")
 
     lefts = [
         jnp.take(fac_left, assign[i], axis=1).reshape(members * rank, width) for i in range(layers)
     ]
+    near_in, near_out = [], []
+    for layer in range(1, layers):
+        near_in.append(lax.all_gather(w_in[layer], "x", axis=0, tiled=True))
+        near_out.append(lax.all_gather(w_out[layer], "x", axis=0, tiled=True))
     rights = [
-        jnp.take(right_perturb_factors, assign[i], axis=1).reshape(members * rank, hid).astype(F32)
+        jnp.take(right_perturb_factors, assign[i], axis=1).reshape(members * rank, hid)
         for i in range(layers)
     ]
 
     base = share(block[0], ("x", "z"), tok)
     natural = jnp.swapaxes(base.reshape(nx, nz, width), 0, 1).reshape(tok, width)
     after = jnp.concatenate([natural[1:], jnp.zeros((1, width), BF)], axis=0)
-    after = jnp.swapaxes(after.reshape(nz, nx, width), 0, 1).reshape(tok, width)
-    place = jnp.arange(tok)
-    token = (place % nz) * nx + place // nz
-    weighting = jnp.where(token < tok - 1, 1.0 + 2.0 * token.astype(F32) / (tok - 2), 0.0)
-    target = jnp.repeat(after, members, axis=0).astype(F32)
-    row_weight = jnp.repeat(weighting, members)
-    row_member = jnp.arange(rows) % members
+    near_after = lax.dynamic_slice(after.reshape(nz, nx, width), (0, x, 0), (nz, 1, width))
+    near_after = near_after.reshape(nz, width)
+    near_token = jnp.arange(nz) * nx + x
+    near_weight = jnp.where(
+        near_token < tok - 1, 1.0 + 2.0 * near_token.astype(F32) / (tok - 2), 0.0
+    )
+    near_rows = nz * members
+    target = jnp.repeat(near_after, members, axis=0).astype(F32)
+    row_weight = jnp.repeat(near_weight, members)
+    row_member = jnp.arange(near_rows) % members
     pick = (row_member[:, None] == (jnp.arange(members * rank) // rank)[None]).astype(F32)
-    chunk = rows // ns
+    chunk = near_rows // ns
     own_member = jnp.arange(chunk) % members
     own_weight = lax.dynamic_slice(row_weight, (seg * chunk,), (chunk,))
     to_member = (own_member[None] == jnp.arange(members)[:, None]).astype(F32)
 
-    my_row = x * nz + z
     mine = jnp.broadcast_to(block, (members, width))
     scores = []
     stream = None
@@ -101,45 +106,47 @@
             hidden, extras = unpacked(total, hid, members * rank + 1)
             scale = lax.rsqrt(extras[:, -1:] / D + EPS)
             low = extras[:, :-1].reshape(tok, members, rank)
+            right = rights[0].reshape(members, rank, hid).astype(F32)
             mixed = scale[:, None] * (
                 hidden[:, None]
-                + jnp.einsum(
-                    "tmr,mrf->tmf",
-                    low,
-                    rights[0].reshape(members, rank, hid),
-                    precision=lax.Precision.HIGHEST,
-                )
+                + jnp.einsum("tmr,mrf->tmf", low, right, precision=lax.Precision.HIGHEST)
             )
-            gated = jax.nn.silu(mixed).astype(BF).reshape(rows, hid)
+            gated = jax.nn.silu(mixed).astype(BF).reshape(tok * members, hid)
+            update = jnp.dot(gated, w_out[layer], preferred_element_type=F32).astype(BF)
+            later = jnp.concatenate(rights[1:], axis=0)
+            later = jnp.broadcast_to(later[None], (nx, *later.shape))
+            part = swap(jnp.concatenate([update.reshape(nx, near_rows, width), later], axis=1), "x")
+            later = jnp.swapaxes(part[:, near_rows:], 0, 1)
+            later = later.reshape(layers - 1, members * rank, nx * hid).astype(F32)
+            part = jnp.sum(part[:, :near_rows].astype(F32), axis=0).astype(BF)
         else:
             wide = stream.astype(F32)
             scaled = (wide * gain).astype(BF)
             part = packed(
-                dot_t(scaled, w_in[layer]),
+                dot_t(scaled, near_in[layer - 1]),
                 dot_t(scaled, lefts[layer]) * pick,
                 jnp.sum(wide * wide, axis=1, keepdims=True),
                 jnp.sum(wide * target, axis=1, keepdims=True),
             )
             parts = swap(part, SEG).reshape(ns, chunk, -1)
             total = jnp.sum(parts.astype(F32), axis=0)
-            hidden, extras = unpacked(total, hid, members * rank + 2)
+            hidden, extras = unpacked(total, nx * hid, members * rank + 2)
             scale = lax.rsqrt(extras[:, -2:-1] / D + EPS)
-            scores.append(jnp.sum(to_member * (extras[:, -1] * scale[:, 0] * own_weight), axis=1))
-            low = jnp.dot(extras[:, :-2], rights[layer], precision=lax.Precision.HIGHEST)
+            scores.append(
+                jnp.sum(to_member * (extras[:, -1] * scale[:, 0] * own_weight), axis=1)
+            )
+            low = jnp.dot(extras[:, :-2], later[layer - 1], precision=lax.Precision.HIGHEST)
             gated = jax.nn.silu(scale * (hidden + low)).astype(BF)
-            gated = share(gated, SEG, ns).reshape(rows, hid)
-        update = jnp.dot(gated, w_out[layer], preferred_element_type=F32).astype(BF)
-        part = swap(update.reshape(nx, rows // nx, width), "x")
-        part = jnp.sum(part.astype(F32), axis=0).astype(BF)
+            gated = share(gated, SEG, ns).reshape(near_rows, nx * hid)
+            part = jnp.dot(gated, near_out[layer - 1], preferred_element_type=F32).astype(BF)
         part = swap(part.reshape(nz, members, width), "z")
         mine = (mine.astype(F32) + jnp.sum(part.astype(F32), axis=0)).astype(BF)
         if layer < layers - 1:
-            stream = share(mine, "z", nz).reshape(nz * members, width)
-            stream = share(stream, "x", nx).reshape(rows, width)
+            stream = share(mine, "z", nz).reshape(near_rows, width)
 
     wide = mine.astype(F32)
-    my_target = lax.dynamic_slice(after, (my_row, 0), (1, width)).astype(F32)
-    first = jnp.where((z == 0) & (x == 0), 1.0, 0.0)
+    my_target = lax.dynamic_slice(near_after, (z, 0), (1, width)).astype(F32)
+    first = jnp.where(z == 0, 1.0, 0.0)
     sums = jnp.concatenate(
         [
             jnp.sum(wide * wide, axis=1),
@@ -150,9 +157,10 @@
     count = nx * ns
     got = share(sums, ("x", *SEG), count).reshape(nx, ns, -1)
     got = jnp.sum(got, axis=1)
-    weights_x = lax.dynamic_slice(weighting.reshape(nx, nz), (0, z), (nx, 1))
+    tokens = z * nx + jnp.arange(nx)
+    weights = jnp.where(tokens < tok - 1, 1.0 + 2.0 * tokens.astype(F32) / (tok - 2), 0.0)
     square, along = got[:, :members], got[:, members : 2 * members]
-    last = jnp.sum(along * lax.rsqrt(square / D + EPS) * weights_x, axis=0)
+    last = jnp.sum(along * lax.rsqrt(square / D + EPS) * weights[:, None], axis=0)
     earlier = jnp.sum(got[:, 2 * members :], axis=0)
     both = jnp.concatenate([earlier, last])
     both = jnp.sum(share(both, "z", nz).reshape(nz, -1), axis=0)

time: 289 us -> 273 us (0.945)
  blocking collectives: 75.8 us -> 24.8 us
  waiting for transfers between devices: 95.6 us -> 110 us
  between operations: 6.68 us -> 19.9 us
  starting transfers between devices: 75.7 us -> 80.6 us
    all_to_all x6 -> x2, blocking collectives: 75.8 us -> 24.8 us  [swap(): return lax.all_to_all(chunks, axes, 0, 0, tiled=True)]
    all_to_all x12, waiting for transfers between devices: 95.6 us -> 106 us  [swap(): return lax.all_to_all(chunks, axes, 0, 0, tiled=True)]
    all_to_all x12, starting transfers between devices: 75.7 us -> 80.5 us  [swap(): return lax.all_to_all(chunks, axes, 0, 0, tiled=True)]
    dot_general x3 -> x1, matrix products: 4.79 us -> 0.48 us  [local(): update = jnp.dot(gated, w_out[layer], preferred_element_type=F32).astype(BF)]
    dot_general x3 -> x5, matrix products: 1.71 us -> 5.93 us  [the longest x2 4.97 us: local(): jnp.dot(gated, near_out[layer - 1], preferred_element_type=F32).astype(BF)]
    slice x0 -> x5, local copies, waits for them, and re-layouts: none -> 4.14 us  [the longest x1 2.75 us: local(): near_in.append(lax.all_gather(w_in[layer], 'x', axis=0, tiled=True))]
  transfers between devices with their start and end apart: 12 -> 16, of which waited for: 12 -> 13; matrix products, arithmetic and copies ran while one was open for 2% -> 10% of each run, Pallas kernels for 0% -> 0%
where the time goes in v2:
time: 273 us; the launch traced here: 271 us
  waiting for transfers between devices  110 us (40%)
  starting transfers between devices  80.6 us (30%)
  blocking collectives  24.8 us (9%)
  between operations  19.9 us (7%)
  local copies, waits for them, and re-layouts  17.4 us (6%)
  matrix products  13.9 us (5%)
  other arithmetic  4.68 us (2%)
    all_to_all x12, waiting for transfers between devices, swap(): return lax.all_to_all(chunks, axes, 0, 0, tiled=True)  106 us
    all_to_all x12, starting transfers between devices, swap(): return lax.all_to_all(chunks, axes, 0, 0, tiled=True)  80.5 us
    all_to_all x2, blocking collectives, swap(): return lax.all_to_all(chunks, axes, 0, 0, tiled=True)  24.8 us
    dot_general x6, matrix products, dot_t(): lax.dot_general(a, b, (((1,), (1,)), ((), ())), preferred_element_type=F3...  7.45 us
    broadcast_in_dim x9, local copies, waits for them, and re-layouts, share(): return swap(jnp.broadcast_to(value[None], (count, *value.shape)), axes)  5.52 us
  transfers between devices with their start and end apart: 16, of which 13 were waited for; matrix products, arithmetic and copies ran while one was open for 10% of the time, Pallas kernels for 0%

profile of v2, /device:TPU:1, one launch (start us, length us, event | category | flops | bytes accessed | tf_op | source)
XLA Modules:
  0.0 271.2 jit_solution(8603173974381024091)
XLA Ops:
  14.7 19.1 %all-to-all-start = ((bf16[64,2,288]{2,1,0:T(2,128)(2,1)}), bf16[64,2,288]{2,1,0:T(2,128)(2,1)S(1)}, u32[]{:S(2)}, u32[]{:S(2)}) async-start(bf16[64,2,288]{2,1,0:T(2,128)(2,1)} %reshape.458), calls=%async_computation | async-start | bytes 196608 | tf_op jit(solution)/shard_map/all_to_all | solution.py:16
  40.2 7.3 %all-to-all-done = bf16[64,2,288]{2,1,0:T(2,128)(2,1)S(1)} async-done(((bf16[64,2,288]{2,1,0:T(2,128)(2,1)}), bf16[64,2,288]{2,1,0:T(2,128)(2,1)S(1)}, u32[]{:S(2)}, u32[]{:S(2)}) %all-to-all-start) | async-done | bytes 73760 | tf_op jit(solution)/shard_map/all_to_all | solution.py:16
  50.7 7.1 %all-to-all-start.1 = ((bf16[8,64,640]{2,1,0:T(8,128)(2,1)}), bf16[8,64,640]{2,1,0:T(8,128)(2,1)S(1)}, u32[]{:S(2)}, u32[]{:S(2)}) async-start(bf16[8,64,640]{2,1,0:T(8,128)(2,1)} %broadcast_in_dim.62), calls=%async_computation.1 | async-start | bytes 1310720 | tf_op jit(solution)/shard_map/all_to_all | solution.py:16
  57.9 10.8 %all-to-all-done.1 = bf16[8,64,640]{2,1,0:T(8,128)(2,1)S(1)} async-done(((bf16[8,64,640]{2,1,0:T(8,128)(2,1)}), bf16[8,64,640]{2,1,0:T(8,128)(2,1)S(1)}, u32[]{:S(2)}, u32[]{:S(2)}) %all-to-all-start.1) | async-done | bytes 655392 | tf_op jit(solution)/shard_map/all_to_all | solution.py:16
  70.9 10.4 %all_to_all.81 = bf16[4,96,576]{2,1,0:T(8,128)(2,1)S(1)} all-to-all(bf16[4,96,576]{2,1,0:T(8,128)(2,1)S(1)} %pad_maximum_fusion), channel_id=1, replica_groups=mesh['z'=16,'x'=4,'y'=4,'c'=2] {'x'}, dimensions={0} | all-to-all | bytes 884736 | tf_op jit(solution)/shard_map/all_to_all | solution.py:16
  82.1 3.6 %all-to-all-start.3 = ((bf16[16,4,576]{2,1,0:T(4,128)(2,1)}), bf16[16,4,576]{2,1,0:T(4,128)(2,1)S(1)}, u32[]{:S(2)}, u32[]{:S(2)}) async-start(bf16[16,4,576]{2,1,0:T(4,128)(2,1)} %reshape.293), calls=%async_computation.3 | async-start | bytes 163840 | tf_op jit(solution)/shard_map/all_to_all | solution.py:16
  86.2 11.2 %all-to-all-done.3 = bf16[16,4,576]{2,1,0:T(4,128)(2,1)S(1)} async-done(((bf16[16,4,576]{2,1,0:T(4,128)(2,1)}), bf16[16,4,576]{2,1,0:T(4,128)(2,1)S(1)}, u32[]{:S(2)}, u32[]{:S(2)}) %all-to-all-start.3) | async-done | bytes 73760 | tf_op jit(solution)/shard_map/all_to_all | solution.py:16
  98.1 3.5 %all-to-all-start.4 = ((bf16[16,4,576]{2,1,0:T(4,128)(2,1)}), bf16[16,4,576]{2,1,0:T(4,128)(2,1)S(1)}, u32[]{:S(2)}, u32[]{:S(2)}) async-start(bf16[16,4,576]{2,1,0:T(4,128)(2,1)} %broadcast_in_dim.64), calls=%async_computation.4 | async-start | bytes 163840 | tf_op jit(solution)/shard_map/all_to_all | solution.py:16
  101.9 11.4 %all-to-all-done.4 = bf16[16,4,576]{2,1,0:T(4,128)(2,1)S(1)} async-done(((bf16[16,4,576]{2,1,0:T(4,128)(2,1)}), bf16[16,4,576]{2,1,0:T(4,128)(2,1)S(1)}, u32[]{:S(2)}, u32[]{:S(2)}) %all-to-all-start.4) | async-done | bytes 73760 | tf_op jit(solution)/shard_map/all_to_all | solution.py:16
  117.8 8.5 %all-to-all-start.5 = ((bf16[8,8,2432]{2,1,0:T(8,128)(2,1)}), bf16[8,8,2432]{2,1,0:T(8,128)(2,1)S(1)}, u32[]{:S(2)}, u32[]{:S(2)}) async-start(bf16[8,8,2432]{2,1,0:T(8,128)(2,1)} %bitcast.17), calls=%async_computation.5 | async-start | bytes 622592 | tf_op jit(solution)/shard_map/all_to_all | solution.py:16
  126.5 6.8 %all-to-all-done.5 = bf16[8,8,2432]{2,1,0:T(8,128)(2,1)S(1)} async-done(((bf16[8,8,2432]{2,1,0:T(8,128)(2,1)}), bf16[8,8,2432]{2,1,0:T(8,128)(2,1)S(1)}, u32[]{:S(2)}, u32[]{:S(2)}) %all-to-all-start.5) | async-done | bytes 311328 | tf_op jit(solution)/shard_map/all_to_all | solution.py:16
  134.6 4.4 %all-to-all-start.6 = ((bf16[8,8,2304]{2,1,0:T(8,128)(2,1)}), bf16[8,8,2304]{2,1,0:T(8,128)(2,1)S(1)}, u32[]{:S(2)}, u32[]{:S(2)}) async-start(bf16[8,8,2304]{2,1,0:T(8,128)(2,1)} %broadcast_in_dim.125), calls=%async_computation.6 | async-start | bytes 589824 | tf_op jit(solution)/shard_map/all_to_all | solution.py:16
  139.0 6.9 %all-to-all-done.6 = bf16[8,8,2304]{2,1,0:T(8,128)(2,1)S(1)} async-done(((bf16[8,8,2304]{2,1,0:T(8,128)(2,1)}), bf16[8,8,2304]{2,1,0:T(8,128)(2,1)S(1)}, u32[]{:S(2)}, u32[]{:S(2)}) %all-to-all-start.6) | async-done | bytes 294944 | tf_op jit(solution)/shard_map/all_to_all | solution.py:16
  148.4 14.4 %all_to_all.82 = bf16[16,4,576]{2,1,0:T(4,128)(2,1)S(1)} all-to-all(bf16[16,4,576]{2,1,0:T(4,128)(2,1)S(1)} %reshape.299), channel_id=1, replica_groups=mesh['z'=16,'x'=4,'y'=4,'c'=2] {'z'}, dimensions={0} | all-to-all | bytes 147456 | tf_op jit(solution)/shard_map/all_to_all | solution.py:16
  167.1 11.7 %all-to-all-done.8 = bf16[16,4,576]{2,1,0:T(4,128)(2,1)S(1)} async-done(((bf16[16,4,576]{2,1,0:T(4,128)(2,1)}), bf16[16,4,576]{2,1,0:T(4,128)(2,1)S(1)}, u32[]{:S(2)}, u32[]{:S(2)}) %all-to-all-start.8) | async-done | bytes 73760 | tf_op jit(solution)/shard_map/all_to_all | solution.py:16
  183.3 7.0 %all-to-all-start.9 = ((bf16[8,8,2432]{2,1,0:T(8,128)(2,1)}), bf16[8,8,2432]{2,1,0:T(8,128)(2,1)S(1)}, u32[]{:S(2)}, u32[]{:S(2)}) async-start(bf16[8,8,2432]{2,1,0:T(8,128)(2,1)} %bitcast.23), calls=%async_computation.9 | async-start | bytes 622592 | tf_op jit(solution)/shard_map/all_to_all | solution.py:16
  190.7 6.6 %all-to-all-done.9 = bf16[8,8,2432]{2,1,0:T(8,128)(2,1)S(1)} async-done(((bf16[8,8,2432]{2,1,0:T(8,128)(2,1)}), bf16[8,8,2432]{2,1,0:T(8,128)(2,1)S(1)}, u32[]{:S(2)}, u32[]{:S(2)}) %all-to-all-start.9) | async-done | bytes 311328 | tf_op jit(solution)/shard_map/all_to_all | solution.py:16
  198.6 4.4 %all-to-all-start.10 = ((bf16[8,8,2304]{2,1,0:T(8,128)(2,1)}), bf16[8,8,2304]{2,1,0:T(8,128)(2,1)S(1)}, u32[]{:S(2)}, u32[]{:S(2)}) async-start(bf16[8,8,2304]{2,1,0:T(8,128)(2,1)} %broadcast_in_dim.129), calls=%async_computation.10 | async-start | bytes 589824 | tf_op jit(solution)/shard_map/all_to_all | solution.py:16
  205.5 4.3 %all-to-all-done.10 = bf16[8,8,2304]{2,1,0:T(8,128)(2,1)S(1)} async-done(((bf16[8,8,2304]{2,1,0:T(8,128)(2,1)}), bf16[8,8,2304]{2,1,0:T(8,128)(2,1)S(1)}, u32[]{:S(2)}, u32[]{:S(2)}) %all-to-all-start.10) | async-done | bytes 294944 | tf_op jit(solution)/shard_map/all_to_all | solution.py:16
  212.9 7.7 %all-to-all-start.11 = ((bf16[16,4,576]{2,1,0:T(4,128)(2,1)}), bf16[16,4,576]{2,1,0:T(4,128)(2,1)S(1)}, u32[]{:S(2)}, u32[]{:S(2)}) async-start(bf16[16,4,576]{2,1,0:T(4,128)(2,1)} %reshape.302), calls=%async_computation.11 | async-start | bytes 163840 | tf_op jit(solution)/shard_map/all_to_all | solution.py:16
  220.7 11.8 %all-to-all-done.11 = bf16[16,4,576]{2,1,0:T(4,128)(2,1)S(1)} async-done(((bf16[16,4,576]{2,1,0:T(4,128)(2,1)}), bf16[16,4,576]{2,1,0:T(4,128)(2,1)S(1)}, u32[]{:S(2)}, u32[]{:S(2)}) %all-to-all-start.11) | async-done | bytes 73760 | tf_op jit(solution)/shard_map/all_to_all | solution.py:16
  233.3 8.1 %all-to-all-start.12 = ((f32[32,1,16]{2,1,0:T(1,128)}), f32[32,1,16]{2,1,0:T(1,128)S(1)}, u32[]{:S(2)}, u32[]{:S(2)}) async-start(f32[32,1,16]{2,1,0:T(1,128)} %broadcast_in_dim.132), calls=%async_computation.12 | async-start | bytes 32768 | tf_op jit(solution)/shard_map/all_to_all | solution.py:16
  241.4 6.9 %all-to-all-done.12 = f32[32,1,16]{2,1,0:T(1,128)S(1)} async-done(((f32[32,1,16]{2,1,0:T(1,128)}), f32[32,1,16]{2,1,0:T(1,128)S(1)}, u32[]{:S(2)}, u32[]{:S(2)}) %all-to-all-start.12) | async-done | bytes 2080 | tf_op jit(solution)/shard_map/all_to_all | solution.py:16
  253.4 10.6 %all-to-all-done.13 = f32[16,1,12]{2,1,0:T(1,128)S(1)} async-done(((f32[16,1,12]{2,1,0:T(1,128)}), f32[16,1,12]{2,1,0:T(1,128)S(1)}, u32[]{:S(2)}, u32[]{:S(2)}) %all-to-all-start.13) | async-done | bytes 800 | tf_op jit(solution)/shard_map/all_to_all | solution.py:16
  (151 shorter events, 46.7 us)
Async XLA Ops:
  7.2 2.9 %copy-start = (bf16[3,576,576]{2,1,0:T(8,128)(2,1)S(1)}, bf16[3,576,576]{2,1,0:T(8,128)(2,1)}, u32[]{:S(2)}) copy-start(bf16[3,576,576]{2,1,0:T(8,128)(2,1)} %param.11) | copy-start | bytes 5971972
  7.2 107.0 %all-gather.9.cloned.1.call-start = ((), (), s32[]{:S(2)}) async-start(), calls=%async_computation.14 | async-start | bytes 3686400 | tf_op jit(solution)/shard_map/all_gather | solution.py:65
  10.0 2.2 copy-start.5
  10.0 23.9 %copy-start.4 = (s32[3]{0:T(128)S(1)}, s32[3]{0:T(128)}, u32[]{:S(2)}) copy-start(s32[3]{0:T(128)} %param.15) | copy-start | bytes 40
  10.0 30.0 %copy-start.1 = (bf16[4,4,4,576]{3,2,1,0:T(4,128)(2,1)S(1)}, bf16[4,4,4,576]{3,2,1,0:T(4,128)(2,1)}, u32[]{:S(2)}) copy-start(bf16[4,4,4,576]{3,2,1,0:T(4,128)(2,1)} %param.13) | copy-start | bytes 221188
  10.0 30.0 %copy-start.2 = (bf16[4,4,4,576]{3,2,1,0:T(4,128)(2,1)S(1)}, bf16[4,4,4,576]{3,2,1,0:T(4,128)(2,1)}, u32[]{:S(2)}) copy-start(bf16[4,4,4,576]{3,2,1,0:T(4,128)(2,1)} %param.14) | copy-start | bytes 221188
  10.0 30.2 %copy-start.3 = (f32[3,576]{1,0:T(4,128)S(1)}, f32[3,576]{1,0:T(4,128)}, u32[]{:S(2)}) copy-start(f32[3,576]{1,0:T(4,128)} %param.12) | copy-start | bytes 20740
  10.0 129.0 %all-gather.11.cloned.1.call-start = ((), (), s32[]{:S(2)}) async-start(), calls=%async_computation.15 | async-start | bytes 3686400 | tf_op jit(solution)/shard_map/all_gather | solution.py:66
  11.4 168.3 %all-gather.13.cloned.1.call-start = ((), (), s32[]{:S(2)}) async-start(), calls=%async_computation.16 | async-start | bytes 3686400 | tf_op jit(solution)/shard_map/all_gather | solution.py:65
  14.7 32.9 %all-to-all-start = ((bf16[64,2,288]{2,1,0:T(2,128)(2,1)}), bf16[64,2,288]{2,1,0:T(2,128)(2,1)S(1)}, u32[]{:S(2)}, u32[]{:S(2)}) async-start(bf16[64,2,288]{2,1,0:T(2,128)(2,1)} %reshape.458), calls=%async_computation | async-start | bytes 196608 | tf_op jit(solution)/shard_map/all_to_all | solution.py:16
  50.7 18.0 %all-to-all-start.1 = ((bf16[8,64,640]{2,1,0:T(8,128)(2,1)}), bf16[8,64,640]{2,1,0:T(8,128)(2,1)S(1)}, u32[]{:S(2)}, u32[]{:S(2)}) async-start(bf16[8,64,640]{2,1,0:T(8,128)(2,1)} %broadcast_in_dim.62), calls=%async_computation.1 | async-start | bytes 1310720 | tf_op jit(solution)/shard_map/all_to_all | solution.py:16
  82.1 15.4 %all-to-all-start.3 = ((bf16[16,4,576]{2,1,0:T(4,128)(2,1)}), bf16[16,4,576]{2,1,0:T(4,128)(2,1)S(1)}, u32[]{:S(2)}, u32[]{:S(2)}) async-start(bf16[16,4,576]{2,1,0:T(4,128)(2,1)} %reshape.293), calls=%async_computation.3 | async-start | bytes 163840 | tf_op jit(solution)/shard_map/all_to_all | solution.py:16
  85.6 119.9 %all-gather.15.cloned.1.call-start = ((), (), s32[]{:S(2)}) async-start(), calls=%async_computation.17 | async-start | bytes 3686400 | tf_op jit(solution)/shard_map/all_gather | solution.py:66
  98.1 15.1 %all-to-all-start.4 = ((bf16[16,4,576]{2,1,0:T(4,128)(2,1)}), bf16[16,4,576]{2,1,0:T(4,128)(2,1)S(1)}, u32[]{:S(2)}, u32[]{:S(2)}) async-start(bf16[16,4,576]{2,1,0:T(4,128)(2,1)} %broadcast_in_dim.64), calls=%async_computation.4 | async-start | bytes 163840 | tf_op jit(solution)/shard_map/all_to_all | solution.py:16
  117.8 15.5 %all-to-all-start.5 = ((bf16[8,8,2432]{2,1,0:T(8,128)(2,1)}), bf16[8,8,2432]{2,1,0:T(8,128)(2,1)S(1)}, u32[]{:S(2)}, u32[]{:S(2)}) async-start(bf16[8,8,2432]{2,1,0:T(8,128)(2,1)} %bitcast.17), calls=%async_computation.5 | async-start | bytes 622592 | tf_op jit(solution)/shard_map/all_to_all | solution.py:16
  134.6 11.3 %all-to-all-start.6 = ((bf16[8,8,2304]{2,1,0:T(8,128)(2,1)}), bf16[8,8,2304]{2,1,0:T(8,128)(2,1)S(1)}, u32[]{:S(2)}, u32[]{:S(2)}) async-start(bf16[8,8,2304]{2,1,0:T(8,128)(2,1)} %broadcast_in_dim.125), calls=%async_computation.6 | async-start | bytes 589824 | tf_op jit(solution)/shard_map/all_to_all | solution.py:16
  163.6 15.2 %all-to-all-start.8 = ((bf16[16,4,576]{2,1,0:T(4,128)(2,1)}), bf16[16,4,576]{2,1,0:T(4,128)(2,1)S(1)}, u32[]{:S(2)}, u32[]{:S(2)}) async-start(bf16[16,4,576]{2,1,0:T(4,128)(2,1)} %broadcast_in_dim.126), calls=%async_computation.8 | async-start | bytes 163840 | tf_op jit(solution)/shard_map/all_to_all | solution.py:16
  183.3 14.0 %all-to-all-start.9 = ((bf16[8,8,2432]{2,1,0:T(8,128)(2,1)}), bf16[8,8,2432]{2,1,0:T(8,128)(2,1)S(1)}, u32[]{:S(2)}, u32[]{:S(2)}) async-start(bf16[8,8,2432]{2,1,0:T(8,128)(2,1)} %bitcast.23), calls=%async_computation.9 | async-start | bytes 622592 | tf_op jit(solution)/shard_map/all_to_all | solution.py:16
  198.6 11.2 %all-to-all-start.10 = ((bf16[8,8,2304]{2,1,0:T(8,128)(2,1)}), bf16[8,8,2304]{2,1,0:T(8,128)(2,1)S(1)}, u32[]{:S(2)}, u32[]{:S(2)}) async-start(bf16[8,8,2304]{2,1,0:T(8,128)(2,1)} %broadcast_in_dim.129), calls=%async_computation.10 | async-start | bytes 589824 | tf_op jit(solution)/shard_map/all_to_all | solution.py:16
  212.9 19.5 %all-to-all-start.11 = ((bf16[16,4,576]{2,1,0:T(4,128)(2,1)}), bf16[16,4,576]{2,1,0:T(4,128)(2,1)S(1)}, u32[]{:S(2)}, u32[]{:S(2)}) async-start(bf16[16,4,576]{2,1,0:T(4,128)(2,1)} %reshape.302), calls=%async_computation.11 | async-start | bytes 163840 | tf_op jit(solution)/shard_map/all_to_all | solution.py:16
  233.3 15.0 %all-to-all-start.12 = ((f32[32,1,16]{2,1,0:T(1,128)}), f32[32,1,16]{2,1,0:T(1,128)S(1)}, u32[]{:S(2)}, u32[]{:S(2)}) async-start(f32[32,1,16]{2,1,0:T(1,128)} %broadcast_in_dim.132), calls=%async_computation.12 | async-start | bytes 32768 | tf_op jit(solution)/shard_map/all_to_all | solution.py:16
  249.3 14.7 %all-to-all-start.13 = ((f32[16,1,12]{2,1,0:T(1,128)}), f32[16,1,12]{2,1,0:T(1,128)S(1)}, u32[]{:S(2)}, u32[]{:S(2)}) async-start(f32[16,1,12]{2,1,0:T(1,128)} %broadcast_in_dim.134), calls=%async_computation.13 | async-start | bytes 16384 | tf_op jit(solution)/shard_map/all_to_all | solution.py:16
Sparse Core Ops, SparseCore 0:
  10.1 51.9 all-gather.8
  64.2 45.5 all-gather.10
  111.9 45.7 all-gather.12
  159.7 45.8 all-gather.14

commit v3 on v2

--- a/solution.py
+++ b/solution.py
@@ -48,7 +48,8 @@
 
 def local(block, w_in, w_out, gains, fac_left, right_perturb_factors, assign):
     nz, nx = lax.axis_size("z"), lax.axis_size("x")
-    ns = lax.axis_size("y") * lax.axis_size("c")
+    ny = lax.axis_size("y")
+    ns = ny * lax.axis_size("c")
     width = block.shape[1]
     hid = w_in.shape[1]
     layers = w_in.shape[0]
@@ -60,17 +61,21 @@
     lefts = [
         jnp.take(fac_left, assign[i], axis=1).reshape(members * rank, width) for i in range(layers)
     ]
-    near_in, near_out = [], []
-    for layer in range(1, layers):
-        near_in.append(lax.all_gather(w_in[layer], "x", axis=0, tiled=True))
-        near_out.append(lax.all_gather(w_out[layer], "x", axis=0, tiled=True))
+    forth = [(i, (i + 1) % nx) for i in range(nx)]
+    back = [(i, (i - 1) % nx) for i in range(nx)]
+    flip = [(0, 1), (1, 0)]
+
     rights = [
         jnp.take(right_perturb_factors, assign[i], axis=1).reshape(members * rank, hid)
         for i in range(layers)
     ]
 
-    base = share(block[0], ("x", "z"), tok)
-    natural = jnp.swapaxes(base.reshape(nx, nz, width), 0, 1).reshape(tok, width)
+    in_far, out_far = w_in[1:], w_out[1:]
+    in_left = lax.ppermute(in_far, "x", forth)
+    in_right = lax.ppermute(in_far, "x", back)
+    base = share(share(block, "x", nx).reshape(nx, width), "z", nz)
+    natural = base.reshape(tok, width)
+    base = jnp.swapaxes(base, 0, 1).reshape(tok, width)
     after = jnp.concatenate([natural[1:], jnp.zeros((1, width), BF)], axis=0)
     near_after = lax.dynamic_slice(after.reshape(nz, nx, width), (0, x, 0), (nz, 1, width))
     near_after = near_after.reshape(nz, width)
@@ -101,8 +106,12 @@
                 dot_t(scaled, lefts[0]),
                 jnp.sum(wide * wide, axis=1, keepdims=True),
             )
-            parts = share(part, SEG, ns).reshape(ns, tok, -1)
-            total = jnp.sum(parts.astype(F32), axis=0)
+            both = part.astype(F32) + lax.ppermute(part, "c", flip).astype(F32)
+            part = packed(*unpacked(both, hid, members * rank + 1))
+            part, in_left, in_right = lax.optimization_barrier((part, in_left, in_right))
+            in_relay = lax.ppermute(in_left, "x", forth)
+            parts = share(part, "y", ny)
+            total = jnp.sum(parts.reshape(ny, tok, -1).astype(F32), axis=0)
             hidden, extras = unpacked(total, hid, members * rank + 1)
             scale = lax.rsqrt(extras[:, -1:] / D + EPS)
             low = extras[:, :-1].reshape(tok, members, rank)
@@ -113,17 +122,30 @@
             )
             gated = jax.nn.silu(mixed).astype(BF).reshape(tok * members, hid)
             update = jnp.dot(gated, w_out[layer], preferred_element_type=F32).astype(BF)
-            later = jnp.concatenate(rights[1:], axis=0)
-            later = jnp.broadcast_to(later[None], (nx, *later.shape))
-            part = swap(jnp.concatenate([update.reshape(nx, near_rows, width), later], axis=1), "x")
-            later = jnp.swapaxes(part[:, near_rows:], 0, 1)
-            later = later.reshape(layers - 1, members * rank, nx * hid).astype(F32)
+            sent = jnp.concatenate(rights[1:], axis=0)
+            sent = jnp.broadcast_to(sent[None], (nx, *sent.shape))
+            part = swap(jnp.concatenate([update.reshape(nx, near_rows, width), sent], axis=1), "x")
+            late = part[:, near_rows:].astype(F32)
+            late = [
+                sum(late[i] * ((x + step) % nx == i).astype(F32) for i in range(nx))
+                for step in (0, -1, 1, -2)
+            ]
+            later = jnp.concatenate(late, axis=1).reshape(layers - 1, members * rank, nx * hid)
             part = jnp.sum(part[:, :near_rows].astype(F32), axis=0).astype(BF)
+            part, out_far = lax.optimization_barrier((part, out_far))
+            out_left = lax.ppermute(out_far, "x", forth)
+            out_right = lax.ppermute(out_far, "x", back)
         else:
             wide = stream.astype(F32)
             scaled = (wide * gain).astype(BF)
             part = packed(
-                dot_t(scaled, near_in[layer - 1]),
+                jnp.concatenate(
+                    [
+                        dot_t(scaled, w[layer - 1])
+                        for w in (in_far, in_left, in_right, in_relay)
+                    ],
+                    axis=1,
+                ),
                 dot_t(scaled, lefts[layer]) * pick,
                 jnp.sum(wide * wide, axis=1, keepdims=True),
                 jnp.sum(wide * target, axis=1, keepdims=True),
@@ -138,11 +160,23 @@
             low = jnp.dot(extras[:, :-2], later[layer - 1], precision=lax.Precision.HIGHEST)
             gated = jax.nn.silu(scale * (hidden + low)).astype(BF)
             gated = share(gated, SEG, ns).reshape(near_rows, nx * hid)
-            part = jnp.dot(gated, near_out[layer - 1], preferred_element_type=F32).astype(BF)
+            part = sum(
+                jnp.dot(
+                    gated[:, i * hid : (i + 1) * hid],
+                    w[layer - 1],
+                    preferred_element_type=F32,
+                )
+                for i, w in enumerate((out_far, out_left, out_right, out_relay))
+            ).astype(BF)
         part = swap(part.reshape(nz, members, width), "z")
         mine = (mine.astype(F32) + jnp.sum(part.astype(F32), axis=0)).astype(BF)
         if layer < layers - 1:
             stream = share(mine, "z", nz).reshape(near_rows, width)
+            if layer == 0:
+                stream, out_left, out_right = lax.optimization_barrier(
+                    (stream, out_left, out_right)
+                )
+                out_relay = lax.ppermute(out_left, "x", forth)
 
     wide = mine.astype(F32)
     my_target = lax.dynamic_slice(near_after, (z, 0), (1, width)).astype(F32)

time: 273 us -> 322 us (1.18)
  starting transfers between devices: 80.6 us -> 103 us
  between operations: 19.9 us -> 7.39 us
  matrix products: 13.9 us -> 25.8 us
  waiting for transfers between devices: 110 us -> 121 us
  blocking collectives: 24.8 us -> 33.8 us
  other arithmetic: 4.68 us -> 9.76 us
    ppermute x0 -> x7, waiting for transfers between devices: none -> 29.6 us  [the longest x1 15.2 us: local(): out_relay = lax.ppermute(out_left, 'x', forth)]
    ppermute x0 -> x7, starting transfers between devices: none -> 21.6 us  [the longest x1 4.8 us: local(): both = part.astype(F32) + lax.ppermute(part, 'c', flip).astype(F32)]
    all_to_all x12 -> x13, waiting for transfers between devices: 106 us -> 91.6 us  [swap(): return lax.all_to_all(chunks, axes, 0, 0, tiled=True)]
    all_to_all x2, blocking collectives: 24.8 us -> 33.8 us  [swap(): return lax.all_to_all(chunks, axes, 0, 0, tiled=True)]
    dot_general x6 -> x12, matrix products: 7.45 us -> 15.5 us  [dot_t(): lax.dot_general(a, b, (((1,), (1,)), ((), ())), preferred_element_type=F3...]
    dot_general x2 -> x8, matrix products: 4.97 us -> 6.7 us  [local(): jnp.dot(gated[:, i * hid:(i + 1) * hid], w[layer - 1], preferred_element_...]
    all_to_all x12 -> x13, starting transfers between devices: 80.5 us -> 81 us  [swap(): return lax.all_to_all(chunks, axes, 0, 0, tiled=True)]
  transfers between devices with their start and end apart: 16 -> 20, of which waited for: 13 -> 15; matrix products, arithmetic and copies ran while one was open for 10% -> 8% of each run, Pallas kernels for 0% -> 0%
where the time goes in v3:
time: 322 us; the launch traced here: 320 us
  waiting for transfers between devices  121 us (38%)
  starting transfers between devices  103 us (32%)
  blocking collectives  33.8 us (10%)
  matrix products  25.8 us (8%)
  local copies, waits for them, and re-layouts  19.5 us (6%)
  other arithmetic  9.76 us (3%)
  between operations  7.39 us (2%)
    all_to_all x13, waiting for transfers between devices, swap(): return lax.all_to_all(chunks, axes, 0, 0, tiled=True)  91.6 us
    all_to_all x13, starting transfers between devices, swap(): return lax.all_to_all(chunks, axes, 0, 0, tiled=True)  81 us
    all_to_all x2, blocking collectives, swap(): return lax.all_to_all(chunks, axes, 0, 0, tiled=True)  33.8 us
    dot_general x12, matrix products, dot_t(): lax.dot_general(a, b, (((1,), (1,)), ((), ())), preferred_element_type=F3...  15.5 us
    ppermute x1, waiting for transfers between devices, local(): out_relay = lax.ppermute(out_left, 'x', forth)  15.2 us
    ppermute x1, waiting for transfers between devices, local(): in_relay = lax.ppermute(in_left, 'x', forth)  13.4 us
    dot_general x8, matrix products, local(): jnp.dot(gated[:, i * hid:(i + 1) * hid], w[layer - 1], preferred_element_...  6.7 us
  transfers between devices with their start and end apart: 20, of which 15 were waited for; matrix products, arithmetic and copies ran while one was open for 8% of the time, Pallas kernels for 0%

profile of v3, /device:TPU:1, one launch (start us, length us, event | category | flops | bytes accessed | tf_op | source)
XLA Modules:
  0.0 319.9 jit_solution(12199679356462372347)
XLA Ops:
  3.2 4.8 %all-to-all-start = ((bf16[4,2,288]{2,1,0:T(2,128)(2,1)}), bf16[4,2,288]{2,1,0:T(2,128)(2,1)S(1)}, u32[]{:S(2)}, u32[]{:S(2)}) async-start(bf16[4,2,288]{2,1,0:T(2,128)(2,1)} %reshape.560), calls=%async_computation | async-start | bytes 12288 | tf_op jit(solution)/shard_map/all_to_all | solution.py:16
  16.9 14.9 %all-to-all-start.1 = ((bf16[16,4,576]{2,1,0:T(4,128)(2,1)}), bf16[16,4,576]{2,1,0:T(4,128)(2,1)S(1)}, u32[]{:S(2)}, u32[]{:S(2)}) async-start(bf16[16,4,576]{2,1,0:T(4,128)(2,1)} %broadcast_in_dim.54), calls=%async_computation.1 | async-start | bytes 163840 | tf_op jit(solution)/shard_map/all_to_all | solution.py:16
  38.4 5.2 %all-to-all-done.1 = bf16[16,4,576]{2,1,0:T(4,128)(2,1)S(1)} async-done(((bf16[16,4,576]{2,1,0:T(4,128)(2,1)}), bf16[16,4,576]{2,1,0:T(4,128)(2,1)S(1)}, u32[]{:S(2)}, u32[]{:S(2)}) %all-to-all-start.1) | async-done | bytes 73760 | tf_op jit(solution)/shard_map/all_to_all | solution.py:16
  45.8 4.8 %collective-permute-start = (bf16[64,640]{1,0:T(8,128)(2,1)S(1)}, bf16[64,640]{1,0:T(8,128)(2,1)S(1)}, u32[]{:S(2)}, u32[]{:S(2)}) collective-permute-start(bf16[64,640]{1,0:T(8,128)(2,1)S(1)} %maximum_maximum_fusion), channel_id=1, source_target_pairs={{0,1},{1,0},{2,3},{3,2},{4,5},{5,4},{6,7},{7,6},{8,9},{9,8},{10,11... | collective-permute-start | bytes 245768 | tf_op jit(solution)/shard_map/ppermute | solution.py:109
  52.5 4.2 %all-to-all-start.2 = ((bf16[4,64,640]{2,1,0:T(8,128)(2,1)}), bf16[4,64,640]{2,1,0:T(8,128)(2,1)S(1)}, u32[]{:S(2)}, u32[]{:S(2)}) async-start(bf16[4,64,640]{2,1,0:T(8,128)(2,1)} %broadcast_in_dim.56), calls=%async_computation.2 | async-start | bytes 655360 | tf_op jit(solution)/shard_map/all_to_all | solution.py:16
  56.8 6.5 %all-to-all-done.2 = bf16[4,64,640]{2,1,0:T(8,128)(2,1)S(1)} async-done(((bf16[4,64,640]{2,1,0:T(8,128)(2,1)}), bf16[4,64,640]{2,1,0:T(8,128)(2,1)S(1)}, u32[]{:S(2)}, u32[]{:S(2)}) %all-to-all-start.2) | async-done | bytes 327712 | tf_op jit(solution)/shard_map/all_to_all | solution.py:16
  72.3 5.4 %all-to-all-done.3 = bf16[4,96,576]{2,1,0:T(8,128)(2,1)S(1)} async-done(((bf16[4,96,576]{2,1,0:T(8,128)(2,1)}), bf16[4,96,576]{2,1,0:T(8,128)(2,1)S(1)}, u32[]{:S(2)}, u32[]{:S(2)}) %all-to-all-start.3) | async-done | bytes 442400 | tf_op jit(solution)/shard_map/all_to_all | solution.py:16
  79.9 4.3 %collective-permute-start.4 = (bf16[2,576,576]{2,1,0:T(8,128)(2,1)S(1)}, bf16[2,576,576]{2,1,0:T(8,128)(2,1)}, u32[]{:S(2)}, u32[]{:S(2)}) collective-permute-start(bf16[2,576,576]{2,1,0:T(8,128)(2,1)S(1)} %slice.234), channel_id=1, source_target_pairs={{0,24},{8,0},{16,8},{24,16},{1,25},{9,1},{17,9},{25,17},{2,26},{10... | collective-permute-start | bytes 3981320 | tf_op jit(solution)/shard_map/ppermute | solution.py:137
  84.9 10.1 %all-to-all-start.4 = ((bf16[16,4,576]{2,1,0:T(4,128)(2,1)}), bf16[16,4,576]{2,1,0:T(4,128)(2,1)S(1)}, u32[]{:S(2)}, u32[]{:S(2)}) async-start(bf16[16,4,576]{2,1,0:T(4,128)(2,1)} %reshape.393), calls=%async_computation.4 | async-start | bytes 163840 | tf_op jit(solution)/shard_map/all_to_all | solution.py:16
  95.4 11.4 %all-to-all-done.4 = bf16[16,4,576]{2,1,0:T(4,128)(2,1)S(1)} async-done(((bf16[16,4,576]{2,1,0:T(4,128)(2,1)}), bf16[16,4,576]{2,1,0:T(4,128)(2,1)S(1)}, u32[]{:S(2)}, u32[]{:S(2)}) %all-to-all-start.4) | async-done | bytes 73760 | tf_op jit(solution)/shard_map/all_to_all | solution.py:16
  113.2 9.5 %all-to-all-done.5 = bf16[16,4,576]{2,1,0:T(4,128)(2,1)S(1)} async-done(((bf16[16,4,576]{2,1,0:T(4,128)(2,1)}), bf16[16,4,576]{2,1,0:T(4,128)(2,1)S(1)}, u32[]{:S(2)}, u32[]{:S(2)}) %all-to-all-start.5) | async-done | bytes 73760 | tf_op jit(solution)/shard_map/all_to_all | solution.py:16
  128.0 13.4 %collective-permute-done.5 = bf16[2,576,576]{2,1,0:T(8,128)(2,1)} collective-permute-done((bf16[2,576,576]{2,1,0:T(8,128)(2,1)}, bf16[2,576,576]{2,1,0:T(8,128)(2,1)}, u32[]{:S(2)}, u32[]{:S(2)}) %collective-permute-start.5) | collective-permute-done | bytes 1327136 | tf_op jit(solution)/shard_map/ppermute | solution.py:112
  143.8 11.3 %all-to-all-start.6 = ((bf16[8,8,2432]{2,1,0:T(8,128)(2,1)}), bf16[8,8,2432]{2,1,0:T(8,128)(2,1)S(1)}, u32[]{:S(2)}, u32[]{:S(2)}) async-start(bf16[8,8,2432]{2,1,0:T(8,128)(2,1)} %concatenate.78), calls=%async_computation.6 | async-start | bytes 622592 | tf_op jit(solution)/shard_map/all_to_all | solution.py:16
  164.0 10.8 %all_to_all.79 = bf16[8,8,2304]{2,1,0:T(8,128)(2,1)S(1)} all-to-all(bf16[8,8,2304]{2,1,0:T(8,128)(2,1)S(1)} %broadcast_in_dim.60), channel_id=1, replica_groups=mesh['z'=16,'x'=4,'y'=4,'c'=2] {'y','c'}, dimensions={0} | all-to-all | bytes 589824 | tf_op jit(solution)/shard_map/all_to_all | solution.py:16
  177.9 15.2 %collective-permute-done.6 = bf16[2,576,576]{2,1,0:T(8,128)(2,1)S(1)} collective-permute-done((bf16[2,576,576]{2,1,0:T(8,128)(2,1)}, bf16[2,576,576]{2,1,0:T(8,128)(2,1)S(1)}, u32[]{:S(2)}, u32[]{:S(2)}) %collective-permute-start.6) | collective-permute-done | bytes 1327136 | tf_op jit(solution)/shard_map/ppermute | solution.py:179
  193.5 23.0 %all_to_all.80 = bf16[16,4,576]{2,1,0:T(4,128)(2,1)S(1)} all-to-all(bf16[16,4,576]{2,1,0:T(4,128)(2,1)S(1)} %reshape.399), channel_id=1, replica_groups=mesh['z'=16,'x'=4,'y'=4,'c'=2] {'z'}, dimensions={0} | all-to-all | bytes 147456 | tf_op jit(solution)/shard_map/all_to_all | solution.py:16
  221.3 11.8 %all-to-all-done.9 = bf16[16,4,576]{2,1,0:T(4,128)(2,1)S(1)} async-done(((bf16[16,4,576]{2,1,0:T(4,128)(2,1)}), bf16[16,4,576]{2,1,0:T(4,128)(2,1)S(1)}, u32[]{:S(2)}, u32[]{:S(2)}) %all-to-all-start.9) | async-done | bytes 73760 | tf_op jit(solution)/shard_map/all_to_all | solution.py:16
  243.6 7.3 %all-to-all-start.10 = ((bf16[8,8,2432]{2,1,0:T(8,128)(2,1)}), bf16[8,8,2432]{2,1,0:T(8,128)(2,1)S(1)}, u32[]{:S(2)}, u32[]{:S(2)}) async-start(bf16[8,8,2432]{2,1,0:T(8,128)(2,1)} %concatenate.84), calls=%async_computation.10 | async-start | bytes 622592 | tf_op jit(solution)/shard_map/all_to_all | solution.py:16
  259.2 4.4 %all-to-all-start.11 = ((bf16[8,8,2304]{2,1,0:T(8,128)(2,1)}), bf16[8,8,2304]{2,1,0:T(8,128)(2,1)S(1)}, u32[]{:S(2)}, u32[]{:S(2)}) async-start(bf16[8,8,2304]{2,1,0:T(8,128)(2,1)} %broadcast_in_dim.62), calls=%async_computation.11 | async-start | bytes 589824 | tf_op jit(solution)/shard_map/all_to_all | solution.py:16
  265.2 5.3 %all-to-all-done.11 = bf16[8,8,2304]{2,1,0:T(8,128)(2,1)S(1)} async-done(((bf16[8,8,2304]{2,1,0:T(8,128)(2,1)}), bf16[8,8,2304]{2,1,0:T(8,128)(2,1)S(1)}, u32[]{:S(2)}, u32[]{:S(2)}) %all-to-all-start.11) | async-done | bytes 294944 | tf_op jit(solution)/shard_map/all_to_all | solution.py:16
  278.1 11.6 %all-to-all-done.12 = bf16[16,4,576]{2,1,0:T(4,128)(2,1)S(1)} async-done(((bf16[16,4,576]{2,1,0:T(4,128)(2,1)}), bf16[16,4,576]{2,1,0:T(4,128)(2,1)S(1)}, u32[]{:S(2)}, u32[]{:S(2)}) %all-to-all-start.12) | async-done | bytes 73760 | tf_op jit(solution)/shard_map/all_to_all | solution.py:16
  290.6 5.9 %all-to-all-start.13 = ((f32[32,1,16]{2,1,0:T(1,128)}), f32[32,1,16]{2,1,0:T(1,128)S(1)}, u32[]{:S(2)}, u32[]{:S(2)}) async-start(f32[32,1,16]{2,1,0:T(1,128)} %broadcast_in_dim.66), calls=%async_computation.13 | async-start | bytes 32768 | tf_op jit(solution)/shard_map/all_to_all | solution.py:16
  296.6 7.0 %all-to-all-done.13 = f32[32,1,16]{2,1,0:T(1,128)S(1)} async-done(((f32[32,1,16]{2,1,0:T(1,128)}), f32[32,1,16]{2,1,0:T(1,128)S(1)}, u32[]{:S(2)}, u32[]{:S(2)}) %all-to-all-start.13) | async-done | bytes 2080 | tf_op jit(solution)/shard_map/all_to_all | solution.py:16
  308.6 10.6 %all-to-all-done.14 = f32[16,1,12]{2,1,0:T(1,128)S(1)} async-done(((f32[16,1,12]{2,1,0:T(1,128)}), f32[16,1,12]{2,1,0:T(1,128)S(1)}, u32[]{:S(2)}, u32[]{:S(2)}) %all-to-all-start.14) | async-done | bytes 800 | tf_op jit(solution)/shard_map/all_to_all | solution.py:16
  (190 shorter events, 93.6 us)
Async XLA Ops:
  3.2 12.9 %all-to-all-start = ((bf16[4,2,288]{2,1,0:T(2,128)(2,1)}), bf16[4,2,288]{2,1,0:T(2,128)(2,1)S(1)}, u32[]{:S(2)}, u32[]{:S(2)}) async-start(bf16[4,2,288]{2,1,0:T(2,128)(2,1)} %reshape.560), calls=%async_computation | async-start | bytes 12288 | tf_op jit(solution)/shard_map/all_to_all | solution.py:16
  9.6 42.1 %collective-permute-start.1 = (bf16[2,576,576]{2,1,0:T(8,128)(2,1)S(1)}, bf16[2,576,576]{2,1,0:T(8,128)(2,1)}, u32[]{:S(2)}, u32[]{:S(2)}) collective-permute-start(bf16[2,576,576]{2,1,0:T(8,128)(2,1)S(1)} %slice.224), channel_id=1, source_target_pairs={{0,8},{8,16},{16,24},{24,0},{1,9},{9,17},{17,25},{25,1},{2,10},{10... | collective-permute-start | bytes 3981320 | tf_op jit(solution)/shard_map/ppermute | solution.py:74
  13.0 38.8 %collective-permute-start.2 = (bf16[2,576,576]{2,1,0:T(8,128)(2,1)S(1)}, bf16[2,576,576]{2,1,0:T(8,128)(2,1)}, u32[]{:S(2)}, u32[]{:S(2)}) collective-permute-start(bf16[2,576,576]{2,1,0:T(8,128)(2,1)S(1)} %slice.224), channel_id=1, source_target_pairs={{0,24},{8,0},{16,8},{24,16},{1,25},{9,1},{17,9},{25,17},{2,26},{10... | collective-permute-start | bytes 3981320 | tf_op jit(solution)/shard_map/ppermute | solution.py:75
  16.9 26.7 %all-to-all-start.1 = ((bf16[16,4,576]{2,1,0:T(4,128)(2,1)}), bf16[16,4,576]{2,1,0:T(4,128)(2,1)S(1)}, u32[]{:S(2)}, u32[]{:S(2)}) async-start(bf16[16,4,576]{2,1,0:T(4,128)(2,1)} %broadcast_in_dim.54), calls=%async_computation.1 | async-start | bytes 163840 | tf_op jit(solution)/shard_map/all_to_all | solution.py:16
  45.8 5.7 %collective-permute-start = (bf16[64,640]{1,0:T(8,128)(2,1)S(1)}, bf16[64,640]{1,0:T(8,128)(2,1)S(1)}, u32[]{:S(2)}, u32[]{:S(2)}) collective-permute-start(bf16[64,640]{1,0:T(8,128)(2,1)S(1)} %maximum_maximum_fusion), channel_id=1, source_target_pairs={{0,1},{1,0},{2,3},{3,2},{4,5},{5,4},{6,7},{7,6},{8,9},{9,8},{10,11... | collective-permute-start | bytes 245768 | tf_op jit(solution)/shard_map/ppermute | solution.py:109
  52.5 10.7 %all-to-all-start.2 = ((bf16[4,64,640]{2,1,0:T(8,128)(2,1)}), bf16[4,64,640]{2,1,0:T(8,128)(2,1)S(1)}, u32[]{:S(2)}, u32[]{:S(2)}) async-start(bf16[4,64,640]{2,1,0:T(8,128)(2,1)} %broadcast_in_dim.56), calls=%async_computation.2 | async-start | bytes 655360 | tf_op jit(solution)/shard_map/all_to_all | solution.py:16
  67.3 10.4 %all-to-all-start.3 = ((bf16[4,96,576]{2,1,0:T(8,128)(2,1)}), bf16[4,96,576]{2,1,0:T(8,128)(2,1)S(1)}, u32[]{:S(2)}, u32[]{:S(2)}) async-start(bf16[4,96,576]{2,1,0:T(8,128)(2,1)} %pad_maximum_fusion), calls=%async_computation.3 | async-start | bytes 983040 | tf_op jit(solution)/shard_map/all_to_all | solution.py:16
  77.7 45.0 %collective-permute-start.3 = (bf16[2,576,576]{2,1,0:T(8,128)(2,1)S(1)}, bf16[2,576,576]{2,1,0:T(8,128)(2,1)}, u32[]{:S(2)}, u32[]{:S(2)}) collective-permute-start(bf16[2,576,576]{2,1,0:T(8,128)(2,1)S(1)} %slice.234), channel_id=1, source_target_pairs={{0,8},{8,16},{16,24},{24,0},{1,9},{9,17},{17,25},{25,1},{2,10},{10... | collective-permute-start | bytes 3981320 | tf_op jit(solution)/shard_map/ppermute | solution.py:136
  79.9 42.8 %collective-permute-start.4 = (bf16[2,576,576]{2,1,0:T(8,128)(2,1)S(1)}, bf16[2,576,576]{2,1,0:T(8,128)(2,1)}, u32[]{:S(2)}, u32[]{:S(2)}) collective-permute-start(bf16[2,576,576]{2,1,0:T(8,128)(2,1)S(1)} %slice.234), channel_id=1, source_target_pairs={{0,24},{8,0},{16,8},{24,16},{1,25},{9,1},{17,9},{25,17},{2,26},{10... | collective-permute-start | bytes 3981320 | tf_op jit(solution)/shard_map/ppermute | solution.py:137
  84.9 21.9 %all-to-all-start.4 = ((bf16[16,4,576]{2,1,0:T(4,128)(2,1)}), bf16[16,4,576]{2,1,0:T(4,128)(2,1)S(1)}, u32[]{:S(2)}, u32[]{:S(2)}) async-start(bf16[16,4,576]{2,1,0:T(4,128)(2,1)} %reshape.393), calls=%async_computation.4 | async-start | bytes 163840 | tf_op jit(solution)/shard_map/all_to_all | solution.py:16
  95.0 121.5 %copy-start.6 = (f32[576]{0:T(1024)}, f32[576]{0:T(1024)S(1)}, u32[]{:S(2)}) copy-start(f32[576]{0:T(1024)S(1)} %convert_element_type.306) | copy-start | bytes 6916
  106.8 109.7 %copy-start.2 = (f32[4,576]{1,0:T(4,128)}, f32[4,576]{1,0:T(4,128)S(1)}, u32[]{:S(2)}) copy-start(f32[4,576]{1,0:T(4,128)S(1)} %convert_reduce_fusion.5) | copy-start | bytes 27652
  107.5 15.1 %all-to-all-start.5 = ((bf16[16,4,576]{2,1,0:T(4,128)(2,1)}), bf16[16,4,576]{2,1,0:T(4,128)(2,1)S(1)}, u32[]{:S(2)}, u32[]{:S(2)}) async-start(bf16[16,4,576]{2,1,0:T(4,128)(2,1)} %broadcast_in_dim.58), calls=%async_computation.5 | async-start | bytes 163840 | tf_op jit(solution)/shard_map/all_to_all | solution.py:16
  111.2 30.2 %collective-permute-start.5 = (bf16[2,576,576]{2,1,0:T(8,128)(2,1)}, bf16[2,576,576]{2,1,0:T(8,128)(2,1)}, u32[]{:S(2)}, u32[]{:S(2)}) collective-permute-start(bf16[2,576,576]{2,1,0:T(8,128)(2,1)} %collective-permute-done.1), channel_id=1, source_target_pairs={{0,8},{8,16},{16,24},{24,0},{1,9},{9,17},{17,25},{25,1},{2,10},{10... | collective-permute-start | bytes 3981320 | tf_op jit(solution)/shard_map/ppermute | solution.py:112
  143.8 18.2 %all-to-all-start.6 = ((bf16[8,8,2432]{2,1,0:T(8,128)(2,1)}), bf16[8,8,2432]{2,1,0:T(8,128)(2,1)S(1)}, u32[]{:S(2)}, u32[]{:S(2)}) async-start(bf16[8,8,2432]{2,1,0:T(8,128)(2,1)} %concatenate.78), calls=%async_computation.6 | async-start | bytes 622592 | tf_op jit(solution)/shard_map/all_to_all | solution.py:16
  156.0 37.2 %collective-permute-start.6 = (bf16[2,576,576]{2,1,0:T(8,128)(2,1)}, bf16[2,576,576]{2,1,0:T(8,128)(2,1)S(1)}, u32[]{:S(2)}, u32[]{:S(2)}) collective-permute-start(bf16[2,576,576]{2,1,0:T(8,128)(2,1)} %collective-permute-done.3), channel_id=1, source_target_pairs={{0,8},{8,16},{16,24},{24,0},{1,9},{9,17},{17,25},{25,1},{2,10},{10... | collective-permute-start | bytes 3981320 | tf_op jit(solution)/shard_map/ppermute | solution.py:179
  217.2 15.8 %all-to-all-start.9 = ((bf16[16,4,576]{2,1,0:T(4,128)(2,1)}), bf16[16,4,576]{2,1,0:T(4,128)(2,1)S(1)}, u32[]{:S(2)}, u32[]{:S(2)}) async-start(bf16[16,4,576]{2,1,0:T(4,128)(2,1)} %broadcast_in_dim.61), calls=%async_computation.9 | async-start | bytes 163840 | tf_op jit(solution)/shard_map/all_to_all | solution.py:16
  243.6 14.3 %all-to-all-start.10 = ((bf16[8,8,2432]{2,1,0:T(8,128)(2,1)}), bf16[8,8,2432]{2,1,0:T(8,128)(2,1)S(1)}, u32[]{:S(2)}, u32[]{:S(2)}) async-start(bf16[8,8,2432]{2,1,0:T(8,128)(2,1)} %concatenate.84), calls=%async_computation.10 | async-start | bytes 622592 | tf_op jit(solution)/shard_map/all_to_all | solution.py:16
  259.2 11.3 %all-to-all-start.11 = ((bf16[8,8,2304]{2,1,0:T(8,128)(2,1)}), bf16[8,8,2304]{2,1,0:T(8,128)(2,1)S(1)}, u32[]{:S(2)}, u32[]{:S(2)}) async-start(bf16[8,8,2304]{2,1,0:T(8,128)(2,1)} %broadcast_in_dim.62), calls=%async_computation.11 | async-start | bytes 589824 | tf_op jit(solution)/shard_map/all_to_all | solution.py:16
  272.2 35.8 %copy-start.3 = (f32[4,576]{1,0:T(4,128)S(1)}, f32[4,576]{1,0:T(4,128)}, u32[]{:S(2)}) copy-start(f32[4,576]{1,0:T(4,128)} %copy-done.2) | copy-start | bytes 27652
  272.2 35.8 %copy-start.5 = (f32[4,576]{1,0:T(4,128)S(1)}, f32[4,576]{1,0:T(4,128)}, u32[]{:S(2)}) copy-start(f32[4,576]{1,0:T(4,128)} %copy-done.4) | copy-start | bytes 27652
  274.6 15.1 %all-to-all-start.12 = ((bf16[16,4,576]{2,1,0:T(4,128)(2,1)}), bf16[16,4,576]{2,1,0:T(4,128)(2,1)S(1)}, u32[]{:S(2)}, u32[]{:S(2)}) async-start(bf16[16,4,576]{2,1,0:T(4,128)(2,1)} %reshape.402), calls=%async_computation.12 | async-start | bytes 163840 | tf_op jit(solution)/shard_map/all_to_all | solution.py:16
  290.6 13.0 %all-to-all-start.13 = ((f32[32,1,16]{2,1,0:T(1,128)}), f32[32,1,16]{2,1,0:T(1,128)S(1)}, u32[]{:S(2)}, u32[]{:S(2)}) async-start(f32[32,1,16]{2,1,0:T(1,128)} %broadcast_in_dim.66), calls=%async_computation.13 | async-start | bytes 32768 | tf_op jit(solution)/shard_map/all_to_all | solution.py:16
  304.5 14.7 %all-to-all-start.14 = ((f32[16,1,12]{2,1,0:T(1,128)}), f32[16,1,12]{2,1,0:T(1,128)S(1)}, u32[]{:S(2)}, u32[]{:S(2)}) async-start(f32[16,1,12]{2,1,0:T(1,128)} %broadcast_in_dim.68), calls=%async_computation.14 | async-start | bytes 16384 | tf_op jit(solution)/shard_map/all_to_all | solution.py:16
  (12 other events, 250.5 us)

commit v4 on v2

v4 whole, which is shorter than its diff:
```python
import functools
import math

import jax
import jax.numpy as jnp
from jax import lax
from jax.experimental import pallas as pl
from jax.experimental.pallas import tpu as pltpu
from jax.sharding import Mesh, PartitionSpec as P

D = 4608
BF = jnp.bfloat16
F32 = jnp.float32
SEG = ("y", "c")
EPS = 1e-06
HALF = 64
SIDE = 128
MIB = 1 << 20


def swap(chunks, axes):
    return lax.all_to_all(chunks, axes, 0, 0, tiled=True)


def share(value, axes, count):
    return swap(jnp.broadcast_to(value[None], (count, *value.shape)), axes)


def split_pair(value):
    high = value.astype(BF)
    low = (value - high.astype(F32)).astype(BF)
    return high, low


def dot_t(a, b):
    return lax.dot_general(a, b, (((1,), (1,)), ((), ())), preferred_element_type=F32)


def packed(hidden, extras):
    high, low = split_pair(extras)
    pad = -(hidden.shape[1] + 2 * high.shape[1]) % 128
    return jnp.concatenate(
        [hidden.astype(BF), high, low, jnp.zeros((hidden.shape[0], pad), BF)], axis=1
    )


def unpacked(total, width, count):
    hidden = total[:, :width]
    extras = total[:, width : width + count] + total[:, width + count : width + 2 * count]
    return hidden, extras


def lanes(rows):
    return lax.broadcasted_iota(jnp.int32, (rows, SIDE), 1)


def fetches(parts, whole, sems):
    copies, start = [], 0
    for i, part in enumerate(parts):
        size = part.shape[0]
        copies.append(
            pltpu.make_async_copy(part, whole.at[pl.ds(start, size)], sems.at[i])
        )
        start += size
    return copies


def enter_kernel(low_lanes, stream, gain, left, target, pick, *rest):
    parts, (out, whole, sems) = rest[:-3], rest[-3:]
    copies = fetches(parts, whole, sems)
    for copy in copies:
        copy.start()
    rows = stream.shape[0]
    wide = stream[...].astype(F32)
    scaled = (wide * gain[...]).astype(BF)
    extras = dot_t(scaled, left[...]) * pick[...]
    lane = lanes(rows)
    place = lane % HALF
    square = jnp.sum(wide * wide, axis=1, keepdims=True)
    along = jnp.sum(wide * target[...].astype(F32), axis=1, keepdims=True)
    extras = jnp.where(place == low_lanes, square, extras)
    extras = jnp.where(place == low_lanes + 1, along, extras)
    high = extras.astype(BF).astype(F32)
    out[:, :SIDE] = jnp.where(lane < HALF, high, extras - high).astype(BF)
    step = 2 * whole.shape[0] // max(len(parts), 2)
    for i in range(whole.shape[0] // step):
        for copy in copies[2 * i : 2 * i + 2]:
            copy.wait()
        out[:, SIDE + i * step : SIDE + (i + 1) * step] = dot_t(
            scaled, whole[i * step : (i + 1) * step]
        ).astype(BF)


def enter(stream, gain, left, target, pick, parts, low_lanes):
    rows, width = stream.shape
    hid = sum(p.shape[0] for p in parts)
    vmem = pl.BlockSpec(memory_space=pltpu.VMEM)
    return pl.pallas_call(
        functools.partial(enter_kernel, low_lanes),
        out_shape=jax.ShapeDtypeStruct((rows, SIDE + hid), BF),
        in_specs=[vmem] * 5 + [pl.BlockSpec(memory_space=pl.ANY)] * len(parts),
        out_specs=vmem,
        scratch_shapes=[
            pltpu.VMEM((hid, width), BF),
            pltpu.SemaphoreType.DMA((len(parts),)),
        ],
        compiler_params=pltpu.CompilerParams(vmem_limit_bytes=12 * MIB),
        cost_estimate=pl.CostEstimate(
            flops=2 * rows * hid * width, bytes_accessed=2 * hid * width, transcendentals=0
        ),
        name="enter",
    )(stream, gain, left, target, pick, *parts)


def middle_kernel(low_lanes, got, right, out, side):
    count, rows, _ = got.shape
    total = got[0].astype(F32)
    for i in range(1, count):
        total += got[i].astype(F32)
    extras = total[:, :SIDE]
    place = lanes(rows) % HALF
    square = jnp.sum(jnp.where(place == low_lanes, extras, 0.0), axis=1, keepdims=True)
    along = jnp.sum(jnp.where(place == low_lanes + 1, extras, 0.0), axis=1, keepdims=True)
    scale = lax.rsqrt(square / D + EPS)
    side[...] = jnp.broadcast_to(along * scale, (rows, SIDE))
    low = jnp.zeros((rows, right.shape[1]), F32)
    left = extras
    for _ in range(3):
        piece = left.astype(BF)
        low += jnp.dot(piece, right[...], preferred_element_type=F32)
        left = left - piece.astype(F32)
    mixed = scale * (total[:, SIDE:] + low)
    gated = (mixed / (1.0 + jnp.exp(-mixed))).astype(BF)
    for i in range(count):
        out[i] = gated


def middle(got, right, low_lanes):
    count, rows, full = got.shape
    vmem = pl.BlockSpec(memory_space=pltpu.VMEM)
    return pl.pallas_call(
        functools.partial(middle_kernel, low_lanes),
        out_shape=(
            jax.ShapeDtypeStruct((count, rows, full - SIDE), BF),
            jax.ShapeDtypeStruct((rows, SIDE), F32),
        ),
        in_specs=[vmem] * 2,
        out_specs=(vmem, vmem),
        compiler_params=pltpu.CompilerParams(vmem_limit_bytes=12 * MIB),
        name="middle",
    )(got, right)


def leave_kernel(gated, *rest):
    parts, (out, whole, sems) = rest[:-3], rest[-3:]
    copies = fetches(parts, whole, sems)
    for copy in copies:
        copy.start()
    step = 2 * whole.shape[0] // max(len(parts), 2)
    total = None
    for i in range(whole.shape[0] // step):
        for copy in copies[2 * i : 2 * i + 2]:
            copy.wait()
        here = slice(i * step, (i + 1) * step)
        piece = jnp.dot(gated[:, here], whole[here], preferred_element_type=F32)
        total = piece if total is None else total + piece
    out[...] = total.astype(BF)


def leave(gated, parts):
    rows, hid = gated.shape
    width = parts[0].shape[1]
    vmem = pl.BlockSpec(memory_space=pltpu.VMEM)
    return pl.pallas_call(
        leave_kernel,
        out_shape=jax.ShapeDtypeStruct((rows, width), BF),
        in_specs=[vmem] + [pl.BlockSpec(memory_space=pl.ANY)] * len(parts),
        out_specs=vmem,
        scratch_shapes=[
            pltpu.VMEM((hid, width), BF),
            pltpu.SemaphoreType.DMA((len(parts),)),
        ],
        compiler_params=pltpu.CompilerParams(vmem_limit_bytes=12 * MIB),
        cost_estimate=pl.CostEstimate(
            flops=2 * rows * hid * width, bytes_accessed=2 * hid * width, transcendentals=0
        ),
        name="leave",
    )(gated, *parts)


def sided(factors):
    empty = jnp.zeros((HALF - factors.shape[0], factors.shape[1]), factors.dtype)
    return jnp.concatenate([factors, empty, factors, empty], axis=0)


def local(block, w_in, w_out, gains, fac_left, right_perturb_factors, assign):
    nz, nx = lax.axis_size("z"), lax.axis_size("x")
    ny = lax.axis_size("y")
    ns = ny * lax.axis_size("c")
    width = block.shape[1]
    hid = w_in.shape[1]
    layers = w_in.shape[0]
    members, _, rank, _ = fac_left.shape
    low_lanes = members * rank
    tok = nz * nx
    z, x = lax.axis_index("z"), lax.axis_index("x")
    seg = lax.axis_index("y") * lax.axis_size("c") + lax.axis_index("c")

    lefts = [
        jnp.take(fac_left, assign[i], axis=1).reshape(low_lanes, width) for i in range(layers)
    ]
    rights = [
        jnp.take(right_perturb_factors, assign[i], axis=1).reshape(low_lanes, hid)
        for i in range(layers)
    ]

    early = w_in[1]
    base = share(block.astype(F32), "x", nx).reshape(nx, width).astype(BF)
    base, far_in, far_out = lax.optimization_barrier((base, w_in, w_out))
    near_in, near_out = [], []
    for layer in range(1, layers):
        far = early if layer == 1 else far_in[layer]
        near_in.append([lax.all_gather(far, "x", axis=0, tiled=True)])
        near_out.append([lax.all_gather(far_out[layer], "x", axis=0, tiled=True)])
    base = share(base, "z", nz)
    natural = base.reshape(tok, width)
    base = jnp.swapaxes(base, 0, 1).reshape(tok, width)
    after = jnp.concatenate([natural[1:], jnp.zeros((1, width), BF)], axis=0)
    near_after = lax.dynamic_slice(after.reshape(nz, nx, width), (0, x, 0), (nz, 1, width))
    near_after = near_after.reshape(nz, width)
    near_token = jnp.arange(nz) * nx + x
    near_weight = jnp.where(
        near_token < tok - 1, 1.0 + 2.0 * near_token.astype(F32) / (tok - 2), 0.0
    )
    near_rows = nz * members
    target = jnp.repeat(near_after, members, axis=0)
    row_weight = jnp.repeat(near_weight, members)
    row_member = jnp.arange(near_rows) % members
    place = jnp.arange(SIDE) % HALF
    pick = (row_member[:, None] == (place // rank)[None]) & (place < low_lanes)[None]
    pick = pick.astype(F32)
    chunk = near_rows // ns
    own_member = jnp.arange(chunk) % members
    own_weight = lax.dynamic_slice(row_weight, (seg * chunk,), (chunk,))
    to_member = (own_member[None] == jnp.arange(members)[:, None]).astype(F32)

    mine = jnp.broadcast_to(block, (members, width))
    scores = []
    stream = None
    for layer in range(layers):
        gain = gains[layer]
        if layer == 0:
            wide = base.astype(F32)
            scaled = (wide * gain).astype(BF)
            extras = jnp.concatenate(
                [dot_t(scaled, lefts[0]), jnp.sum(wide * wide, axis=1, keepdims=True)], axis=1
            )
            part = packed(dot_t(scaled, w_in[0]), extras)
            parts = share(part, SEG, ns)
            total = jnp.sum(parts.reshape(ns, tok, -1).astype(F32), axis=0)
            hidden, extras = unpacked(total, hid, low_lanes + 1)
            scale = lax.rsqrt(extras[:, -1:] / D + EPS)
            low = extras[:, :-1].reshape(tok, members, rank)
            right = rights[0].reshape(members, rank, hid).astype(F32)
            mixed = scale[:, None] * (
                hidden[:, None]
                + jnp.einsum("tmr,mrf->tmf", low, right, precision=lax.Precision.HIGHEST)
            )
            gated = jax.nn.silu(mixed).astype(BF).reshape(tok * members, hid)
            update = jnp.dot(gated, w_out[layer], preferred_element_type=F32).astype(BF)
            sent = jnp.concatenate(rights[1:], axis=0)
            sent = jnp.broadcast_to(sent[None], (nx, *sent.shape))
            part = swap(jnp.concatenate([update.reshape(nx, near_rows, width), sent], axis=1), "x")
            late = part[:, near_rows:].astype(F32)
            late = [
                sum(late[i] * ((x + step) % nx == i).astype(F32) for i in range(nx))
                for step in (-x, 1 - x, 2 - x, 3 - x)
            ]
            later = jnp.concatenate(late, axis=1).astype(BF)
            later = [
                sided(later[i * low_lanes : (i + 1) * low_lanes]) for i in range(layers - 1)
            ]
            part = jnp.sum(part[:, :near_rows].astype(F32), axis=0).astype(BF)
        else:
            part = enter(
                stream,
                gain[None],
                sided(lefts[layer]),
                target,
                pick,
                near_in[layer - 1],
                low_lanes,
            )
            part = swap(part.reshape(ns, chunk, -1), SEG)
            gated, side = middle(part, later[layer - 1], low_lanes)
            scores.append(jnp.sum(to_member * (side[:, 0] * own_weight), axis=1))
            gated = swap(gated, SEG)
            part = leave(gated.reshape(near_rows, nx * hid), near_out[layer - 1])
        part = swap(part.reshape(nz, members, width), "z")
        mine = (mine.astype(F32) + jnp.sum(part.astype(F32), axis=0)).astype(BF)
        if layer < layers - 1:
            stream = share(mine, "z", nz)
            stream = stream.reshape(near_rows, width)

    wide = mine.astype(F32)
    my_target = lax.dynamic_slice(near_after, (z, 0), (1, width)).astype(F32)
    first = jnp.where(z == 0, 1.0, 0.0)
    sums = jnp.concatenate(
        [
            jnp.sum(wide * wide, axis=1),
            jnp.sum(wide * my_target, axis=1),
            *[first * s for s in scores],
        ]
    )
    count = nx * ns
    got = share(sums[None], ("x", *SEG), count).reshape(nx, ns, -1)
    got = jnp.sum(got, axis=1)
    tokens = z * nx + jnp.arange(nx)
    weights = jnp.where(tokens < tok - 1, 1.0 + 2.0 * tokens.astype(F32) / (tok - 2), 0.0)
    square, along = got[:, :members], got[:, members : 2 * members]
    last = jnp.sum(along * lax.rsqrt(square / D + EPS) * weights[:, None], axis=0)
    earlier = jnp.sum(got[:, 2 * members :], axis=0)
    both = jnp.concatenate([earlier, last])
    both = jnp.sum(share(both[None], "z", nz).reshape(nz, -1), axis=0)
    return both.reshape(layers, members) / math.sqrt((tok - 1) * D), mine[None]


def solution(mesh):
    split = Mesh(mesh.devices.reshape(16, 4, 4, 2), ("z", "x", "y", "c"))
    pop = ("z", "x")
    return jax.shard_map(
        local,
        mesh=split,
        in_specs=(
            P(pop, SEG),
            P(None, pop, SEG),
            P(None, pop, SEG),
            P(None, SEG),
            P(None, None, None, SEG),
            P(None, None, None, pop),
            P(),
        ),
        out_specs=(P(), P(pop, None, SEG)),
        check_vma=False,
    )
```

time: 273 us -> 283 us (1.037)
  blocking collectives: 24.8 us -> 38.4 us
  matrix products: 13.9 us -> 2.71 us
  starting transfers between devices: 80.6 us -> 69.7 us
  Pallas kernels: 0 us -> 8.53 us
  waiting for transfers between devices: 110 us -> 116 us
  local copies, waits for them, and re-layouts: 17.4 us -> 22 us
    all_to_all x2 -> x3, blocking collectives: 24.8 us -> 38.4 us  [swap(): return lax.all_to_all(chunks, axes, 0, 0, tiled=True)]
    dot_general x10 -> x2, matrix products: 12.8 us -> 0.47 us  [dot_t(): lax.dot_general(a, b, (((1,), (1,)), ((), ())), preferred_element_type=F32)]
    all_to_all x12, starting transfers between devices: 80.5 us -> 69.6 us  [swap(): return lax.all_to_all(chunks, axes, 0, 0, tiled=True)]
    all_to_all x12, waiting for transfers between devices: 106 us -> 115 us  [swap(): return lax.all_to_all(chunks, axes, 0, 0, tiled=True)]
    pallas_call x0 -> x6, Pallas kernels: none -> 8.53 us  [the longest x2 4.45 us: enter(): pl.pallas_call(functools.partial(enter_kernel, low_lanes), out_shape=jax....]
    unnamed x15 -> x24, local copies, waits for them, and re-layouts: 0.96 us -> 7.54 us
    slice x5 -> x6, local copies, waits for them, and re-layouts: 4.14 us -> 6.04 us  [the longest x1 2.8 us: local(): near_out.append([lax.all_gather(far_out[layer], 'x', axis=0, tiled=True)])]
  transfers between devices with their start and end apart: 16 -> 16, of which waited for: 13 -> 12; matrix products, arithmetic and copies ran while one was open for 10% -> 6% of each run, Pallas kernels for 0% -> 3%
where the time goes in v4:
time: 283 us; the launch traced here: 282 us
  waiting for transfers between devices  116 us (41%)
  starting transfers between devices  69.7 us (25%)
  blocking collectives  38.4 us (14%)
  local copies, waits for them, and re-layouts  22 us (8%)
  between operations  20.3 us (7%)
  Pallas kernels  8.53 us (3%)
  other arithmetic  4.17 us (1%)
    all_to_all x12, waiting for transfers between devices, swap(): return lax.all_to_all(chunks, axes, 0, 0, tiled=True)  115 us
    all_to_all x12, starting transfers between devices, swap(): return lax.all_to_all(chunks, axes, 0, 0, tiled=True)  69.6 us
    all_to_all x3, blocking collectives, swap(): return lax.all_to_all(chunks, axes, 0, 0, tiled=True)  38.4 us
    unnamed x24, local copies, waits for them, and re-layouts  7.54 us
  transfers between devices with their start and end apart: 16, of which 12 were waited for; matrix products, arithmetic and copies ran while one was open for 6% of the time, Pallas kernels for 3%

profile of v4, /device:TPU:1, one launch (start us, length us, event | category | flops | bytes accessed | tf_op | source)
XLA Modules:
  0.0 281.6 jit_solution(10322332404816732878)
XLA Ops:
  10.7 8.8 %all_to_all.75 = bf16[4,2,288]{2,1,0:T(2,128)(2,1)S(1)} all-to-all(bf16[4,2,288]{2,1,0:T(2,128)(2,1)S(1)} %reshape.440), channel_id=1, replica_groups=mesh['z'=16,'x'=4,'y'=4,'c'=2] {'x'}, dimensions={0} | all-to-all | bytes 9216 | tf_op jit(solution)/shard_map/all_to_all | solution.py:22
  30.8 14.9 %all-to-all-start.1 = ((bf16[16,4,576]{2,1,0:T(4,128)(2,1)}), bf16[16,4,576]{2,1,0:T(4,128)(2,1)S(1)}, u32[]{:S(2)}, u32[]{:S(2)}) async-start(bf16[16,4,576]{2,1,0:T(4,128)(2,1)} %broadcast_in_dim.46), calls=%async_computation.1 | async-start | bytes 163840 | tf_op jit(solution)/shard_map/all_to_all | solution.py:22
  45.9 11.7 %all-to-all-done.1 = bf16[16,4,576]{2,1,0:T(4,128)(2,1)S(1)} async-done(((bf16[16,4,576]{2,1,0:T(4,128)(2,1)}), bf16[16,4,576]{2,1,0:T(4,128)(2,1)S(1)}, u32[]{:S(2)}, u32[]{:S(2)}) %all-to-all-start.1) | async-done | bytes 73760 | tf_op jit(solution)/shard_map/all_to_all | solution.py:22
  59.5 8.0 %all-to-all-start.2 = ((bf16[8,64,640]{2,1,0:T(8,128)(2,1)}), bf16[8,64,640]{2,1,0:T(8,128)(2,1)S(1)}, u32[]{:S(2)}, u32[]{:S(2)}) async-start(bf16[8,64,640]{2,1,0:T(8,128)(2,1)} %broadcast_in_dim.49), calls=%async_computation.2 | async-start | bytes 1310720 | tf_op jit(solution)/shard_map/all_to_all | solution.py:22
  67.8 10.7 %all-to-all-done.2 = bf16[8,64,640]{2,1,0:T(8,128)(2,1)S(1)} async-done(((bf16[8,64,640]{2,1,0:T(8,128)(2,1)}), bf16[8,64,640]{2,1,0:T(8,128)(2,1)S(1)}, u32[]{:S(2)}, u32[]{:S(2)}) %all-to-all-start.2) | async-done | bytes 655392 | tf_op jit(solution)/shard_map/all_to_all | solution.py:22
  87.0 13.6 %all-to-all-done.3 = bf16[4,96,576]{2,1,0:T(8,128)(2,1)S(1)} async-done(((bf16[4,96,576]{2,1,0:T(8,128)(2,1)}), bf16[4,96,576]{2,1,0:T(8,128)(2,1)S(1)}, u32[]{:S(2)}, u32[]{:S(2)}) %all-to-all-start.3) | async-done | bytes 442400 | tf_op jit(solution)/shard_map/all_to_all | solution.py:22
  101.3 3.5 %all-to-all-start.4 = ((bf16[16,4,576]{2,1,0:T(4,128)(2,1)}), bf16[16,4,576]{2,1,0:T(4,128)(2,1)S(1)}, u32[]{:S(2)}, u32[]{:S(2)}) async-start(bf16[16,4,576]{2,1,0:T(4,128)(2,1)} %reshape.276), calls=%async_computation.4 | async-start | bytes 163840 | tf_op jit(solution)/shard_map/all_to_all | solution.py:22
  105.1 11.5 %all-to-all-done.4 = bf16[16,4,576]{2,1,0:T(4,128)(2,1)S(1)} async-done(((bf16[16,4,576]{2,1,0:T(4,128)(2,1)}), bf16[16,4,576]{2,1,0:T(4,128)(2,1)S(1)}, u32[]{:S(2)}, u32[]{:S(2)}) %all-to-all-start.4) | async-done | bytes 73760 | tf_op jit(solution)/shard_map/all_to_all | solution.py:22
  117.2 3.5 %all-to-all-start.5 = ((bf16[16,4,576]{2,1,0:T(4,128)(2,1)}), bf16[16,4,576]{2,1,0:T(4,128)(2,1)S(1)}, u32[]{:S(2)}, u32[]{:S(2)}) async-start(bf16[16,4,576]{2,1,0:T(4,128)(2,1)} %broadcast_in_dim.51), calls=%async_computation.5 | async-start | bytes 163840 | tf_op jit(solution)/shard_map/all_to_all | solution.py:22
  120.8 11.6 %all-to-all-done.5 = bf16[16,4,576]{2,1,0:T(4,128)(2,1)S(1)} async-done(((bf16[16,4,576]{2,1,0:T(4,128)(2,1)}), bf16[16,4,576]{2,1,0:T(4,128)(2,1)S(1)}, u32[]{:S(2)}, u32[]{:S(2)}) %all-to-all-start.5) | async-done | bytes 73760 | tf_op jit(solution)/shard_map/all_to_all | solution.py:22
  136.5 7.4 %all-to-all-start.6 = ((bf16[8,8,2432]{2,1,0:T(8,128)(2,1)}), bf16[8,8,2432]{2,1,0:T(8,128)(2,1)S(1)}, u32[]{:S(2)}, u32[]{:S(2)}) async-start(bf16[8,8,2432]{2,1,0:T(8,128)(2,1)} %bitcast.18), calls=%async_computation.6 | async-start | bytes 622592 | tf_op jit(solution)/shard_map/all_to_all | solution.py:22
  144.1 6.9 %all-to-all-done.6.got = bf16[8,8,2432]{2,1,0:T(8,128)(2,1)S(1)} async-done(((bf16[8,8,2432]{2,1,0:T(8,128)(2,1)}), bf16[8,8,2432]{2,1,0:T(8,128)(2,1)S(1)}, u32[]{:S(2)}, u32[]{:S(2)}) %all-to-all-start.6) | async-done | bytes 311328 | tf_op jit(solution)/shard_map/all_to_all | solution.py:22
  152.1 4.4 %all-to-all-start.7 = ((bf16[8,8,2304]{2,1,0:T(8,128)(2,1)}), bf16[8,8,2304]{2,1,0:T(8,128)(2,1)S(1)}, u32[]{:S(2)}, u32[]{:S(2)}) async-start(bf16[8,8,2304]{2,1,0:T(8,128)(2,1)} %get-tuple-element.11), calls=%async_computation.7 | async-start | bytes 589824 | tf_op jit(solution)/shard_map/all_to_all | solution.py:22
  156.5 6.8 %all-to-all-done.7 = bf16[8,8,2304]{2,1,0:T(8,128)(2,1)S(1)} async-done(((bf16[8,8,2304]{2,1,0:T(8,128)(2,1)}), bf16[8,8,2304]{2,1,0:T(8,128)(2,1)S(1)}, u32[]{:S(2)}, u32[]{:S(2)}) %all-to-all-start.7) | async-done | bytes 294944 | tf_op jit(solution)/shard_map/all_to_all | solution.py:22
  166.1 14.8 %all_to_all.76 = bf16[16,4,576]{2,1,0:T(4,128)(2,1)S(1)} all-to-all(bf16[16,4,576]{2,1,0:T(4,128)(2,1)S(1)} %reshape.285), channel_id=1, replica_groups=mesh['z'=16,'x'=4,'y'=4,'c'=2] {'z'}, dimensions={0} | all-to-all | bytes 147456 | tf_op jit(solution)/shard_map/all_to_all | solution.py:22
  181.0 14.9 %all_to_all.77 = bf16[16,4,576]{2,1,0:T(4,128)(2,1)S(1)} all-to-all(bf16[16,4,576]{2,1,0:T(4,128)(2,1)S(1)} %broadcast_in_dim.54), channel_id=1, replica_groups=mesh['z'=16,'x'=4,'y'=4,'c'=2] {'z'}, dimensions={0} | all-to-all | bytes 147456 | tf_op jit(solution)/shard_map/all_to_all | solution.py:22
  200.0 6.9 %all-to-all-start.10 = ((bf16[8,8,2432]{2,1,0:T(8,128)(2,1)}), bf16[8,8,2432]{2,1,0:T(8,128)(2,1)S(1)}, u32[]{:S(2)}, u32[]{:S(2)}) async-start(bf16[8,8,2432]{2,1,0:T(8,128)(2,1)} %bitcast.28), calls=%async_computation.10 | async-start | bytes 622592 | tf_op jit(solution)/shard_map/all_to_all | solution.py:22
  207.3 6.6 %all-to-all-done.10.got = bf16[8,8,2432]{2,1,0:T(8,128)(2,1)S(1)} async-done(((bf16[8,8,2432]{2,1,0:T(8,128)(2,1)}), bf16[8,8,2432]{2,1,0:T(8,128)(2,1)S(1)}, u32[]{:S(2)}, u32[]{:S(2)}) %all-to-all-start.10) | async-done | bytes 311328 | tf_op jit(solution)/shard_map/all_to_all | solution.py:22
  215.0 4.4 %all-to-all-start.11 = ((bf16[8,8,2304]{2,1,0:T(8,128)(2,1)}), bf16[8,8,2304]{2,1,0:T(8,128)(2,1)S(1)}, u32[]{:S(2)}, u32[]{:S(2)}) async-start(bf16[8,8,2304]{2,1,0:T(8,128)(2,1)} %get-tuple-element.14), calls=%async_computation.11 | async-start | bytes 589824 | tf_op jit(solution)/shard_map/all_to_all | solution.py:22
  219.8 6.5 %all-to-all-done.11 = bf16[8,8,2304]{2,1,0:T(8,128)(2,1)S(1)} async-done(((bf16[8,8,2304]{2,1,0:T(8,128)(2,1)}), bf16[8,8,2304]{2,1,0:T(8,128)(2,1)S(1)}, u32[]{:S(2)}, u32[]{:S(2)}) %all-to-all-start.11) | async-done | bytes 294944 | tf_op jit(solution)/shard_map/all_to_all | solution.py:22
  233.2 11.6 %all-to-all-done.12 = bf16[16,4,576]{2,1,0:T(4,128)(2,1)S(1)} async-done(((bf16[16,4,576]{2,1,0:T(4,128)(2,1)}), bf16[16,4,576]{2,1,0:T(4,128)(2,1)S(1)}, u32[]{:S(2)}, u32[]{:S(2)}) %all-to-all-start.12) | async-done | bytes 73760 | tf_op jit(solution)/shard_map/all_to_all | solution.py:22
  245.8 5.9 %all-to-all-start.13 = ((f32[32,1,16]{2,1,0:T(1,128)}), f32[32,1,16]{2,1,0:T(1,128)S(1)}, u32[]{:S(2)}, u32[]{:S(2)}) async-start(f32[32,1,16]{2,1,0:T(1,128)} %broadcast_in_dim.57), calls=%async_computation.13 | async-start | bytes 32768 | tf_op jit(solution)/shard_map/all_to_all | solution.py:22
  251.7 7.0 %all-to-all-done.13 = f32[32,1,16]{2,1,0:T(1,128)S(1)} async-done(((f32[32,1,16]{2,1,0:T(1,128)}), f32[32,1,16]{2,1,0:T(1,128)S(1)}, u32[]{:S(2)}, u32[]{:S(2)}) %all-to-all-start.13) | async-done | bytes 2080 | tf_op jit(solution)/shard_map/all_to_all | solution.py:22
  263.7 10.6 %all-to-all-done.14 = f32[16,1,12]{2,1,0:T(1,128)S(1)} async-done(((f32[16,1,12]{2,1,0:T(1,128)}), f32[16,1,12]{2,1,0:T(1,128)S(1)}, u32[]{:S(2)}, u32[]{:S(2)}) %all-to-all-start.14) | async-done | bytes 800 | tf_op jit(solution)/shard_map/all_to_all | solution.py:22
  (142 shorter events, 48.6 us)
Async XLA Ops:
  7.2 2.2 copy-start.9
  7.2 125.3 %all-gather.9.cloned.1.call-start = ((), (), s32[]{:S(2)}) async-start(), calls=%async_computation.15 | async-start | bytes 3686400 | tf_op jit(solution)/shard_map/all_gather | solution.py:223
  9.3 147.2 %all-gather.11.cloned.1.call-start = ((), (), s32[]{:S(2)}) async-start(), calls=%async_computation.16 | async-start | bytes 3686400 | tf_op jit(solution)/shard_map/all_gather | solution.py:224
  19.6 2.9 %copy-start.4 = (bf16[3,576,576]{2,1,0:T(8,128)(2,1)S(1)}, bf16[3,576,576]{2,1,0:T(8,128)(2,1)}, u32[]{:S(2)}) copy-start(bf16[3,576,576]{2,1,0:T(8,128)(2,1)} %param.10) | copy-start | bytes 5971972
  22.4 23.3 %copy-start.5 = (bf16[4,4,4,576]{3,2,1,0:T(4,128)(2,1)S(1)}, bf16[4,4,4,576]{3,2,1,0:T(4,128)(2,1)}, u32[]{:S(2)}) copy-start(bf16[4,4,4,576]{3,2,1,0:T(4,128)(2,1)} %param.13) | copy-start | bytes 221188
  22.4 23.3 %copy-start.6 = (bf16[4,4,4,576]{3,2,1,0:T(4,128)(2,1)S(1)}, bf16[4,4,4,576]{3,2,1,0:T(4,128)(2,1)}, u32[]{:S(2)}) copy-start(bf16[4,4,4,576]{3,2,1,0:T(4,128)(2,1)} %param.14) | copy-start | bytes 221188
  22.4 23.5 %copy-start.7 = (f32[3,576]{1,0:T(4,128)S(1)}, f32[3,576]{1,0:T(4,128)}, u32[]{:S(2)}) copy-start(f32[3,576]{1,0:T(4,128)} %param.12) | copy-start | bytes 20740
  22.4 173.5 %all-gather.13.cloned.1.call-start = ((), (), s32[]{:S(2)}) async-start(), calls=%async_computation.17 | async-start | bytes 3686400 | tf_op jit(solution)/shard_map/all_gather | solution.py:223
  30.8 26.8 %all-to-all-start.1 = ((bf16[16,4,576]{2,1,0:T(4,128)(2,1)}), bf16[16,4,576]{2,1,0:T(4,128)(2,1)S(1)}, u32[]{:S(2)}, u32[]{:S(2)}) async-start(bf16[16,4,576]{2,1,0:T(4,128)(2,1)} %broadcast_in_dim.46), calls=%async_computation.1 | async-start | bytes 163840 | tf_op jit(solution)/shard_map/all_to_all | solution.py:22
  59.5 18.9 %all-to-all-start.2 = ((bf16[8,64,640]{2,1,0:T(8,128)(2,1)}), bf16[8,64,640]{2,1,0:T(8,128)(2,1)S(1)}, u32[]{:S(2)}, u32[]{:S(2)}) async-start(bf16[8,64,640]{2,1,0:T(8,128)(2,1)} %broadcast_in_dim.49), calls=%async_computation.2 | async-start | bytes 1310720 | tf_op jit(solution)/shard_map/all_to_all | solution.py:22
  82.7 17.9 %all-to-all-start.3 = ((bf16[4,96,576]{2,1,0:T(8,128)(2,1)}), bf16[4,96,576]{2,1,0:T(8,128)(2,1)S(1)}, u32[]{:S(2)}, u32[]{:S(2)}) async-start(bf16[4,96,576]{2,1,0:T(8,128)(2,1)} %pad_maximum_fusion.4), calls=%async_computation.3 | async-start | bytes 983040 | tf_op jit(solution)/shard_map/all_to_all | solution.py:22
  86.1 133.7 %all-gather.15.cloned.1.call-start = ((), (), s32[]{:S(2)}) async-start(), calls=%async_computation.18 | async-start | bytes 3686400 | tf_op jit(solution)/shard_map/all_gather | solution.py:224
  101.3 15.2 %all-to-all-start.4 = ((bf16[16,4,576]{2,1,0:T(4,128)(2,1)}), bf16[16,4,576]{2,1,0:T(4,128)(2,1)S(1)}, u32[]{:S(2)}, u32[]{:S(2)}) async-start(bf16[16,4,576]{2,1,0:T(4,128)(2,1)} %reshape.276), calls=%async_computation.4 | async-start | bytes 163840 | tf_op jit(solution)/shard_map/all_to_all | solution.py:22
  117.2 15.1 %all-to-all-start.5 = ((bf16[16,4,576]{2,1,0:T(4,128)(2,1)}), bf16[16,4,576]{2,1,0:T(4,128)(2,1)S(1)}, u32[]{:S(2)}, u32[]{:S(2)}) async-start(bf16[16,4,576]{2,1,0:T(4,128)(2,1)} %broadcast_in_dim.51), calls=%async_computation.5 | async-start | bytes 163840 | tf_op jit(solution)/shard_map/all_to_all | solution.py:22
  132.5 1.8 copy-start.2
  136.5 14.5 %all-to-all-start.6 = ((bf16[8,8,2432]{2,1,0:T(8,128)(2,1)}), bf16[8,8,2432]{2,1,0:T(8,128)(2,1)S(1)}, u32[]{:S(2)}, u32[]{:S(2)}) async-start(bf16[8,8,2432]{2,1,0:T(8,128)(2,1)} %bitcast.18), calls=%async_computation.6 | async-start | bytes 622592 | tf_op jit(solution)/shard_map/all_to_all | solution.py:22
  152.1 11.2 %all-to-all-start.7 = ((bf16[8,8,2304]{2,1,0:T(8,128)(2,1)}), bf16[8,8,2304]{2,1,0:T(8,128)(2,1)S(1)}, u32[]{:S(2)}, u32[]{:S(2)}) async-start(bf16[8,8,2304]{2,1,0:T(8,128)(2,1)} %get-tuple-element.11), calls=%async_computation.7 | async-start | bytes 589824 | tf_op jit(solution)/shard_map/all_to_all | solution.py:22
  163.3 1.8 copy-start.1
  195.9 1.8 copy-start
  200.0 13.9 %all-to-all-start.10 = ((bf16[8,8,2432]{2,1,0:T(8,128)(2,1)}), bf16[8,8,2432]{2,1,0:T(8,128)(2,1)S(1)}, u32[]{:S(2)}, u32[]{:S(2)}) async-start(bf16[8,8,2432]{2,1,0:T(8,128)(2,1)} %bitcast.28), calls=%async_computation.10 | async-start | bytes 622592 | tf_op jit(solution)/shard_map/all_to_all | solution.py:22
  215.0 11.3 %all-to-all-start.11 = ((bf16[8,8,2304]{2,1,0:T(8,128)(2,1)}), bf16[8,8,2304]{2,1,0:T(8,128)(2,1)S(1)}, u32[]{:S(2)}, u32[]{:S(2)}) async-start(bf16[8,8,2304]{2,1,0:T(8,128)(2,1)} %get-tuple-element.14), calls=%async_computation.11 | async-start | bytes 589824 | tf_op jit(solution)/shard_map/all_to_all | solution.py:22
  229.7 15.1 %all-to-all-start.12 = ((bf16[16,4,576]{2,1,0:T(4,128)(2,1)}), bf16[16,4,576]{2,1,0:T(4,128)(2,1)S(1)}, u32[]{:S(2)}, u32[]{:S(2)}) async-start(bf16[16,4,576]{2,1,0:T(4,128)(2,1)} %reshape.290), calls=%async_computation.12 | async-start | bytes 163840 | tf_op jit(solution)/shard_map/all_to_all | solution.py:22
  245.8 13.0 %all-to-all-start.13 = ((f32[32,1,16]{2,1,0:T(1,128)}), f32[32,1,16]{2,1,0:T(1,128)S(1)}, u32[]{:S(2)}, u32[]{:S(2)}) async-start(f32[32,1,16]{2,1,0:T(1,128)} %broadcast_in_dim.57), calls=%async_computation.13 | async-start | bytes 32768 | tf_op jit(solution)/shard_map/all_to_all | solution.py:22
  259.6 14.7 %all-to-all-start.14 = ((f32[16,1,12]{2,1,0:T(1,128)}), f32[16,1,12]{2,1,0:T(1,128)S(1)}, u32[]{:S(2)}, u32[]{:S(2)}) async-start(f32[16,1,12]{2,1,0:T(1,128)} %broadcast_in_dim.108), calls=%async_computation.14 | async-start | bytes 16384 | tf_op jit(solution)/shard_map/all_to_all | solution.py:22
  (2 other events, 2.9 us)
Sparse Core Ops, SparseCore 0:
  10.1 50.8 all-gather.8
  63.1 51.0 all-gather.10
  116.3 40.5 all-gather.12
  158.9 45.7 all-gather.14

commit v5 on v4

v5 whole, which is shorter than its diff:
```python
import functools
import math

import jax
import jax.numpy as jnp
from jax import lax
from jax.experimental import pallas as pl
from jax.experimental.pallas import tpu as pltpu
from jax.sharding import Mesh, PartitionSpec as P

D = 4608
BF = jnp.bfloat16
F32 = jnp.float32
SEG = ("y", "c")
EPS = 1e-06
HALF = 64
SIDE = 128
MIB = 1 << 20
WIDE = 59 * MIB


def swap(chunks, axes):
    return lax.all_to_all(chunks, axes, 0, 0, tiled=True)


def share(value, axes, count):
    return swap(jnp.broadcast_to(value[None], (count, *value.shape)), axes)


def dot_t(a, b):
    return lax.dot_general(a, b, (((1,), (1,)), ((), ())), preferred_element_type=F32)


def lanes(rows):
    return lax.broadcasted_iota(jnp.int32, (rows, SIDE), 1)


def fetches(source, first, size, whole, sems):
    return [
        pltpu.make_async_copy(
            source.at[i, pl.ds(first, size)], whole.at[pl.ds(i * size, size)], sems.at[i]
        )
        for i in range(source.shape[0])
    ]


def side_lanes(extras, square, along, low_lanes):
    lane = lanes(extras.shape[0])
    place = lane % HALF
    extras = jnp.where(place == low_lanes, square, extras)
    if along is not None:
        extras = jnp.where(place == low_lanes + 1, along, extras)
    high = extras.astype(BF).astype(F32)
    return jnp.where(lane < HALF, high, extras - high).astype(BF)


def pack_kernel(layer, *refs):
    if len(refs) == 4:
        w_in, w_out, out, sems = refs
    else:
        w_in, w_out, block, out, copies, sems = refs
    size = w_in.shape[1]
    moves = [
        pltpu.make_async_copy(w.at[layer], out.at[pl.ds(i * size, size)], sems.at[i])
        for i, w in enumerate((w_in, w_out))
    ]
    for move in moves:
        move.start()
    if len(refs) > 4:
        copies[...] = jnp.broadcast_to(block[...][None], copies.shape)
    for move in moves:
        move.wait()


def pack(w_in, w_out, layer, block=None, count=0):
    _, size, width = w_in.shape
    hbm = pl.BlockSpec(memory_space=pltpu.HBM)
    vmem = pl.BlockSpec(memory_space=pltpu.VMEM)
    out_shape = [jax.ShapeDtypeStruct((2 * size, width), BF)]
    given = [w_in, w_out]
    if block is not None:
        given.append(block.reshape(2, width // 2))
        out_shape.append(jax.ShapeDtypeStruct((count, 2, width // 2), BF))
    got = pl.pallas_call(
        functools.partial(pack_kernel, layer),
        out_shape=out_shape,
        in_specs=[hbm] * 2 + [vmem] * (len(given) - 2),
        out_specs=[hbm] + [vmem] * (len(out_shape) - 1),
        scratch_shapes=[pltpu.SemaphoreType.DMA((2,))],
        compiler_params=pltpu.CompilerParams(vmem_limit_bytes=WIDE),
        name="pack",
    )(*given)
    return got if block is not None else got[0]


def first_kernel(low_lanes, stream, gain, left, weight, out):
    wide = stream[...].astype(F32)
    scaled = (wide * gain[...]).astype(BF)
    square = jnp.sum(wide * wide, axis=1, keepdims=True)
    extras = side_lanes(dot_t(scaled, left[...]), square, None, low_lanes)
    hidden = dot_t(scaled, weight[...]).astype(BF)
    for i in range(out.shape[0]):
        out[i, :, :SIDE] = extras
        out[i, :, SIDE:] = hidden


def first(stream, gain, left, weight, low_lanes, count):
    rows = stream.shape[0]
    hid = weight.shape[0]
    vmem = pl.BlockSpec(memory_space=pltpu.VMEM)
    return pl.pallas_call(
        functools.partial(first_kernel, low_lanes),
        out_shape=jax.ShapeDtypeStruct((count, rows, SIDE + hid), BF),
        in_specs=[vmem] * 4,
        out_specs=vmem,
        compiler_params=pltpu.CompilerParams(vmem_limit_bytes=12 * MIB),
        name="first",
    )(stream, gain, left, weight)


def enter_kernel(low_lanes, first, size, stream, gain, left, target, pick, source, out, whole, sems):
    copies = fetches(source, first, size, whole, sems)
    for copy in copies:
        copy.start()
    wide = stream[...].astype(F32)
    scaled = (wide * gain[...]).astype(BF)
    square = jnp.sum(wide * wide, axis=1, keepdims=True)
    along = jnp.sum(wide * target[...].astype(F32), axis=1, keepdims=True)
    extras = dot_t(scaled, left[...]) * pick[...]
    out[:, :SIDE] = side_lanes(extras, square, along, low_lanes)
    step = 2 * size
    for i in range(len(copies) // 2):
        copies[2 * i].wait()
        copies[2 * i + 1].wait()
        out[:, SIDE + i * step : SIDE + (i + 1) * step] = dot_t(
            scaled, whole[i * step : (i + 1) * step]
        ).astype(BF)


def enter(stream, gain, left, target, pick, source, low_lanes, first, size):
    rows, width = stream.shape
    parts = source.shape[0]
    hid = parts * size
    vmem = pl.BlockSpec(memory_space=pltpu.VMEM)
    return pl.pallas_call(
        functools.partial(enter_kernel, low_lanes, first, size),
        out_shape=jax.ShapeDtypeStruct((rows, SIDE + hid), BF),
        in_specs=[vmem] * 5 + [pl.BlockSpec(memory_space=pltpu.HBM)],
        out_specs=vmem,
        scratch_shapes=[pltpu.VMEM((hid, width), BF), pltpu.SemaphoreType.DMA((parts,))],
        compiler_params=pltpu.CompilerParams(vmem_limit_bytes=WIDE),
        cost_estimate=pl.CostEstimate(
            flops=2 * rows * hid * width, bytes_accessed=2 * hid * width, transcendentals=0
        ),
        name="enter",
    )(stream, gain, left, target, pick, source)


def middle_kernel(low_lanes, got, right, out, side):
    count, rows, _ = got.shape
    total = got[0].astype(F32)
    for i in range(1, count):
        total += got[i].astype(F32)
    extras = total[:, :SIDE]
    place = lanes(rows) % HALF
    square = jnp.sum(jnp.where(place == low_lanes, extras, 0.0), axis=1, keepdims=True)
    along = jnp.sum(jnp.where(place == low_lanes + 1, extras, 0.0), axis=1, keepdims=True)
    scale = lax.rsqrt(square / D + EPS)
    side[...] = jnp.broadcast_to(along * scale, (rows, SIDE))
    low = jnp.zeros((rows, right.shape[1]), F32)
    left = extras
    for _ in range(3):
        piece = left.astype(BF)
        low += jnp.dot(piece, right[...], preferred_element_type=F32)
        left = left - piece.astype(F32)
    mixed = scale * (total[:, SIDE:] + low)
    gated = (mixed / (1.0 + jnp.exp(-mixed))).astype(BF)
    for i in range(count):
        out[i] = gated


def middle(got, right, low_lanes):
    count, rows, full = got.shape
    vmem = pl.BlockSpec(memory_space=pltpu.VMEM)
    return pl.pallas_call(
        functools.partial(middle_kernel, low_lanes),
        out_shape=(
            jax.ShapeDtypeStruct((count, rows, full - SIDE), BF),
            jax.ShapeDtypeStruct((rows, SIDE), F32),
        ),
        in_specs=[vmem] * 2,
        out_specs=(vmem, vmem),
        compiler_params=pltpu.CompilerParams(vmem_limit_bytes=12 * MIB),
        name="middle",
    )(got, right)


def leave_kernel(first, size, gated, source, out, whole, sems):
    copies = fetches(source, first, size, whole, sems)
    for copy in copies:
        copy.start()
    step = 2 * size
    total = None
    for i in range(len(copies) // 2):
        copies[2 * i].wait()
        copies[2 * i + 1].wait()
        here = slice(i * step, (i + 1) * step)
        piece = jnp.dot(gated[:, here], whole[here], preferred_element_type=F32)
        total = piece if total is None else total + piece
    out[...] = total.astype(BF)


def leave(gated, source, first, size):
    rows, hid = gated.shape
    parts, _, width = source.shape
    vmem = pl.BlockSpec(memory_space=pltpu.VMEM)
    return pl.pallas_call(
        functools.partial(leave_kernel, first, size),
        out_shape=jax.ShapeDtypeStruct((rows, width), BF),
        in_specs=[vmem, pl.BlockSpec(memory_space=pltpu.HBM)],
        out_specs=vmem,
        scratch_shapes=[pltpu.VMEM((hid, width), BF), pltpu.SemaphoreType.DMA((parts,))],
        compiler_params=pltpu.CompilerParams(vmem_limit_bytes=WIDE),
        cost_estimate=pl.CostEstimate(
            flops=2 * rows * hid * width, bytes_accessed=2 * hid * width, transcendentals=0
        ),
        name="leave",
    )(gated, source)


def sided(factors):
    empty = jnp.zeros((HALF - factors.shape[0], factors.shape[1]), factors.dtype)
    return jnp.concatenate([factors, empty, factors, empty], axis=0)


def local(block, w_in, w_out, gains, fac_left, right_perturb_factors, assign):
    nz, nx = lax.axis_size("z"), lax.axis_size("x")
    ny = lax.axis_size("y")
    ns = ny * lax.axis_size("c")
    width = block.shape[1]
    hid = w_in.shape[1]
    layers = w_in.shape[0]
    members, _, rank, _ = fac_left.shape
    low_lanes = members * rank
    tok = nz * nx
    z, x = lax.axis_index("z"), lax.axis_index("x")
    seg = lax.axis_index("y") * lax.axis_size("c") + lax.axis_index("c")

    chosen = (jnp.arange(fac_left.shape[1])[None] == assign[:, None]).astype(F32)

    def section(factors, layer):
        picked = jnp.sum(factors.astype(F32) * chosen[layer][None, :, None, None], axis=1)
        return picked.astype(BF).reshape(low_lanes, factors.shape[-1])

    lefts = [section(fac_left, i) for i in range(layers)]
    rights = [section(right_perturb_factors, i) for i in range(layers)]
    first_right = rights[0].reshape(members, rank, hid).astype(F32)

    def gathered(packed):
        value = lax.all_gather(packed, "x", axis=0, tiled=True)
        return value.reshape(nx, 2 * hid, width)

    packed, copies = pack(w_in, w_out, 1, block, tok)
    near = [gathered(packed)]
    base = swap(copies, ("z", "x")).reshape(nz, nx, width)
    natural = base.reshape(tok, width)
    base = jnp.swapaxes(base, 0, 1).reshape(tok, width)
    after = jnp.concatenate([natural[1:], jnp.zeros((1, width), BF)], axis=0)
    near_after = lax.dynamic_slice(after.reshape(nz, nx, width), (0, x, 0), (nz, 1, width))
    near_after = near_after.reshape(nz, width)
    near_token = jnp.arange(nz) * nx + x
    near_weight = jnp.where(
        near_token < tok - 1, 1.0 + 2.0 * near_token.astype(F32) / (tok - 2), 0.0
    )
    near_rows = nz * members
    target = jnp.repeat(near_after, members, axis=0)
    row_weight = jnp.repeat(near_weight, members)
    row_member = jnp.arange(near_rows) % members
    place = jnp.arange(SIDE) % HALF
    pick = (row_member[:, None] == (place // rank)[None]) & (place < low_lanes)[None]
    pick = pick.astype(F32)
    chunk = near_rows // ns
    own_member = jnp.arange(chunk) % members
    own_weight = lax.dynamic_slice(row_weight, (seg * chunk,), (chunk,))
    to_member = (own_member[None] == jnp.arange(members)[:, None]).astype(F32)

    mine = jnp.broadcast_to(block, (members, width))
    scores = []
    stream = None
    for layer in range(layers):
        gain = gains[layer]
        if layer == 0:
            parts = first(base, gain[None], sided(lefts[0]), w_in[0], low_lanes, ns)
            parts = swap(parts, SEG)
            total = jnp.sum(parts.astype(F32), axis=0)
            extras = total[:, :HALF] + total[:, HALF:SIDE]
            scale = lax.rsqrt(extras[:, low_lanes : low_lanes + 1] / D + EPS)
            low = extras[:, :low_lanes].reshape(tok, members, rank)
            mixed = scale[:, None] * (
                total[:, None, SIDE:]
                + jnp.einsum("tmr,mrf->tmf", low, first_right, precision=lax.Precision.HIGHEST)
            )
            gated = jax.nn.silu(mixed).astype(BF).reshape(tok * members, hid)
            far_in, far_out, gated = lax.optimization_barrier((w_in, w_out, gated))
            near.append(gathered(pack(far_in, far_out, 2)))
            update = jnp.dot(gated, w_out[layer], preferred_element_type=F32).astype(BF)
            sent = jnp.concatenate(rights[1:], axis=0)
            sent = jnp.broadcast_to(sent[None], (nx, *sent.shape))
            part = swap(jnp.concatenate([update.reshape(nx, near_rows, width), sent], axis=1), "x")
            later = jnp.swapaxes(part[:, near_rows:], 0, 1).reshape(-1, nx * hid)
            later = [
                sided(later[i * low_lanes : (i + 1) * low_lanes]) for i in range(layers - 1)
            ]
            part = jnp.sum(part[:, :near_rows].astype(F32), axis=0).astype(BF)
        else:
            part = enter(
                stream,
                gain[None],
                sided(lefts[layer]),
                target,
                pick,
                near[layer - 1],
                low_lanes,
                0,
                hid,
            )
            part = swap(part.reshape(ns, chunk, -1), SEG)
            gated, side = middle(part, later[layer - 1], low_lanes)
            scores.append(jnp.sum(to_member * (side[:, 0] * own_weight), axis=1))
            gated = swap(gated, SEG)
            part = leave(
                gated.reshape(near_rows, nx * hid), near[layer - 1], hid, hid
            )
        part = swap(part.reshape(nz, members, width), "z")
        mine = (mine.astype(F32) + jnp.sum(part.astype(F32), axis=0)).astype(BF)
        if layer < layers - 1:
            stream = share(mine, "z", nz)
            stream = stream.reshape(near_rows, width)

    wide = mine.astype(F32)
    my_target = lax.dynamic_slice(near_after, (z, 0), (1, width)).astype(F32)
    once = jnp.where(z == 0, 1.0, 0.0)
    sums = jnp.concatenate(
        [
            jnp.sum(wide * wide, axis=1),
            jnp.sum(wide * my_target, axis=1),
            *[once * s for s in scores],
        ]
    )
    count = nx * ns
    got = share(sums[None], ("x", *SEG), count).reshape(nx, ns, -1)
    got = jnp.sum(got, axis=1)
    tokens = z * nx + jnp.arange(nx)
    weights = jnp.where(tokens < tok - 1, 1.0 + 2.0 * tokens.astype(F32) / (tok - 2), 0.0)
    square, along = got[:, :members], got[:, members : 2 * members]
    last = jnp.sum(along * lax.rsqrt(square / D + EPS) * weights[:, None], axis=0)
    earlier = jnp.sum(got[:, 2 * members :], axis=0)
    both = jnp.concatenate([earlier, last])
    both = jnp.sum(share(both[None], "z", nz).reshape(nz, -1), axis=0)
    return both.reshape(layers, members) / math.sqrt((tok - 1) * D), mine[None]


def solution(mesh):
    split = Mesh(mesh.devices.reshape(16, 4, 4, 2), ("z", "x", "y", "c"))
    pop = ("z", "x")
    return jax.shard_map(
        local,
        mesh=split,
        in_specs=(
            P(pop, SEG),
            P(None, pop, SEG),
            P(None, pop, SEG),
            P(None, SEG),
            P(None, None, None, SEG),
            P(None, None, None, pop),
            P(),
        ),
        out_specs=(P(), P(pop, None, SEG)),
        check_vma=False,
    )
```

time: 283 us -> 365 us (1.29)
  Pallas kernels: 8.53 us -> 111 us
  blocking collectives: 38.4 us -> 61.1 us
  waiting for transfers between devices: 116 us -> 94.6 us
  local copies, waits for them, and re-layouts: 22 us -> 13 us
  starting transfers between devices: 69.7 us -> 61.4 us
  between operations: 20.3 us -> 14.5 us
    pallas_call x4 -> x7, Pallas kernels: 6.29 us -> 110 us  [the longest x2 92.9 us: pack(): pl.pallas_call(functools.partial(pack_kernel, layer), out_shape=out_shape...]
    all_to_all x3 -> x4, blocking collectives: 38.4 us -> 61.1 us  [swap(): return lax.all_to_all(chunks, axes, 0, 0, tiled=True)]
    all_to_all x12 -> x10, waiting for transfers between devices: 115 us -> 94.5 us  [swap(): return lax.all_to_all(chunks, axes, 0, 0, tiled=True)]
    all_to_all x12 -> x10, starting transfers between devices: 69.6 us -> 61.4 us  [swap(): return lax.all_to_all(chunks, axes, 0, 0, tiled=True)]
    unnamed x24 -> x13, local copies, waits for them, and re-layouts: 7.54 us -> 0.75 us
    slice x5 -> x2, local copies, waits for them, and re-layouts: 6.53 us -> 0.08 us  [the longest x1 0.06 us: local(): low = extras[:, :low_lanes].reshape(tok, members, rank)]
  transfers between devices with their start and end apart: 16 -> 12, of which waited for: 12 -> 10; matrix products, arithmetic and copies ran while one was open for 6% -> 4% of each run, Pallas kernels for 3% -> 15%
where the time goes in v5:
time: 365 us; the launch traced here: 364 us
  Pallas kernels  111 us (30%)
  waiting for transfers between devices  94.6 us (26%)
  starting transfers between devices  61.4 us (17%)
  blocking collectives  61.1 us (17%)
  between operations  14.5 us (4%)
  local copies, waits for them, and re-layouts  13 us (4%)
  other arithmetic  5.57 us (2%)
    all_to_all x10, waiting for transfers between devices, swap(): return lax.all_to_all(chunks, axes, 0, 0, tiled=True)  94.5 us
    pallas_call x2, Pallas kernels, pack(): pl.pallas_call(functools.partial(pack_kernel, layer), out_shape=out_shape...  92.9 us
    all_to_all x10, starting transfers between devices, swap(): return lax.all_to_all(chunks, axes, 0, 0, tiled=True)  61.4 us
    all_to_all x4, blocking collectives, swap(): return lax.all_to_all(chunks, axes, 0, 0, tiled=True)  61.1 us
    pallas_call x2, Pallas kernels, enter(): pl.pallas_call(functools.partial(enter_kernel, low_lanes, first, size), o...  8.71 us
    pallas_call x2, Pallas kernels, leave(): pl.pallas_call(functools.partial(leave_kernel, first, size), out_shape=ja...  7.88 us
  transfers between devices with their start and end apart: 12, of which 10 were waited for; matrix products, arithmetic and copies ran while one was open for 4% of the time, Pallas kernels for 15%

profile of v5, /device:TPU:1, one launch (start us, length us, event | category | flops | bytes accessed | tf_op | source)
XLA Modules:
  0.0 363.7 jit_solution(7519876181471341644)
XLA Ops:
  8.6 47.1 %pack.2 = (bf16[1152,576]{1,0:T(8,128)(2,1)}, bf16[64,2,288]{2,1,0:T(2,128)(2,1)}) custom-call(bf16[3,576,576]{2,1,0:T(8,128)(2,1)} %refs_0_.2, bf16[3,576,576]{2,1,0:T(8,128)(2,1)} %refs_1_.2, bf16[2,288]{1,0:T(2,128)(2,1)} %reshape.262.refs_2_), custom_call_target="tpu_custom_call" | custom-call | tf_op jit(solution)/shard_map/pack/pallas_call | solution.py:84
  55.7 19.3 %all-to-all-start = ((bf16[64,2,288]{2,1,0:T(2,128)(2,1)}), bf16[64,2,288]{2,1,0:T(2,128)(2,1)S(1)}, u32[]{:S(2)}, u32[]{:S(2)}) async-start(bf16[64,2,288]{2,1,0:T(2,128)(2,1)} %get-tuple-element.11), calls=%async_computation | async-start | bytes 196608 | tf_op jit(solution)/shard_map/all_to_all | solution.py:23
  78.2 11.3 %all-to-all-done = bf16[64,2,288]{2,1,0:T(2,128)(2,1)S(1)} async-done(((bf16[64,2,288]{2,1,0:T(2,128)(2,1)}), bf16[64,2,288]{2,1,0:T(2,128)(2,1)S(1)}, u32[]{:S(2)}, u32[]{:S(2)}) %all-to-all-start) | async-done | bytes 73760 | tf_op jit(solution)/shard_map/all_to_all | solution.py:23
  90.1 19.3 %all_to_all.70 = bf16[8,64,704]{2,1,0:T(8,128)(2,1)S(1)} all-to-all(bf16[8,64,704]{2,1,0:T(8,128)(2,1)S(1)} %first.1), channel_id=1, replica_groups=mesh['z'=16,'x'=4,'y'=4,'c'=2] {'y','c'}, dimensions={0} | all-to-all | bytes 1441792 | tf_op jit(solution)/shard_map/all_to_all | solution.py:23
  110.9 45.8 %pack.3 = bf16[1152,576]{1,0:T(8,128)(2,1)} custom-call(bf16[3,576,576]{2,1,0:T(8,128)(2,1)} %refs_0_.2, bf16[3,576,576]{2,1,0:T(8,128)(2,1)} %refs_1_.2), custom_call_target="tpu_custom_call" | custom-call | tf_op jit(solution)/shard_map/pack/pallas_call | solution.py:84
  163.0 12.9 %all-to-all-done.2 = bf16[4,96,576]{2,1,0:T(8,128)(2,1)S(1)} async-done(((bf16[4,96,576]{2,1,0:T(8,128)(2,1)}), bf16[4,96,576]{2,1,0:T(8,128)(2,1)S(1)}, u32[]{:S(2)}, u32[]{:S(2)}) %all-to-all-start.2) | async-done | bytes 442400 | tf_op jit(solution)/shard_map/all_to_all | solution.py:23
  181.9 9.8 %all-to-all-done.3 = bf16[16,4,576]{2,1,0:T(4,128)(2,1)S(1)} async-done(((bf16[16,4,576]{2,1,0:T(4,128)(2,1)}), bf16[16,4,576]{2,1,0:T(4,128)(2,1)S(1)}, u32[]{:S(2)}, u32[]{:S(2)}) %all-to-all-start.3) | async-done | bytes 73760 | tf_op jit(solution)/shard_map/all_to_all | solution.py:23
  196.3 11.3 %all-to-all-done.4 = bf16[16,4,576]{2,1,0:T(4,128)(2,1)S(1)} async-done(((bf16[16,4,576]{2,1,0:T(4,128)(2,1)}), bf16[16,4,576]{2,1,0:T(4,128)(2,1)S(1)}, u32[]{:S(2)}, u32[]{:S(2)}) %all-to-all-start.4) | async-done | bytes 73760 | tf_op jit(solution)/shard_map/all_to_all | solution.py:23
  208.2 4.4 %enter.2 = bf16[64,2432]{1,0:T(8,128)(2,1)} custom-call(bf16[64,576]{1,0:T(8,128)(2,1)} %reshape.269.stream, f32[1,576]{1,0:T(1,128)} %get-tuple-element.42.gain, bf16[128,576]{1,0:T(8,128)(2,1)} %get-tuple-element.38.left, bf16[64,576]{1,0:T(8,128)(2,1)} %reshape.272.target, f32[64,128]{1,0:T(8,128)} %and_convert_fusion.pick, bf16[4,1152,576]{2,1,0:T(8,128)(2,1)} %bitcast.63), custom_call_target="tpu_custom_call" | custom-call | flops 169869312 | bytes 2654208 | tf_op jit(solution)/shard_map/enter/pallas_call | solution.py:145
  212.6 8.5 %all-to-all-start.5 = ((bf16[8,8,2432]{2,1,0:T(8,128)(2,1)}), bf16[8,8,2432]{2,1,0:T(8,128)(2,1)S(1)}, u32[]{:S(2)}, u32[]{:S(2)}) async-start(bf16[8,8,2432]{2,1,0:T(8,128)(2,1)} %bitcast.67), calls=%async_computation.5 | async-start | bytes 622592 | tf_op jit(solution)/shard_map/all_to_all | solution.py:23
  221.1 6.9 %all-to-all-done.5.got = bf16[8,8,2432]{2,1,0:T(8,128)(2,1)S(1)} async-done(((bf16[8,8,2432]{2,1,0:T(8,128)(2,1)}), bf16[8,8,2432]{2,1,0:T(8,128)(2,1)S(1)}, u32[]{:S(2)}, u32[]{:S(2)}) %all-to-all-start.5) | async-done | bytes 311328 | tf_op jit(solution)/shard_map/all_to_all | solution.py:23
  228.4 11.5 %all_to_all.71 = bf16[8,8,2304]{2,1,0:T(8,128)(2,1)} all-to-all(bf16[8,8,2304]{2,1,0:T(8,128)(2,1)S(1)} %get-tuple-element.14), channel_id=1, replica_groups=mesh['z'=16,'x'=4,'y'=4,'c'=2] {'y','c'}, dimensions={0} | all-to-all | bytes 589824 | tf_op jit(solution)/shard_map/all_to_all | solution.py:23
  244.7 14.4 %all_to_all.72 = bf16[16,4,576]{2,1,0:T(4,128)(2,1)S(1)} all-to-all(bf16[16,4,576]{2,1,0:T(4,128)(2,1)S(1)} %reshape.276), channel_id=1, replica_groups=mesh['z'=16,'x'=4,'y'=4,'c'=2] {'z'}, dimensions={0} | all-to-all | bytes 147456 | tf_op jit(solution)/shard_map/all_to_all | solution.py:23
  259.3 15.9 %all_to_all.73 = bf16[16,4,576]{2,1,0:T(4,128)(2,1)S(1)} all-to-all(bf16[16,4,576]{2,1,0:T(4,128)(2,1)S(1)} %broadcast_in_dim.29), channel_id=1, replica_groups=mesh['z'=16,'x'=4,'y'=4,'c'=2] {'z'}, dimensions={0} | all-to-all | bytes 147456 | tf_op jit(solution)/shard_map/all_to_all | solution.py:23
  275.8 4.4 %enter.3 = bf16[64,2432]{1,0:T(8,128)(2,1)} custom-call(bf16[64,576]{1,0:T(8,128)(2,1)} %reshape.277.stream, f32[1,576]{1,0:T(1,128)} %get-tuple-element.40.gain, bf16[128,576]{1,0:T(8,128)(2,1)} %get-tuple-element.37.left, bf16[64,576]{1,0:T(8,128)(2,1)} %reshape.272.target, f32[64,128]{1,0:T(8,128)} %and_convert_fusion.pick, bf16[4,1152,576]{2,1,0:T(8,128)(2,1)} %bitcast.61), custom_call_target="tpu_custom_call" | custom-call | flops 169869312 | bytes 2654208 | tf_op jit(solution)/shard_map/enter/pallas_call | solution.py:145
  280.2 5.8 %all-to-all-start.9 = ((bf16[8,8,2432]{2,1,0:T(8,128)(2,1)}), bf16[8,8,2432]{2,1,0:T(8,128)(2,1)S(1)}, u32[]{:S(2)}, u32[]{:S(2)}) async-start(bf16[8,8,2432]{2,1,0:T(8,128)(2,1)} %bitcast.66), calls=%async_computation.9 | async-start | bytes 622592 | tf_op jit(solution)/shard_map/all_to_all | solution.py:23
  286.3 6.6 %all-to-all-done.9.got = bf16[8,8,2432]{2,1,0:T(8,128)(2,1)S(1)} async-done(((bf16[8,8,2432]{2,1,0:T(8,128)(2,1)}), bf16[8,8,2432]{2,1,0:T(8,128)(2,1)S(1)}, u32[]{:S(2)}, u32[]{:S(2)}) %all-to-all-start.9) | async-done | bytes 311328 | tf_op jit(solution)/shard_map/all_to_all | solution.py:23
  294.1 4.4 %all-to-all-start.10 = ((bf16[8,8,2304]{2,1,0:T(8,128)(2,1)}), bf16[8,8,2304]{2,1,0:T(8,128)(2,1)S(1)}, u32[]{:S(2)}, u32[]{:S(2)}) async-start(bf16[8,8,2304]{2,1,0:T(8,128)(2,1)} %get-tuple-element.17), calls=%async_computation.10 | async-start | bytes 589824 | tf_op jit(solution)/shard_map/all_to_all | solution.py:23
  298.7 6.6 %all-to-all-done.10 = bf16[8,8,2304]{2,1,0:T(8,128)(2,1)S(1)} async-done(((bf16[8,8,2304]{2,1,0:T(8,128)(2,1)}), bf16[8,8,2304]{2,1,0:T(8,128)(2,1)S(1)}, u32[]{:S(2)}, u32[]{:S(2)}) %all-to-all-start.10) | async-done | bytes 294944 | tf_op jit(solution)/shard_map/all_to_all | solution.py:23
  306.0 3.9 %leave.3 = bf16[64,576]{1,0:T(8,128)(2,1)} custom-call(bf16[64,2304]{1,0:T(8,128)(2,1)} %bitcast.68, bf16[4,1152,576]{2,1,0:T(8,128)(2,1)} %bitcast.62), custom_call_target="tpu_custom_call" | custom-call | flops 169869312 | bytes 2654208 | tf_op jit(solution)/shard_map/leave/pallas_call | solution.py:217
  315.2 11.5 %all-to-all-done.11 = bf16[16,4,576]{2,1,0:T(4,128)(2,1)S(1)} async-done(((bf16[16,4,576]{2,1,0:T(4,128)(2,1)}), bf16[16,4,576]{2,1,0:T(4,128)(2,1)S(1)}, u32[]{:S(2)}, u32[]{:S(2)}) %all-to-all-start.11) | async-done | bytes 73760 | tf_op jit(solution)/shard_map/all_to_all | solution.py:23
  327.6 5.9 %all-to-all-start.12 = ((f32[32,1,16]{2,1,0:T(1,128)}), f32[32,1,16]{2,1,0:T(1,128)S(1)}, u32[]{:S(2)}, u32[]{:S(2)}) async-start(f32[32,1,16]{2,1,0:T(1,128)} %broadcast_in_dim.32), calls=%async_computation.12 | async-start | bytes 32768 | tf_op jit(solution)/shard_map/all_to_all | solution.py:23
  333.5 7.0 %all-to-all-done.12 = f32[32,1,16]{2,1,0:T(1,128)S(1)} async-done(((f32[32,1,16]{2,1,0:T(1,128)}), f32[32,1,16]{2,1,0:T(1,128)S(1)}, u32[]{:S(2)}, u32[]{:S(2)}) %all-to-all-start.12) | async-done | bytes 2080 | tf_op jit(solution)/shard_map/all_to_all | solution.py:23
  345.5 10.6 %all-to-all-done.13 = f32[16,1,12]{2,1,0:T(1,128)S(1)} async-done(((f32[16,1,12]{2,1,0:T(1,128)}), f32[16,1,12]{2,1,0:T(1,128)S(1)}, u32[]{:S(2)}, u32[]{:S(2)}) %all-to-all-start.13) | async-done | bytes 800 | tf_op jit(solution)/shard_map/all_to_all | solution.py:23
  (113 shorter events, 44.2 us)
Async XLA Ops:
  7.2 201.1 %all-gather.3.cloned.1.call-start = ((), (), s32[]{:S(2)}) async-start(), calls=%async_computation.14 | async-start | bytes 7372800 | tf_op jit(solution)/shard_map/all_gather | solution.py:260
  55.7 19.4 %copy-start.5 = (s32[3]{0:T(128)S(1)}, s32[3]{0:T(128)}, u32[]{:S(2)}) copy-start(s32[3]{0:T(128)} %param.13) | copy-start | bytes 40
  55.7 19.5 %copy-start.1 = (bf16[4,4,4,576]{3,2,1,0:T(4,128)(2,1)S(1)}, bf16[4,4,4,576]{3,2,1,0:T(4,128)(2,1)}, u32[]{:S(2)}) copy-start(bf16[4,4,4,576]{3,2,1,0:T(4,128)(2,1)} %param.12) | copy-start | bytes 221188
  55.7 19.5 %copy-start.2 = (bf16[4,4,4,576]{3,2,1,0:T(4,128)(2,1)S(1)}, bf16[4,4,4,576]{3,2,1,0:T(4,128)(2,1)}, u32[]{:S(2)}) copy-start(bf16[4,4,4,576]{3,2,1,0:T(4,128)(2,1)} %param.11) | copy-start | bytes 221188
  55.7 19.8 %copy-start.4 = (f32[3,576]{1,0:T(4,128)S(1)}, f32[3,576]{1,0:T(4,128)}, u32[]{:S(2)}) copy-start(f32[3,576]{1,0:T(4,128)} %param.10) | copy-start | bytes 20740
  55.7 33.7 %all-to-all-start = ((bf16[64,2,288]{2,1,0:T(2,128)(2,1)}), bf16[64,2,288]{2,1,0:T(2,128)(2,1)S(1)}, u32[]{:S(2)}, u32[]{:S(2)}) async-start(bf16[64,2,288]{2,1,0:T(2,128)(2,1)} %get-tuple-element.11), calls=%async_computation | async-start | bytes 196608 | tf_op jit(solution)/shard_map/all_to_all | solution.py:23
  75.0 200.8 %all-gather.5.cloned.1.call-start = ((), (), s32[]{:S(2)}) async-start(), calls=%async_computation.15 | async-start | bytes 7372800 | tf_op jit(solution)/shard_map/all_gather | solution.py:260
  158.6 22.2 %copy-start.3 = (bf16[1,576]{1,0:T(2,128)(2,1)S(1)}, bf16[1,576]{1,0:T(2,128)(2,1)}, u32[]{:S(2)}) copy-start(bf16[1,576]{1,0:T(2,128)(2,1)} %param.7) | copy-start | bytes 3460
  159.4 16.4 %all-to-all-start.2 = ((bf16[4,96,576]{2,1,0:T(8,128)(2,1)}), bf16[4,96,576]{2,1,0:T(8,128)(2,1)S(1)}, u32[]{:S(2)}, u32[]{:S(2)}) async-start(bf16[4,96,576]{2,1,0:T(8,128)(2,1)} %pad_maximum_fusion.4), calls=%async_computation.2 | async-start | bytes 983040 | tf_op jit(solution)/shard_map/all_to_all | solution.py:23
  176.5 15.1 %all-to-all-start.3 = ((bf16[16,4,576]{2,1,0:T(4,128)(2,1)}), bf16[16,4,576]{2,1,0:T(4,128)(2,1)S(1)}, u32[]{:S(2)}, u32[]{:S(2)}) async-start(bf16[16,4,576]{2,1,0:T(4,128)(2,1)} %reshape.268), calls=%async_computation.3 | async-start | bytes 163840 | tf_op jit(solution)/shard_map/all_to_all | solution.py:23
  192.4 15.1 %all-to-all-start.4 = ((bf16[16,4,576]{2,1,0:T(4,128)(2,1)}), bf16[16,4,576]{2,1,0:T(4,128)(2,1)S(1)}, u32[]{:S(2)}, u32[]{:S(2)}) async-start(bf16[16,4,576]{2,1,0:T(4,128)(2,1)} %broadcast_in_dim.27), calls=%async_computation.4 | async-start | bytes 163840 | tf_op jit(solution)/shard_map/all_to_all | solution.py:23
  212.6 15.4 %all-to-all-start.5 = ((bf16[8,8,2432]{2,1,0:T(8,128)(2,1)}), bf16[8,8,2432]{2,1,0:T(8,128)(2,1)S(1)}, u32[]{:S(2)}, u32[]{:S(2)}) async-start(bf16[8,8,2432]{2,1,0:T(8,128)(2,1)} %bitcast.67), calls=%async_computation.5 | async-start | bytes 622592 | tf_op jit(solution)/shard_map/all_to_all | solution.py:23
  280.2 12.8 %all-to-all-start.9 = ((bf16[8,8,2432]{2,1,0:T(8,128)(2,1)}), bf16[8,8,2432]{2,1,0:T(8,128)(2,1)S(1)}, u32[]{:S(2)}, u32[]{:S(2)}) async-start(bf16[8,8,2432]{2,1,0:T(8,128)(2,1)} %bitcast.66), calls=%async_computation.9 | async-start | bytes 622592 | tf_op jit(solution)/shard_map/all_to_all | solution.py:23
  294.1 11.3 %all-to-all-start.10 = ((bf16[8,8,2304]{2,1,0:T(8,128)(2,1)}), bf16[8,8,2304]{2,1,0:T(8,128)(2,1)S(1)}, u32[]{:S(2)}, u32[]{:S(2)}) async-start(bf16[8,8,2304]{2,1,0:T(8,128)(2,1)} %get-tuple-element.17), calls=%async_computation.10 | async-start | bytes 589824 | tf_op jit(solution)/shard_map/all_to_all | solution.py:23
  305.3 0.7 copy-start
  311.5 15.1 %all-to-all-start.11 = ((bf16[16,4,576]{2,1,0:T(4,128)(2,1)}), bf16[16,4,576]{2,1,0:T(4,128)(2,1)S(1)}, u32[]{:S(2)}, u32[]{:S(2)}) async-start(bf16[16,4,576]{2,1,0:T(4,128)(2,1)} %reshape.281), calls=%async_computation.11 | async-start | bytes 163840 | tf_op jit(solution)/shard_map/all_to_all | solution.py:23
  327.6 13.0 %all-to-all-start.12 = ((f32[32,1,16]{2,1,0:T(1,128)}), f32[32,1,16]{2,1,0:T(1,128)S(1)}, u32[]{:S(2)}, u32[]{:S(2)}) async-start(f32[32,1,16]{2,1,0:T(1,128)} %broadcast_in_dim.32), calls=%async_computation.12 | async-start | bytes 32768 | tf_op jit(solution)/shard_map/all_to_all | solution.py:23
  341.4 14.7 %all-to-all-start.13 = ((f32[16,1,12]{2,1,0:T(1,128)}), f32[16,1,12]{2,1,0:T(1,128)S(1)}, u32[]{:S(2)}, u32[]{:S(2)}) async-start(f32[16,1,12]{2,1,0:T(1,128)} %broadcast_in_dim.34), calls=%async_computation.13 | async-start | bytes 16384 | tf_op jit(solution)/shard_map/all_to_all | solution.py:23
Sparse Core Ops, SparseCore 0:
  55.9 75.9 all-gather.2
  156.8 63.1 all-gather.4

commit v6 on v5

--- a/solution.py
+++ b/solution.py
@@ -35,15 +35,6 @@
     return lax.broadcasted_iota(jnp.int32, (rows, SIDE), 1)
 
 
-def fetches(source, first, size, whole, sems):
-    return [
-        pltpu.make_async_copy(
-            source.at[i, pl.ds(first, size)], whole.at[pl.ds(i * size, size)], sems.at[i]
-        )
-        for i in range(source.shape[0])
-    ]
-
-
 def side_lanes(extras, square, along, low_lanes):
     lane = lanes(extras.shape[0])
     place = lane % HALF
@@ -55,21 +46,32 @@
 
 
 def pack_kernel(layer, *refs):
-    if len(refs) == 4:
-        w_in, w_out, out, sems = refs
-    else:
-        w_in, w_out, block, out, copies, sems = refs
+    *given, held, sems, done = refs
+    w_in, w_out = given[:2]
+    out = given[-1] if len(given) == 3 else given[-2]
     size = w_in.shape[1]
-    moves = [
-        pltpu.make_async_copy(w.at[layer], out.at[pl.ds(i * size, size)], sems.at[i])
-        for i, w in enumerate((w_in, w_out))
+    spans = [pl.ds(i * size, size) for i in range(2)]
+    here = [
+        pltpu.make_async_copy(w.at[layer], held.at[span], sems.at[i])
+        for i, (w, span) in enumerate(zip((w_in, w_out), spans))
     ]
-    for move in moves:
+    there = [
+        pltpu.make_async_copy(held.at[span], out.at[span], done.at[i])
+        for i, span in enumerate(spans)
+    ]
+    for move in here:
         move.start()
-    if len(refs) > 4:
-        copies[...] = jnp.broadcast_to(block[...][None], copies.shape)
-    for move in moves:
+    if len(given) > 3:
+        block, copies = given[2], given[-1]
+        half = copies.shape[2]
+        wide = block[...].astype(F32)
+        copies[:, 0] = jnp.broadcast_to(wide[:, :half], (copies.shape[0], half)).astype(BF)
+        copies[:, 1] = jnp.broadcast_to(wide[:, half:], (copies.shape[0], half)).astype(BF)
+    for move, back in zip(here, there):
         move.wait()
+        back.start()
+    for back in there:
+        back.wait()
 
 
 def pack(w_in, w_out, layer, block=None, count=0):
@@ -79,14 +81,18 @@
     out_shape = [jax.ShapeDtypeStruct((2 * size, width), BF)]
     given = [w_in, w_out]
     if block is not None:
-        given.append(block.reshape(2, width // 2))
+        given.append(block)
         out_shape.append(jax.ShapeDtypeStruct((count, 2, width // 2), BF))
     got = pl.pallas_call(
         functools.partial(pack_kernel, layer),
         out_shape=out_shape,
         in_specs=[hbm] * 2 + [vmem] * (len(given) - 2),
         out_specs=[hbm] + [vmem] * (len(out_shape) - 1),
-        scratch_shapes=[pltpu.SemaphoreType.DMA((2,))],
+        scratch_shapes=[
+            pltpu.VMEM((2 * size, width), BF),
+            pltpu.SemaphoreType.DMA((2,)),
+            pltpu.SemaphoreType.DMA((2,)),
+        ],
         compiler_params=pltpu.CompilerParams(vmem_limit_bytes=WIDE),
         name="pack",
     )(*given)
@@ -118,42 +124,31 @@
     )(stream, gain, left, weight)
 
 
-def enter_kernel(low_lanes, first, size, stream, gain, left, target, pick, source, out, whole, sems):
-    copies = fetches(source, first, size, whole, sems)
-    for copy in copies:
-        copy.start()
+def enter_kernel(low_lanes, stream, gain, left, target, pick, weight, out):
     wide = stream[...].astype(F32)
     scaled = (wide * gain[...]).astype(BF)
     square = jnp.sum(wide * wide, axis=1, keepdims=True)
     along = jnp.sum(wide * target[...].astype(F32), axis=1, keepdims=True)
     extras = dot_t(scaled, left[...]) * pick[...]
     out[:, :SIDE] = side_lanes(extras, square, along, low_lanes)
-    step = 2 * size
-    for i in range(len(copies) // 2):
-        copies[2 * i].wait()
-        copies[2 * i + 1].wait()
-        out[:, SIDE + i * step : SIDE + (i + 1) * step] = dot_t(
-            scaled, whole[i * step : (i + 1) * step]
-        ).astype(BF)
-
-
-def enter(stream, gain, left, target, pick, source, low_lanes, first, size):
+    out[:, SIDE:] = dot_t(scaled, weight[...]).astype(BF)
+
+
+def enter(stream, gain, left, target, pick, weight, low_lanes):
     rows, width = stream.shape
-    parts = source.shape[0]
-    hid = parts * size
+    hid = weight.shape[0]
     vmem = pl.BlockSpec(memory_space=pltpu.VMEM)
     return pl.pallas_call(
-        functools.partial(enter_kernel, low_lanes, first, size),
+        functools.partial(enter_kernel, low_lanes),
         out_shape=jax.ShapeDtypeStruct((rows, SIDE + hid), BF),
-        in_specs=[vmem] * 5 + [pl.BlockSpec(memory_space=pltpu.HBM)],
+        in_specs=[vmem] * 6,
         out_specs=vmem,
-        scratch_shapes=[pltpu.VMEM((hid, width), BF), pltpu.SemaphoreType.DMA((parts,))],
-        compiler_params=pltpu.CompilerParams(vmem_limit_bytes=WIDE),
+        compiler_params=pltpu.CompilerParams(vmem_limit_bytes=16 * MIB),
         cost_estimate=pl.CostEstimate(
             flops=2 * rows * hid * width, bytes_accessed=2 * hid * width, transcendentals=0
         ),
         name="enter",
-    )(stream, gain, left, target, pick, source)
+    )(stream, gain, left, target, pick, weight)
 
 
 def middle_kernel(low_lanes, got, right, out, side):
@@ -195,37 +190,25 @@
     )(got, right)
 
 
-def leave_kernel(first, size, gated, source, out, whole, sems):
-    copies = fetches(source, first, size, whole, sems)
-    for copy in copies:
-        copy.start()
-    step = 2 * size
-    total = None
-    for i in range(len(copies) // 2):
-        copies[2 * i].wait()
-        copies[2 * i + 1].wait()
-        here = slice(i * step, (i + 1) * step)
-        piece = jnp.dot(gated[:, here], whole[here], preferred_element_type=F32)
-        total = piece if total is None else total + piece
-    out[...] = total.astype(BF)
-
-
-def leave(gated, source, first, size):
+def leave_kernel(gated, weight, out):
+    out[...] = jnp.dot(gated[...], weight[...], preferred_element_type=F32).astype(BF)
+
+
+def leave(gated, weight):
     rows, hid = gated.shape
-    parts, _, width = source.shape
+    width = weight.shape[1]
     vmem = pl.BlockSpec(memory_space=pltpu.VMEM)
     return pl.pallas_call(
-        functools.partial(leave_kernel, first, size),
+        leave_kernel,
         out_shape=jax.ShapeDtypeStruct((rows, width), BF),
-        in_specs=[vmem, pl.BlockSpec(memory_space=pltpu.HBM)],
+        in_specs=[vmem] * 2,
         out_specs=vmem,
-        scratch_shapes=[pltpu.VMEM((hid, width), BF), pltpu.SemaphoreType.DMA((parts,))],
-        compiler_params=pltpu.CompilerParams(vmem_limit_bytes=WIDE),
+        compiler_params=pltpu.CompilerParams(vmem_limit_bytes=16 * MIB),
         cost_estimate=pl.CostEstimate(
             flops=2 * rows * hid * width, bytes_accessed=2 * hid * width, transcendentals=0
         ),
         name="leave",
-    )(gated, source)
+    )(gated, weight)
 
 
 def sided(factors):
@@ -301,8 +284,6 @@
                 + jnp.einsum("tmr,mrf->tmf", low, first_right, precision=lax.Precision.HIGHEST)
             )
             gated = jax.nn.silu(mixed).astype(BF).reshape(tok * members, hid)
-            far_in, far_out, gated = lax.optimization_barrier((w_in, w_out, gated))
-            near.append(gathered(pack(far_in, far_out, 2)))
             update = jnp.dot(gated, w_out[layer], preferred_element_type=F32).astype(BF)
             sent = jnp.concatenate(rights[1:], axis=0)
             sent = jnp.broadcast_to(sent[None], (nx, *sent.shape))
@@ -312,6 +293,8 @@
                 sided(later[i * low_lanes : (i + 1) * low_lanes]) for i in range(layers - 1)
             ]
             part = jnp.sum(part[:, :near_rows].astype(F32), axis=0).astype(BF)
+            part, far_in, far_out = lax.optimization_barrier((part, w_in, w_out))
+            near.append(gathered(pack(far_in, far_out, 2)))
         else:
             part = enter(
                 stream,
@@ -319,17 +302,16 @@
                 sided(lefts[layer]),
                 target,
                 pick,
-                near[layer - 1],
+                near[layer - 1][:, :hid].reshape(nx * hid, width),
                 low_lanes,
-                0,
-                hid,
             )
             part = swap(part.reshape(ns, chunk, -1), SEG)
             gated, side = middle(part, later[layer - 1], low_lanes)
             scores.append(jnp.sum(to_member * (side[:, 0] * own_weight), axis=1))
             gated = swap(gated, SEG)
             part = leave(
-                gated.reshape(near_rows, nx * hid), near[layer - 1], hid, hid
+                gated.reshape(near_rows, nx * hid),
+                near[layer - 1][:, hid:].reshape(nx * hid, width),
             )
         part = swap(part.reshape(nz, members, width), "z")
         mine = (mine.astype(F32) + jnp.sum(part.astype(F32), axis=0)).astype(BF)

time: 365 us -> 276 us (0.76)
  Pallas kernels: 111 us -> 14.1 us
  local copies, waits for them, and re-layouts: 13 us -> 24.1 us
  waiting for transfers between devices: 94.6 us -> 88.2 us
  starting transfers between devices: 61.4 us -> 65.4 us
    pallas_call x2, Pallas kernels: 92.9 us -> 5.94 us  [pack(): pl.pallas_call(functools.partial(pack_kernel, layer), out_shape=out_shape...]
    pallas_call x4, Pallas kernels: 16.6 us -> 4.14 us  [the longest x2 2.9 us: enter(): pl.pallas_call(functools.partial(enter_kernel, low_lanes), out_shape=jax....]
    slice x0 -> x2, local copies, waits for them, and re-layouts: none -> 6.61 us  [local(): near[layer - 1][:, hid:].reshape(nx * hid, width)]
    all_to_all x10, waiting for transfers between devices: 94.5 us -> 88.2 us  [swap(): return lax.all_to_all(chunks, axes, 0, 0, tiled=True)]
    all_to_all x10, starting transfers between devices: 61.4 us -> 65.4 us  [swap(): return lax.all_to_all(chunks, axes, 0, 0, tiled=True)]
  transfers between devices with their start and end apart: 12 -> 12, of which waited for: 10 -> 10; matrix products, arithmetic and copies ran while one was open for 4% -> 9% of each run, Pallas kernels for 15% -> 3%
where the time goes in v6:
time: 276 us; the launch traced here: 274 us
  waiting for transfers between devices  88.2 us (32%)
  starting transfers between devices  65.4 us (24%)
  blocking collectives  58 us (21%)
  local copies, waits for them, and re-layouts  24.1 us (9%)
  between operations  14.7 us (5%)
  Pallas kernels  14.1 us (5%)
  other arithmetic  7.91 us (3%)
    all_to_all x10, waiting for transfers between devices, swap(): return lax.all_to_all(chunks, axes, 0, 0, tiled=True)  88.2 us
    all_to_all x10, starting transfers between devices, swap(): return lax.all_to_all(chunks, axes, 0, 0, tiled=True)  65.4 us
    all_to_all x4, blocking collectives, swap(): return lax.all_to_all(chunks, axes, 0, 0, tiled=True)  58 us
    slice x2, local copies, waits for them, and re-layouts, local(): near[layer - 1][:, hid:].reshape(nx * hid, width)  6.61 us
    pallas_call x2, Pallas kernels, pack(): pl.pallas_call(functools.partial(pack_kernel, layer), out_shape=out_shape...  5.94 us
  transfers between devices with their start and end apart: 12, of which 10 were waited for; matrix products, arithmetic and copies ran while one was open for 9% of the time, Pallas kernels for 3%

profile of v6, /device:TPU:1, one launch (start us, length us, event | category | flops | bytes accessed | tf_op | source)
XLA Modules:
  0.0 274.5 jit_solution(396549110811640197)
XLA Ops:
  7.2 3.6 %pack.2 = (bf16[1152,576]{1,0:T(8,128)(2,1)}, bf16[64,2,288]{2,1,0:T(2,128)(2,1)}) custom-call(bf16[3,576,576]{2,1,0:T(8,128)(2,1)} %refs_0_.2, bf16[3,576,576]{2,1,0:T(8,128)(2,1)} %refs_1_.2, bf16[1,576]{1,0:T(2,128)(2,1)} %refs_2_.1), custom_call_target="tpu_custom_call" | custom-call | tf_op jit(solution)/shard_map/pack/pallas_call | solution.py:86
  10.9 19.1 %all-to-all-start = ((bf16[64,2,288]{2,1,0:T(2,128)(2,1)}), bf16[64,2,288]{2,1,0:T(2,128)(2,1)S(1)}, u32[]{:S(2)}, u32[]{:S(2)}) async-start(bf16[64,2,288]{2,1,0:T(2,128)(2,1)} %get-tuple-element.11), calls=%async_computation | async-start | bytes 196608 | tf_op jit(solution)/shard_map/all_to_all | solution.py:23
  32.5 12.1 %all-to-all-done = bf16[64,2,288]{2,1,0:T(2,128)(2,1)S(1)} async-done(((bf16[64,2,288]{2,1,0:T(2,128)(2,1)}), bf16[64,2,288]{2,1,0:T(2,128)(2,1)S(1)}, u32[]{:S(2)}, u32[]{:S(2)}) %all-to-all-start) | async-done | bytes 73760 | tf_op jit(solution)/shard_map/all_to_all | solution.py:23
  46.1 7.0 %all-to-all-start.1 = ((bf16[8,64,704]{2,1,0:T(8,128)(2,1)}), bf16[8,64,704]{2,1,0:T(8,128)(2,1)S(1)}, u32[]{:S(2)}, u32[]{:S(2)}) async-start(bf16[8,64,704]{2,1,0:T(8,128)(2,1)} %first.1), calls=%async_computation.1 | async-start | bytes 1572864 | tf_op jit(solution)/shard_map/all_to_all | solution.py:23
  53.2 12.2 %all-to-all-done.1 = bf16[8,64,704]{2,1,0:T(8,128)(2,1)S(1)} async-done(((bf16[8,64,704]{2,1,0:T(8,128)(2,1)}), bf16[8,64,704]{2,1,0:T(8,128)(2,1)S(1)}, u32[]{:S(2)}, u32[]{:S(2)}) %all-to-all-start.1) | async-done | bytes 720928 | tf_op jit(solution)/shard_map/all_to_all | solution.py:23
  68.8 16.6 %all_to_all.70 = bf16[4,96,576]{2,1,0:T(8,128)(2,1)S(1)} all-to-all(bf16[4,96,576]{2,1,0:T(8,128)(2,1)S(1)} %pad_maximum_fusion.4), channel_id=1, replica_groups=mesh['z'=16,'x'=4,'y'=4,'c'=2] {'x'}, dimensions={0} | all-to-all | bytes 884736 | tf_op jit(solution)/shard_map/all_to_all | solution.py:23
  88.5 3.5 %all-to-all-start.3 = ((bf16[16,4,576]{2,1,0:T(4,128)(2,1)}), bf16[16,4,576]{2,1,0:T(4,128)(2,1)S(1)}, u32[]{:S(2)}, u32[]{:S(2)}) async-start(bf16[16,4,576]{2,1,0:T(4,128)(2,1)} %reshape.276), calls=%async_computation.3 | async-start | bytes 163840 | tf_op jit(solution)/shard_map/all_to_all | solution.py:23
  93.2 10.5 %all-to-all-done.3 = bf16[16,4,576]{2,1,0:T(4,128)(2,1)S(1)} async-done(((bf16[16,4,576]{2,1,0:T(4,128)(2,1)}), bf16[16,4,576]{2,1,0:T(4,128)(2,1)S(1)}, u32[]{:S(2)}, u32[]{:S(2)}) %all-to-all-start.3) | async-done | bytes 73760 | tf_op jit(solution)/shard_map/all_to_all | solution.py:23
  104.4 3.5 %all-to-all-start.4 = ((bf16[16,4,576]{2,1,0:T(4,128)(2,1)}), bf16[16,4,576]{2,1,0:T(4,128)(2,1)S(1)}, u32[]{:S(2)}, u32[]{:S(2)}) async-start(bf16[16,4,576]{2,1,0:T(4,128)(2,1)} %broadcast_in_dim.27), calls=%async_computation.4 | async-start | bytes 163840 | tf_op jit(solution)/shard_map/all_to_all | solution.py:23
  109.5 10.0 %all-to-all-done.4 = bf16[16,4,576]{2,1,0:T(4,128)(2,1)S(1)} async-done(((bf16[16,4,576]{2,1,0:T(4,128)(2,1)}), bf16[16,4,576]{2,1,0:T(4,128)(2,1)S(1)}, u32[]{:S(2)}, u32[]{:S(2)}) %all-to-all-start.4) | async-done | bytes 73760 | tf_op jit(solution)/shard_map/all_to_all | solution.py:23
  125.4 8.3 %all-to-all-start.5 = ((bf16[8,8,2432]{2,1,0:T(8,128)(2,1)}), bf16[8,8,2432]{2,1,0:T(8,128)(2,1)}, u32[]{:S(2)}, u32[]{:S(2)}) async-start(bf16[8,8,2432]{2,1,0:T(8,128)(2,1)} %bitcast.12), calls=%async_computation.5 | async-start | bytes 622592 | tf_op jit(solution)/shard_map/all_to_all | solution.py:23
  135.7 5.2 %all-to-all-done.5.got = bf16[8,8,2432]{2,1,0:T(8,128)(2,1)} async-done(((bf16[8,8,2432]{2,1,0:T(8,128)(2,1)}), bf16[8,8,2432]{2,1,0:T(8,128)(2,1)}, u32[]{:S(2)}, u32[]{:S(2)}) %all-to-all-start.5) | async-done | bytes 311328 | tf_op jit(solution)/shard_map/all_to_all | solution.py:23
  143.3 10.8 %all_to_all.71 = bf16[8,8,2304]{2,1,0:T(8,128)(2,1)S(1)} all-to-all(bf16[8,8,2304]{2,1,0:T(8,128)(2,1)S(1)} %get-tuple-element.14), channel_id=1, replica_groups=mesh['z'=16,'x'=4,'y'=4,'c'=2] {'y','c'}, dimensions={0} | all-to-all | bytes 589824 | tf_op jit(solution)/shard_map/all_to_all | solution.py:23
  156.3 14.7 %all_to_all.72 = bf16[16,4,576]{2,1,0:T(4,128)(2,1)S(1)} all-to-all(bf16[16,4,576]{2,1,0:T(4,128)(2,1)S(1)} %reshape.286), channel_id=1, replica_groups=mesh['z'=16,'x'=4,'y'=4,'c'=2] {'z'}, dimensions={0} | all-to-all | bytes 147456 | tf_op jit(solution)/shard_map/all_to_all | solution.py:23
  172.4 15.9 %all_to_all.73 = bf16[16,4,576]{2,1,0:T(4,128)(2,1)S(1)} all-to-all(bf16[16,4,576]{2,1,0:T(4,128)(2,1)S(1)} %broadcast_in_dim.29), channel_id=1, replica_groups=mesh['z'=16,'x'=4,'y'=4,'c'=2] {'z'}, dimensions={0} | all-to-all | bytes 147456 | tf_op jit(solution)/shard_map/all_to_all | solution.py:23
  194.1 6.4 %all-to-all-start.9 = ((bf16[8,8,2432]{2,1,0:T(8,128)(2,1)}), bf16[8,8,2432]{2,1,0:T(8,128)(2,1)}, u32[]{:S(2)}, u32[]{:S(2)}) async-start(bf16[8,8,2432]{2,1,0:T(8,128)(2,1)} %bitcast.68), calls=%async_computation.9 | async-start | bytes 622592 | tf_op jit(solution)/shard_map/all_to_all | solution.py:23
  209.7 4.6 %all-to-all-start.10 = ((bf16[8,8,2304]{2,1,0:T(8,128)(2,1)}), bf16[8,8,2304]{2,1,0:T(8,128)(2,1)S(1)}, u32[]{:S(2)}, u32[]{:S(2)}) async-start(bf16[8,8,2304]{2,1,0:T(8,128)(2,1)} %copy-done.11), calls=%async_computation.10 | async-start | bytes 589824 | tf_op jit(solution)/shard_map/all_to_all | solution.py:23
  215.1 5.9 %all-to-all-done.10 = bf16[8,8,2304]{2,1,0:T(8,128)(2,1)S(1)} async-done(((bf16[8,8,2304]{2,1,0:T(8,128)(2,1)}), bf16[8,8,2304]{2,1,0:T(8,128)(2,1)S(1)}, u32[]{:S(2)}, u32[]{:S(2)}) %all-to-all-start.10) | async-done | bytes 294944 | tf_op jit(solution)/shard_map/all_to_all | solution.py:23
  222.4 3.5 %all-to-all-start.11 = ((bf16[16,4,576]{2,1,0:T(4,128)(2,1)}), bf16[16,4,576]{2,1,0:T(4,128)(2,1)S(1)}, u32[]{:S(2)}, u32[]{:S(2)}) async-start(bf16[16,4,576]{2,1,0:T(4,128)(2,1)} %reshape.293), calls=%async_computation.11 | async-start | bytes 163840 | tf_op jit(solution)/shard_map/all_to_all | solution.py:23
  226.0 11.5 %all-to-all-done.11 = bf16[16,4,576]{2,1,0:T(4,128)(2,1)S(1)} async-done(((bf16[16,4,576]{2,1,0:T(4,128)(2,1)}), bf16[16,4,576]{2,1,0:T(4,128)(2,1)S(1)}, u32[]{:S(2)}, u32[]{:S(2)}) %all-to-all-start.11) | async-done | bytes 73760 | tf_op jit(solution)/shard_map/all_to_all | solution.py:23
  238.4 5.9 %all-to-all-start.12 = ((f32[32,1,16]{2,1,0:T(1,128)}), f32[32,1,16]{2,1,0:T(1,128)S(1)}, u32[]{:S(2)}, u32[]{:S(2)}) async-start(f32[32,1,16]{2,1,0:T(1,128)} %broadcast_in_dim.32), calls=%async_computation.12 | async-start | bytes 32768 | tf_op jit(solution)/shard_map/all_to_all | solution.py:23
  244.4 7.0 %all-to-all-done.12 = f32[32,1,16]{2,1,0:T(1,128)S(1)} async-done(((f32[32,1,16]{2,1,0:T(1,128)}), f32[32,1,16]{2,1,0:T(1,128)S(1)}, u32[]{:S(2)}, u32[]{:S(2)}) %all-to-all-start.12) | async-done | bytes 2080 | tf_op jit(solution)/shard_map/all_to_all | solution.py:23
  252.3 3.5 %all-to-all-start.13 = ((f32[16,1,12]{2,1,0:T(1,128)}), f32[16,1,12]{2,1,0:T(1,128)S(1)}, u32[]{:S(2)}, u32[]{:S(2)}) async-start(f32[16,1,12]{2,1,0:T(1,128)} %broadcast_in_dim.34), calls=%async_computation.13 | async-start | bytes 16384 | tf_op jit(solution)/shard_map/all_to_all | solution.py:23
  256.4 10.6 %all-to-all-done.13 = f32[16,1,12]{2,1,0:T(1,128)S(1)} async-done(((f32[16,1,12]{2,1,0:T(1,128)}), f32[16,1,12]{2,1,0:T(1,128)S(1)}, u32[]{:S(2)}, u32[]{:S(2)}) %all-to-all-start.13) | async-done | bytes 800 | tf_op jit(solution)/shard_map/all_to_all | solution.py:23
  (151 shorter events, 47.8 us)
Async XLA Ops:
  7.2 22.9 %copy-start.23 = (s32[3]{0:T(128)S(1)}, s32[3]{0:T(128)}, u32[]{:S(2)}) copy-start(s32[3]{0:T(128)} %param.13) | copy-start | bytes 40
  7.2 22.9 %copy-start.17 = (bf16[4,4,4,576]{3,2,1,0:T(4,128)(2,1)S(1)}, bf16[4,4,4,576]{3,2,1,0:T(4,128)(2,1)}, u32[]{:S(2)}) copy-start(bf16[4,4,4,576]{3,2,1,0:T(4,128)(2,1)} %param.12) | copy-start | bytes 221188
  7.2 22.9 %copy-start.18 = (bf16[4,4,4,576]{3,2,1,0:T(4,128)(2,1)S(1)}, bf16[4,4,4,576]{3,2,1,0:T(4,128)(2,1)}, u32[]{:S(2)}) copy-start(bf16[4,4,4,576]{3,2,1,0:T(4,128)(2,1)} %param.11) | copy-start | bytes 221188
  7.2 23.3 %copy-start.22 = (f32[3,576]{1,0:T(4,128)S(1)}, f32[3,576]{1,0:T(4,128)}, u32[]{:S(2)}) copy-start(f32[3,576]{1,0:T(4,128)} %param.10) | copy-start | bytes 20740
  7.2 113.0 %all-gather.3.cloned.1.call-start = ((), (), s32[]{:S(2)}) async-start(), calls=%async_computation.14 | async-start | bytes 7372800 | tf_op jit(solution)/shard_map/all_gather | solution.py:243
  10.9 33.7 %all-to-all-start = ((bf16[64,2,288]{2,1,0:T(2,128)(2,1)}), bf16[64,2,288]{2,1,0:T(2,128)(2,1)S(1)}, u32[]{:S(2)}, u32[]{:S(2)}) async-start(bf16[64,2,288]{2,1,0:T(2,128)(2,1)} %get-tuple-element.11), calls=%async_computation | async-start | bytes 196608 | tf_op jit(solution)/shard_map/all_to_all | solution.py:23
  46.1 19.3 %all-to-all-start.1 = ((bf16[8,64,704]{2,1,0:T(8,128)(2,1)}), bf16[8,64,704]{2,1,0:T(8,128)(2,1)S(1)}, u32[]{:S(2)}, u32[]{:S(2)}) async-start(bf16[8,64,704]{2,1,0:T(8,128)(2,1)} %first.1), calls=%async_computation.1 | async-start | bytes 1572864 | tf_op jit(solution)/shard_map/all_to_all | solution.py:23
  53.1 135.8 %all-gather.5.cloned.1.call-start = ((), (), s32[]{:S(2)}) async-start(), calls=%async_computation.15 | async-start | bytes 7372800 | tf_op jit(solution)/shard_map/all_gather | solution.py:243
  85.5 6.7 %copy-start.21 = (bf16[1,576]{1,0:T(2,128)(2,1)S(1)}, bf16[1,576]{1,0:T(2,128)(2,1)}, u32[]{:S(2)}) copy-start(bf16[1,576]{1,0:T(2,128)(2,1)} %refs_2_.1) | copy-start | bytes 3460
  88.5 15.1 %all-to-all-start.3 = ((bf16[16,4,576]{2,1,0:T(4,128)(2,1)}), bf16[16,4,576]{2,1,0:T(4,128)(2,1)S(1)}, u32[]{:S(2)}, u32[]{:S(2)}) async-start(bf16[16,4,576]{2,1,0:T(4,128)(2,1)} %reshape.276), calls=%async_computation.3 | async-start | bytes 163840 | tf_op jit(solution)/shard_map/all_to_all | solution.py:23
  92.1 31.5 %copy-start.9 = (f32[64,128]{1,0:T(8,128)}, f32[64,128]{1,0:T(8,128)S(1)}, u32[]{:S(2)}) copy-start(f32[64,128]{1,0:T(8,128)S(1)} %and_convert_fusion.pick) | copy-start | bytes 98308
  93.2 30.4 %copy-start.2 = (bf16[64,576]{1,0:T(8,128)(2,1)}, bf16[64,576]{1,0:T(8,128)(2,1)S(1)}, u32[]{:S(2)}) copy-start(bf16[64,576]{1,0:T(8,128)(2,1)S(1)} %reshape.280.target) | copy-start | bytes 221188
  104.4 15.1 %all-to-all-start.4 = ((bf16[16,4,576]{2,1,0:T(4,128)(2,1)}), bf16[16,4,576]{2,1,0:T(4,128)(2,1)S(1)}, u32[]{:S(2)}, u32[]{:S(2)}) async-start(bf16[16,4,576]{2,1,0:T(4,128)(2,1)} %broadcast_in_dim.27), calls=%async_computation.4 | async-start | bytes 163840 | tf_op jit(solution)/shard_map/all_to_all | solution.py:23
  120.2 3.4 %copy-start.8 = (bf16[64,576]{1,0:T(8,128)(2,1)S(1)}, bf16[64,576]{1,0:T(8,128)(2,1)}, u32[]{:S(2)}) copy-start(bf16[64,576]{1,0:T(8,128)(2,1)} %reshape.277.stream) | copy-start | bytes 221188
  125.4 15.4 %all-to-all-start.5 = ((bf16[8,8,2432]{2,1,0:T(8,128)(2,1)}), bf16[8,8,2432]{2,1,0:T(8,128)(2,1)}, u32[]{:S(2)}, u32[]{:S(2)}) async-start(bf16[8,8,2432]{2,1,0:T(8,128)(2,1)} %bitcast.12), calls=%async_computation.5 | async-start | bytes 622592 | tf_op jit(solution)/shard_map/all_to_all | solution.py:23
  194.1 13.5 %all-to-all-start.9 = ((bf16[8,8,2432]{2,1,0:T(8,128)(2,1)}), bf16[8,8,2432]{2,1,0:T(8,128)(2,1)}, u32[]{:S(2)}, u32[]{:S(2)}) async-start(bf16[8,8,2432]{2,1,0:T(8,128)(2,1)} %bitcast.68), calls=%async_computation.9 | async-start | bytes 622592 | tf_op jit(solution)/shard_map/all_to_all | solution.py:23
  209.7 16.2 %copy-start.24 = (s32[8]{0:T(128)S(1)}, s32[8]{0:T(128)}, u32[]{:S(2)}) copy-start(s32[8]{0:T(128)} %and_select_fusion) | copy-start | bytes 100
  209.7 27.9 %copy-start.20 = (bf16[4,576]{1,0:T(4,128)(2,1)S(1)}, bf16[4,576]{1,0:T(4,128)(2,1)}, u32[]{:S(2)}) copy-start(bf16[4,576]{1,0:T(4,128)(2,1)} %copy-done.19) | copy-start | bytes 13828
  209.7 46.1 %copy-start.14 = (f32[4,576]{1,0:T(4,128)S(1)}, f32[4,576]{1,0:T(4,128)}, u32[]{:S(2)}) copy-start(f32[4,576]{1,0:T(4,128)} %copy-done.13) | copy-start | bytes 27652
  209.7 46.1 %copy-start.16 = (f32[4,576]{1,0:T(4,128)S(1)}, f32[4,576]{1,0:T(4,128)}, u32[]{:S(2)}) copy-start(f32[4,576]{1,0:T(4,128)} %copy-done.15) | copy-start | bytes 27652
  209.7 11.4 %all-to-all-start.10 = ((bf16[8,8,2304]{2,1,0:T(8,128)(2,1)}), bf16[8,8,2304]{2,1,0:T(8,128)(2,1)S(1)}, u32[]{:S(2)}, u32[]{:S(2)}) async-start(bf16[8,8,2304]{2,1,0:T(8,128)(2,1)} %copy-done.11), calls=%async_computation.10 | async-start | bytes 589824 | tf_op jit(solution)/shard_map/all_to_all | solution.py:23
  222.4 15.1 %all-to-all-start.11 = ((bf16[16,4,576]{2,1,0:T(4,128)(2,1)}), bf16[16,4,576]{2,1,0:T(4,128)(2,1)S(1)}, u32[]{:S(2)}, u32[]{:S(2)}) async-start(bf16[16,4,576]{2,1,0:T(4,128)(2,1)} %reshape.293), calls=%async_computation.11 | async-start | bytes 163840 | tf_op jit(solution)/shard_map/all_to_all | solution.py:23
  238.4 13.0 %all-to-all-start.12 = ((f32[32,1,16]{2,1,0:T(1,128)}), f32[32,1,16]{2,1,0:T(1,128)S(1)}, u32[]{:S(2)}, u32[]{:S(2)}) async-start(f32[32,1,16]{2,1,0:T(1,128)} %broadcast_in_dim.32), calls=%async_computation.12 | async-start | bytes 32768 | tf_op jit(solution)/shard_map/all_to_all | solution.py:23
  252.3 14.7 %all-to-all-start.13 = ((f32[16,1,12]{2,1,0:T(1,128)}), f32[16,1,12]{2,1,0:T(1,128)S(1)}, u32[]{:S(2)}, u32[]{:S(2)}) async-start(f32[16,1,12]{2,1,0:T(1,128)} %broadcast_in_dim.34), calls=%async_computation.13 | async-start | bytes 16384 | tf_op jit(solution)/shard_map/all_to_all | solution.py:23
  (13 other events, 22.4 us)
Sparse Core Ops, SparseCore 0:
  11.0 81.2 all-gather.2
  94.4 70.1 all-gather.4

commit v7 on v6

--- a/solution.py
+++ b/solution.py
@@ -12,6 +12,9 @@
 BF = jnp.bfloat16
 F32 = jnp.float32
 SEG = ("y", "c")
+NEAR = ("h", "l")
+FAR = "a"
+DEEP = (FAR, *NEAR)
 EPS = 1e-06
 HALF = 64
 SIDE = 128
@@ -124,8 +127,38 @@
     )(stream, gain, left, weight)
 
 
-def enter_kernel(low_lanes, stream, gain, left, target, pick, weight, out):
-    wide = stream[...].astype(F32)
+def summed(parts):
+    total = parts[0].astype(F32)
+    for i in range(1, parts.shape[0]):
+        total += parts[i].astype(F32)
+    return total
+
+
+def fold_kernel(rows, parts, out):
+    total = parts[0, :rows].astype(F32)
+    for i in range(1, parts.shape[0]):
+        total += parts[i, :rows].astype(F32)
+    total = total.astype(BF)
+    for i in range(out.shape[0]):
+        out[i] = total
+
+
+def fold(parts, count, rows):
+    vmem = pl.BlockSpec(memory_space=pltpu.VMEM)
+    return pl.pallas_call(
+        functools.partial(fold_kernel, rows),
+        out_shape=jax.ShapeDtypeStruct((count, rows, parts.shape[2]), BF),
+        in_specs=[vmem],
+        out_specs=vmem,
+        compiler_params=pltpu.CompilerParams(vmem_limit_bytes=8 * MIB),
+        name="fold",
+    )(parts)
+
+
+def enter_kernel(low_lanes, parts, before, gain, left, target, pick, weight, out, stream):
+    fresh = (before[...].astype(F32) + summed(parts)).astype(BF)
+    stream[...] = fresh
+    wide = fresh.astype(F32)
     scaled = (wide * gain[...]).astype(BF)
     square = jnp.sum(wide * wide, axis=1, keepdims=True)
     along = jnp.sum(wide * target[...].astype(F32), axis=1, keepdims=True)
@@ -134,21 +167,49 @@
     out[:, SIDE:] = dot_t(scaled, weight[...]).astype(BF)
 
 
-def enter(stream, gain, left, target, pick, weight, low_lanes):
-    rows, width = stream.shape
+def enter(parts, before, gain, left, target, pick, weight, low_lanes):
+    rows, width = before.shape
     hid = weight.shape[0]
     vmem = pl.BlockSpec(memory_space=pltpu.VMEM)
     return pl.pallas_call(
         functools.partial(enter_kernel, low_lanes),
-        out_shape=jax.ShapeDtypeStruct((rows, SIDE + hid), BF),
-        in_specs=[vmem] * 6,
-        out_specs=vmem,
+        out_shape=(
+            jax.ShapeDtypeStruct((rows, SIDE + hid), BF),
+            jax.ShapeDtypeStruct((rows, width), BF),
+        ),
+        in_specs=[vmem] * 7,
+        out_specs=(vmem, vmem),
         compiler_params=pltpu.CompilerParams(vmem_limit_bytes=16 * MIB),
         cost_estimate=pl.CostEstimate(
             flops=2 * rows * hid * width, bytes_accessed=2 * hid * width, transcendentals=0
         ),
         name="enter",
-    )(stream, gain, left, target, pick, weight)
+    )(parts, before, gain, left, target, pick, weight)
+
+
+def last_kernel(parts, before, target, out, sides):
+    fresh = (before[...].astype(F32) + summed(parts)).astype(BF)
+    out[...] = fresh
+    wide = fresh.astype(F32)
+    square = jnp.sum(wide * wide, axis=1, keepdims=True)
+    along = jnp.sum(wide * target[...].astype(F32), axis=1, keepdims=True)
+    sides[...] = jnp.where(lanes(fresh.shape[0]) < HALF, square, along)
+
+
+def last(parts, before, target):
+    rows, width = before.shape
+    vmem = pl.BlockSpec(memory_space=pltpu.VMEM)
+    return pl.pallas_call(
+        last_kernel,
+        out_shape=(
+            jax.ShapeDtypeStruct((rows, width), BF),
+            jax.ShapeDtypeStruct((rows, SIDE), F32),
+        ),
+        in_specs=[vmem] * 3,
+        out_specs=(vmem, vmem),
+        compiler_params=pltpu.CompilerParams(vmem_limit_bytes=8 * MIB),
+        name="last",
+    )(parts, before, target)
 
 
 def middle_kernel(low_lanes, got, right, out, side):
@@ -191,16 +252,18 @@
 
 
 def leave_kernel(gated, weight, out):
-    out[...] = jnp.dot(gated[...], weight[...], preferred_element_type=F32).astype(BF)
-
-
-def leave(gated, weight):
+    part = jnp.dot(gated[...], weight[...], preferred_element_type=F32).astype(BF)
+    for i in range(out.shape[0]):
+        out[i] = part
+
+
+def leave(gated, weight, count):
     rows, hid = gated.shape
     width = weight.shape[1]
     vmem = pl.BlockSpec(memory_space=pltpu.VMEM)
     return pl.pallas_call(
         leave_kernel,
-        out_shape=jax.ShapeDtypeStruct((rows, width), BF),
+        out_shape=jax.ShapeDtypeStruct((count, rows, width), BF),
         in_specs=[vmem] * 2,
         out_specs=vmem,
         compiler_params=pltpu.CompilerParams(vmem_limit_bytes=16 * MIB),
@@ -217,7 +280,8 @@
 
 
 def local(block, w_in, w_out, gains, fac_left, right_perturb_factors, assign):
-    nz, nx = lax.axis_size("z"), lax.axis_size("x")
+    nz, nx = lax.axis_size(DEEP), lax.axis_size("x")
+    nf, nn = lax.axis_size(FAR), lax.axis_size(NEAR)
     ny = lax.axis_size("y")
     ns = ny * lax.axis_size("c")
     width = block.shape[1]
@@ -226,7 +290,7 @@
     members, _, rank, _ = fac_left.shape
     low_lanes = members * rank
     tok = nz * nx
-    z, x = lax.axis_index("z"), lax.axis_index("x")
+    z, x = lax.axis_index(DEEP), lax.axis_index("x")
     seg = lax.axis_index("y") * lax.axis_size("c") + lax.axis_index("c")
 
     chosen = (jnp.arange(fac_left.shape[1])[None] == assign[:, None]).astype(F32)
@@ -245,8 +309,10 @@
 
     packed, copies = pack(w_in, w_out, 1, block, tok)
     near = [gathered(packed)]
-    base = swap(copies, ("z", "x")).reshape(nz, nx, width)
+    base = swap(copies, (*DEEP, "x")).reshape(nz, nx, width)
     natural = base.reshape(tok, width)
+    near_base = lax.dynamic_slice(base, (0, x, 0), (nz, 1, width))
+    stream = jnp.repeat(near_base.reshape(nz, width), members, axis=0)
     base = jnp.swapaxes(base, 0, 1).reshape(tok, width)
     after = jnp.concatenate([natural[1:], jnp.zeros((1, width), BF)], axis=0)
     near_after = lax.dynamic_slice(after.reshape(nz, nx, width), (0, x, 0), (nz, 1, width))
@@ -267,9 +333,8 @@
     own_weight = lax.dynamic_slice(row_weight, (seg * chunk,), (chunk,))
     to_member = (own_member[None] == jnp.arange(members)[:, None]).astype(F32)
 
-    mine = jnp.broadcast_to(block, (members, width))
     scores = []
-    stream = None
+    parts = None
     for layer in range(layers):
         gain = gains[layer]
         if layer == 0:
@@ -292,59 +357,52 @@
             later = [
                 sided(later[i * low_lanes : (i + 1) * low_lanes]) for i in range(layers - 1)
             ]
-            part = jnp.sum(part[:, :near_rows].astype(F32), axis=0).astype(BF)
+            part = fold(part, nn, near_rows)
             part, far_in, far_out = lax.optimization_barrier((part, w_in, w_out))
             near.append(gathered(pack(far_in, far_out, 2)))
         else:
-            part = enter(
+            part, stream = enter(
+                parts,
                 stream,
                 gain[None],
                 sided(lefts[layer]),
                 target,
                 pick,
-                near[layer - 1][:, :hid].reshape(nx * hid, width),
+                weight_in,
                 low_lanes,
             )
             part = swap(part.reshape(ns, chunk, -1), SEG)
             gated, side = middle(part, later[layer - 1], low_lanes)
             scores.append(jnp.sum(to_member * (side[:, 0] * own_weight), axis=1))
-            gated = swap(gated, SEG)
-            part = leave(
-                gated.reshape(near_rows, nx * hid),
-                near[layer - 1][:, hid:].reshape(nx * hid, width),
+            gated, weight_out = lax.optimization_barrier(
+                (swap(gated, SEG), near[layer - 1][:, hid:].reshape(nx * hid, width))
             )
-        part = swap(part.reshape(nz, members, width), "z")
-        mine = (mine.astype(F32) + jnp.sum(part.astype(F32), axis=0)).astype(BF)
+            part = leave(gated.reshape(near_rows, nx * hid), weight_out, nn)
+        parts = swap(fold(swap(part, NEAR), nf, near_rows), FAR)
         if layer < layers - 1:
-            stream = share(mine, "z", nz)
-            stream = stream.reshape(near_rows, width)
-
-    wide = mine.astype(F32)
-    my_target = lax.dynamic_slice(near_after, (z, 0), (1, width)).astype(F32)
-    once = jnp.where(z == 0, 1.0, 0.0)
-    sums = jnp.concatenate(
-        [
-            jnp.sum(wide * wide, axis=1),
-            jnp.sum(wide * my_target, axis=1),
-            *[once * s for s in scores],
-        ]
-    )
+            parts, weight_in = lax.optimization_barrier(
+                (parts, near[layer][:, :hid].reshape(nx * hid, width))
+            )
+
+    final, sides = last(parts, stream, target)
+    sums = jnp.concatenate([sides[:, 0], sides[:, HALF], *scores])
     count = nx * ns
     got = share(sums[None], ("x", *SEG), count).reshape(nx, ns, -1)
     got = jnp.sum(got, axis=1)
-    tokens = z * nx + jnp.arange(nx)
+    square, along = got[:, :near_rows], got[:, near_rows : 2 * near_rows]
+    tokens = (jnp.arange(near_rows) // members)[None] * nx + jnp.arange(nx)[:, None]
     weights = jnp.where(tokens < tok - 1, 1.0 + 2.0 * tokens.astype(F32) / (tok - 2), 0.0)
-    square, along = got[:, :members], got[:, members : 2 * members]
-    last = jnp.sum(along * lax.rsqrt(square / D + EPS) * weights[:, None], axis=0)
-    earlier = jnp.sum(got[:, 2 * members :], axis=0)
-    both = jnp.concatenate([earlier, last])
-    both = jnp.sum(share(both[None], "z", nz).reshape(nz, -1), axis=0)
-    return both.reshape(layers, members) / math.sqrt((tok - 1) * D), mine[None]
+    each = along * lax.rsqrt(square / D + EPS) * weights
+    latest = jnp.sum(each.reshape(nx * nz, members), axis=0)
+    earlier = jnp.sum(got[:, 2 * near_rows :], axis=0)
+    both = jnp.concatenate([earlier, latest])
+    mine = lax.dynamic_slice(final.reshape(nz, members, width), (z, 0, 0), (1, members, width))
+    return both.reshape(layers, members) / math.sqrt((tok - 1) * D), mine
 
 
 def solution(mesh):
-    split = Mesh(mesh.devices.reshape(16, 4, 4, 2), ("z", "x", "y", "c"))
-    pop = ("z", "x")
+    split = Mesh(mesh.devices.reshape(4, 2, 2, 4, 4, 2), (*DEEP, "x", *SEG))
+    pop = (*DEEP, "x")
     return jax.shard_map(
         local,
         mesh=split,

time: 276 us -> 289 us (1.047)
  local copies, waits for them, and re-layouts: 24.1 us -> 29.1 us
  blocking collectives: 58 us -> 63 us
  other arithmetic: 7.91 us -> 4.08 us
  Pallas kernels: 14.1 us -> 17.3 us
    unnamed x51 -> x43, local copies, waits for them, and re-layouts: 4.35 us -> 11.1 us
    all_to_all x4 -> x5, blocking collectives: 58 us -> 63 us  [swap(): return lax.all_to_all(chunks, axes, 0, 0, tiled=True)]
    pallas_call x4 -> x9, Pallas kernels: 4.14 us -> 8.34 us  [the longest x2 3.14 us: enter(): pl.pallas_call(functools.partial(enter_kernel, low_lanes), out_shape=(jax...]
    slice x2, local copies, waits for them, and re-layouts: 6.61 us -> 9.78 us  [local(): near[layer - 1][:, hid:].reshape(nx * hid, width)]
    all_to_all x10 -> x9, waiting for transfers between devices: 88.2 us -> 90.2 us  [swap(): return lax.all_to_all(chunks, axes, 0, 0, tiled=True)]
    all_to_all x10 -> x9, starting transfers between devices: 65.4 us -> 67.4 us  [swap(): return lax.all_to_all(chunks, axes, 0, 0, tiled=True)]
  transfers between devices with their start and end apart: 12 -> 11, of which waited for: 10 -> 9; matrix products, arithmetic and copies ran while one was open for 9% -> 8% of each run, Pallas kernels for 3% -> 3%
where the time goes in v7:
time: 289 us; the launch traced here: 288 us
  waiting for transfers between devices  90.3 us (31%)
  starting transfers between devices  67.4 us (23%)
  blocking collectives  63 us (22%)
  local copies, waits for them, and re-layouts  29.1 us (10%)
  Pallas kernels  17.3 us (6%)
  between operations  14.5 us (5%)
  other arithmetic  4.08 us (1%)
    all_to_all x9, waiting for transfers between devices, swap(): return lax.all_to_all(chunks, axes, 0, 0, tiled=True)  90.2 us
    all_to_all x9, starting transfers between devices, swap(): return lax.all_to_all(chunks, axes, 0, 0, tiled=True)  67.4 us
    all_to_all x5, blocking collectives, swap(): return lax.all_to_all(chunks, axes, 0, 0, tiled=True)  63 us
    unnamed x43, local copies, waits for them, and re-layouts  11.1 us
    slice x2, local copies, waits for them, and re-layouts, local(): near[layer - 1][:, hid:].reshape(nx * hid, width)  9.78 us
    pallas_call x2, Pallas kernels, pack(): pl.pallas_call(functools.partial(pack_kernel, layer), out_shape=out_shape...  5.98 us
  transfers between devices with their start and end apart: 11, of which 9 were waited for; matrix products, arithmetic and copies ran while one was open for 8% of the time, Pallas kernels for 3%

profile of v7, /device:TPU:1, one launch (start us, length us, event | category | flops | bytes accessed | tf_op | source)
XLA Modules:
  0.0 287.9 jit_solution(11887906052916452393)
XLA Ops:
  7.2 3.7 %pack.2 = (bf16[1152,576]{1,0:T(8,128)(2,1)}, bf16[64,2,288]{2,1,0:T(2,128)(2,1)}) custom-call(bf16[3,576,576]{2,1,0:T(8,128)(2,1)} %refs_0_.2, bf16[3,576,576]{2,1,0:T(8,128)(2,1)} %refs_1_.2, bf16[1,576]{1,0:T(2,128)(2,1)} %refs_2_.1), custom_call_target="tpu_custom_call" | custom-call | tf_op jit(solution)/shard_map/pack/pallas_call | solution.py:89
  11.0 19.1 %all-to-all-start = ((bf16[64,2,288]{2,1,0:T(2,128)(2,1)}), bf16[64,2,288]{2,1,0:T(2,128)(2,1)S(1)}, u32[]{:S(2)}, u32[]{:S(2)}) async-start(bf16[64,2,288]{2,1,0:T(2,128)(2,1)} %get-tuple-element.25), calls=%async_computation | async-start | bytes 196608 | tf_op jit(solution)/shard_map/all_to_all | solution.py:26
  33.2 11.5 %all-to-all-done = bf16[64,2,288]{2,1,0:T(2,128)(2,1)S(1)} async-done(((bf16[64,2,288]{2,1,0:T(2,128)(2,1)}), bf16[64,2,288]{2,1,0:T(2,128)(2,1)S(1)}, u32[]{:S(2)}, u32[]{:S(2)}) %all-to-all-start) | async-done | bytes 73760 | tf_op jit(solution)/shard_map/all_to_all | solution.py:26
  46.2 7.2 %all-to-all-start.1 = ((bf16[8,64,704]{2,1,0:T(8,128)(2,1)}), bf16[8,64,704]{2,1,0:T(8,128)(2,1)S(1)}, u32[]{:S(2)}, u32[]{:S(2)}) async-start(bf16[8,64,704]{2,1,0:T(8,128)(2,1)} %first.1), calls=%async_computation.1 | async-start | bytes 1572864 | tf_op jit(solution)/shard_map/all_to_all | solution.py:26
  53.4 12.2 %all-to-all-done.1 = bf16[8,64,704]{2,1,0:T(8,128)(2,1)S(1)} async-done(((bf16[8,64,704]{2,1,0:T(8,128)(2,1)}), bf16[8,64,704]{2,1,0:T(8,128)(2,1)S(1)}, u32[]{:S(2)}, u32[]{:S(2)}) %all-to-all-start.1) | async-done | bytes 720928 | tf_op jit(solution)/shard_map/all_to_all | solution.py:26
  69.0 16.6 %all_to_all.70.parts = bf16[4,96,576]{2,1,0:T(8,128)(2,1)S(1)} all-to-all(bf16[4,96,576]{2,1,0:T(8,128)(2,1)S(1)} %pad_maximum_fusion.4), channel_id=1, replica_groups=mesh['a'=4,'h'=2,'l'=2,'x'=4,'y'=4,'c'=2] {'x'}, dimensions={0} | all-to-all | bytes 884736 | tf_op jit(solution)/shard_map/all_to_all | solution.py:26
  93.5 6.9 %all-to-all-done.3.parts = bf16[4,64,576]{2,1,0:T(8,128)(2,1)S(1)} async-done(((bf16[4,64,576]{2,1,0:T(8,128)(2,1)}), bf16[4,64,576]{2,1,0:T(8,128)(2,1)S(1)}, u32[]{:S(2)}, u32[]{:S(2)}) %all-to-all-start.3) | async-done | bytes 294944 | tf_op jit(solution)/shard_map/all_to_all | solution.py:26
  106.3 4.9 %fusion.27 = (bf16[4,576,576]{2,1,0:T(8,128)(2,1)S(1)}, bf16[4,576,576]{2,1,0:T(8,128)(2,1)}) fusion(bf16[4,1152,576]{2,1,0:T(8,128)(2,1)} %bitcast.56), kind=kLoop, calls=%fused_computation.90 | loop fusion | bytes 10616832 | tf_op jit(solution)/shard_map/slice | solution.py:378
  111.2 8.8 %all-to-all-done.4.parts = bf16[4,64,576]{2,1,0:T(8,128)(2,1)S(1)} async-done(((bf16[4,64,576]{2,1,0:T(8,128)(2,1)}), bf16[4,64,576]{2,1,0:T(8,128)(2,1)S(1)}, u32[]{:S(2)}, u32[]{:S(2)}) %all-to-all-start.4) | async-done | bytes 294944 | tf_op jit(solution)/shard_map/all_to_all | solution.py:26
  125.8 9.9 %all-to-all-start.5 = ((bf16[8,8,2432]{2,1,0:T(8,128)(2,1)}), bf16[8,8,2432]{2,1,0:T(8,128)(2,1)}, u32[]{:S(2)}, u32[]{:S(2)}) async-start(bf16[8,8,2432]{2,1,0:T(8,128)(2,1)} %bitcast.54), calls=%async_computation.5 | async-start | bytes 622592 | tf_op jit(solution)/shard_map/all_to_all | solution.py:26
  137.6 5.2 %all-to-all-done.5.got = bf16[8,8,2432]{2,1,0:T(8,128)(2,1)} async-done(((bf16[8,8,2432]{2,1,0:T(8,128)(2,1)}), bf16[8,8,2432]{2,1,0:T(8,128)(2,1)}, u32[]{:S(2)}, u32[]{:S(2)}) %all-to-all-start.5) | async-done | bytes 311328 | tf_op jit(solution)/shard_map/all_to_all | solution.py:26
  145.2 10.8 %all_to_all.71 = bf16[8,8,2304]{2,1,0:T(8,128)(2,1)S(1)} all-to-all(bf16[8,8,2304]{2,1,0:T(8,128)(2,1)S(1)} %get-tuple-element.31), channel_id=1, replica_groups=mesh['a'=4,'h'=2,'l'=2,'x'=4,'y'=4,'c'=2] {'y','c'}, dimensions={0} | all-to-all | bytes 589824 | tf_op jit(solution)/shard_map/all_to_all | solution.py:26
  156.6 14.2 %all_to_all.72.parts = bf16[4,64,576]{2,1,0:T(8,128)(2,1)S(1)} all-to-all(bf16[4,64,576]{2,1,0:T(8,128)(2,1)S(1)} %leave.2), channel_id=1, replica_groups=mesh['a'=4,'h'=2,'l'=2,'x'=4,'y'=4,'c'=2] {'h','l'}, dimensions={0} | all-to-all | bytes 589824 | tf_op jit(solution)/shard_map/all_to_all | solution.py:26
  171.6 4.1 %all-to-all-start.8 = ((bf16[4,64,576]{2,1,0:T(8,128)(2,1)}), bf16[4,64,576]{2,1,0:T(8,128)(2,1)}, u32[]{:S(2)}, u32[]{:S(2)}) async-start(bf16[4,64,576]{2,1,0:T(8,128)(2,1)} %fold.6), calls=%async_computation.8 | async-start | bytes 655360 | tf_op jit(solution)/shard_map/all_to_all | solution.py:26
  175.7 4.9 %fusion.26 = (bf16[4,576,576]{2,1,0:T(8,128)(2,1)S(1)}, bf16[4,576,576]{2,1,0:T(8,128)(2,1)}) fusion(bf16[4,1152,576]{2,1,0:T(8,128)(2,1)} %bitcast.57), kind=kLoop, calls=%fused_computation.89 | loop fusion | bytes 10616832 | tf_op jit(solution)/shard_map/slice | solution.py:378
  180.6 13.3 %all-to-all-done.8.parts = bf16[4,64,576]{2,1,0:T(8,128)(2,1)} async-done(((bf16[4,64,576]{2,1,0:T(8,128)(2,1)}), bf16[4,64,576]{2,1,0:T(8,128)(2,1)}, u32[]{:S(2)}, u32[]{:S(2)}) %all-to-all-start.8) | async-done | bytes 294944 | tf_op jit(solution)/shard_map/all_to_all | solution.py:26
  201.3 11.0 %all_to_all.73.got = bf16[8,8,2432]{2,1,0:T(8,128)(2,1)S(1)} all-to-all(bf16[8,8,2432]{2,1,0:T(8,128)(2,1)S(1)} %bitcast.55), channel_id=1, replica_groups=mesh['a'=4,'h'=2,'l'=2,'x'=4,'y'=4,'c'=2] {'y','c'}, dimensions={0} | all-to-all | bytes 622592 | tf_op jit(solution)/shard_map/all_to_all | solution.py:26
  212.6 10.3 %all_to_all.74 = bf16[8,8,2304]{2,1,0:T(8,128)(2,1)S(1)} all-to-all(bf16[8,8,2304]{2,1,0:T(8,128)(2,1)S(1)} %get-tuple-element.40), channel_id=1, replica_groups=mesh['a'=4,'h'=2,'l'=2,'x'=4,'y'=4,'c'=2] {'y','c'}, dimensions={0} | all-to-all | bytes 589824 | tf_op jit(solution)/shard_map/all_to_all | solution.py:26
  224.3 7.8 %all-to-all-start.11 = ((bf16[4,64,576]{2,1,0:T(8,128)(2,1)}), bf16[4,64,576]{2,1,0:T(8,128)(2,1)S(1)}, u32[]{:S(2)}, u32[]{:S(2)}) async-start(bf16[4,64,576]{2,1,0:T(8,128)(2,1)} %leave.3), calls=%async_computation.11 | async-start | bytes 655360 | tf_op jit(solution)/shard_map/all_to_all | solution.py:26
  232.2 8.7 %all-to-all-done.11.parts = bf16[4,64,576]{2,1,0:T(8,128)(2,1)S(1)} async-done(((bf16[4,64,576]{2,1,0:T(8,128)(2,1)}), bf16[4,64,576]{2,1,0:T(8,128)(2,1)S(1)}, u32[]{:S(2)}, u32[]{:S(2)}) %all-to-all-start.11) | async-done | bytes 294944 | tf_op jit(solution)/shard_map/all_to_all | solution.py:26
  241.6 3.6 %all-to-all-start.12 = ((bf16[4,64,576]{2,1,0:T(8,128)(2,1)}), bf16[4,64,576]{2,1,0:T(8,128)(2,1)S(1)}, u32[]{:S(2)}, u32[]{:S(2)}) async-start(bf16[4,64,576]{2,1,0:T(8,128)(2,1)} %fold.7), calls=%async_computation.12 | async-start | bytes 655360 | tf_op jit(solution)/shard_map/all_to_all | solution.py:26
  245.8 17.0 %all-to-all-done.12.parts = bf16[4,64,576]{2,1,0:T(8,128)(2,1)S(1)} async-done(((bf16[4,64,576]{2,1,0:T(8,128)(2,1)}), bf16[4,64,576]{2,1,0:T(8,128)(2,1)S(1)}, u32[]{:S(2)}, u32[]{:S(2)}) %all-to-all-start.12) | async-done | bytes 294944 | tf_op jit(solution)/shard_map/all_to_all | solution.py:26
  263.9 8.8 %all-to-all-start.13 = ((f32[32,1,136]{2,1,0:T(1,128)}), f32[32,1,136]{2,1,0:T(1,128)S(1)}, u32[]{:S(2)}, u32[]{:S(2)}) async-start(f32[32,1,136]{2,1,0:T(1,128)} %broadcast_in_dim.22), calls=%async_computation.13 | async-start | bytes 65536 | tf_op jit(solution)/shard_map/all_to_all | solution.py:26
  273.4 6.6 %all-to-all-done.13 = f32[32,1,136]{2,1,0:T(1,128)S(1)} async-done(((f32[32,1,136]{2,1,0:T(1,128)}), f32[32,1,136]{2,1,0:T(1,128)S(1)}, u32[]{:S(2)}, u32[]{:S(2)}) %all-to-all-start.13) | async-done | bytes 17440 | tf_op jit(solution)/shard_map/all_to_all | solution.py:26
  (134 shorter events, 46.2 us)
Async XLA Ops:
  7.2 23.0 %copy-start.20 = (s32[3]{0:T(128)S(1)}, s32[3]{0:T(128)}, u32[]{:S(2)}) copy-start(s32[3]{0:T(128)} %param.13) | copy-start | bytes 40
  7.2 23.0 %copy-start.17 = (bf16[4,4,4,576]{3,2,1,0:T(4,128)(2,1)S(1)}, bf16[4,4,4,576]{3,2,1,0:T(4,128)(2,1)}, u32[]{:S(2)}) copy-start(bf16[4,4,4,576]{3,2,1,0:T(4,128)(2,1)} %param.12) | copy-start | bytes 221188
  7.2 23.0 %copy-start.18 = (bf16[4,4,4,576]{3,2,1,0:T(4,128)(2,1)S(1)}, bf16[4,4,4,576]{3,2,1,0:T(4,128)(2,1)}, u32[]{:S(2)}) copy-start(bf16[4,4,4,576]{3,2,1,0:T(4,128)(2,1)} %param.11) | copy-start | bytes 221188
  7.2 23.4 %copy-start.19 = (f32[3,576]{1,0:T(4,128)S(1)}, f32[3,576]{1,0:T(4,128)}, u32[]{:S(2)}) copy-start(f32[3,576]{1,0:T(4,128)} %param.10) | copy-start | bytes 20740
  7.2 99.1 %all-gather.3.cloned.1.call-start = ((), (), s32[]{:S(2)}) async-start(), calls=%async_computation.14 | async-start | bytes 7372800 | tf_op jit(solution)/shard_map/all_gather | solution.py:307
  11.0 33.7 %all-to-all-start = ((bf16[64,2,288]{2,1,0:T(2,128)(2,1)}), bf16[64,2,288]{2,1,0:T(2,128)(2,1)S(1)}, u32[]{:S(2)}, u32[]{:S(2)}) async-start(bf16[64,2,288]{2,1,0:T(2,128)(2,1)} %get-tuple-element.25), calls=%async_computation | async-start | bytes 196608 | tf_op jit(solution)/shard_map/all_to_all | solution.py:26
  46.2 19.5 %all-to-all-start.1 = ((bf16[8,64,704]{2,1,0:T(8,128)(2,1)}), bf16[8,64,704]{2,1,0:T(8,128)(2,1)S(1)}, u32[]{:S(2)}, u32[]{:S(2)}) async-start(bf16[8,64,704]{2,1,0:T(8,128)(2,1)} %first.1), calls=%async_computation.1 | async-start | bytes 1572864 | tf_op jit(solution)/shard_map/all_to_all | solution.py:26
  53.4 122.4 %all-gather.5.cloned.1.call-start = ((), (), s32[]{:S(2)}) async-start(), calls=%async_computation.15 | async-start | bytes 7372800 | tf_op jit(solution)/shard_map/all_gather | solution.py:307
  88.7 11.7 %all-to-all-start.3 = ((bf16[4,64,576]{2,1,0:T(8,128)(2,1)}), bf16[4,64,576]{2,1,0:T(8,128)(2,1)S(1)}, u32[]{:S(2)}, u32[]{:S(2)}) async-start(bf16[4,64,576]{2,1,0:T(8,128)(2,1)} %fold.4), calls=%async_computation.3 | async-start | bytes 655360 | tf_op jit(solution)/shard_map/all_to_all | solution.py:26
  92.3 27.6 %copy-start.9 = (f32[64,128]{1,0:T(8,128)}, f32[64,128]{1,0:T(8,128)S(1)}, u32[]{:S(2)}) copy-start(f32[64,128]{1,0:T(8,128)S(1)} %and_convert_fusion.pick) | copy-start | bytes 98308
  93.5 26.4 %copy-start.3 = (bf16[64,576]{1,0:T(8,128)(2,1)}, bf16[64,576]{1,0:T(8,128)(2,1)S(1)}, u32[]{:S(2)}) copy-start(bf16[64,576]{1,0:T(8,128)(2,1)S(1)} %reshape.181.target) | copy-start | bytes 221188
  101.2 18.7 %all-to-all-start.4 = ((bf16[4,64,576]{2,1,0:T(8,128)(2,1)}), bf16[4,64,576]{2,1,0:T(8,128)(2,1)S(1)}, u32[]{:S(2)}, u32[]{:S(2)}) async-start(bf16[4,64,576]{2,1,0:T(8,128)(2,1)} %fold.5), calls=%async_computation.4 | async-start | bytes 655360 | tf_op jit(solution)/shard_map/all_to_all | solution.py:26
  119.9 1.8 copy-start.1
  125.8 17.0 %all-to-all-start.5 = ((bf16[8,8,2432]{2,1,0:T(8,128)(2,1)}), bf16[8,8,2432]{2,1,0:T(8,128)(2,1)}, u32[]{:S(2)}, u32[]{:S(2)}) async-start(bf16[8,8,2432]{2,1,0:T(8,128)(2,1)} %bitcast.54), calls=%async_computation.5 | async-start | bytes 622592 | tf_op jit(solution)/shard_map/all_to_all | solution.py:26
  142.7 1.1 copy-start.2
  171.6 22.3 %all-to-all-start.8 = ((bf16[4,64,576]{2,1,0:T(8,128)(2,1)}), bf16[4,64,576]{2,1,0:T(8,128)(2,1)}, u32[]{:S(2)}, u32[]{:S(2)}) async-start(bf16[4,64,576]{2,1,0:T(8,128)(2,1)} %fold.6), calls=%async_computation.8 | async-start | bytes 655360 | tf_op jit(solution)/shard_map/all_to_all | solution.py:26
  175.7 18.2 %copy-start.15 = (f32[1,576]{1,0:T(1,128)S(1)}, f32[1,576]{1,0:T(1,128)}, u32[]{:S(2)}) copy-start(f32[1,576]{1,0:T(1,128)} %get-tuple-element.72.gain) | copy-start | bytes 6916
  193.9 1.8 copy-start
  201.3 21.7 %copy-start.11 = (bf16[64,576]{1,0:T(8,128)(2,1)}, bf16[64,576]{1,0:T(8,128)(2,1)S(1)}, u32[]{:S(2)}) copy-start(bf16[64,576]{1,0:T(8,128)(2,1)S(1)} %get-tuple-element.43.before) | copy-start | bytes 221188
  223.0 39.9 %copy-start.5 = (bf16[64,576]{1,0:T(8,128)(2,1)S(1)}, bf16[64,576]{1,0:T(8,128)(2,1)}, u32[]{:S(2)}) copy-start(bf16[64,576]{1,0:T(8,128)(2,1)} %copy-done.3) | copy-start | bytes 221188
  223.0 39.9 %copy-start.12 = (bf16[64,576]{1,0:T(8,128)(2,1)S(1)}, bf16[64,576]{1,0:T(8,128)(2,1)}, u32[]{:S(2)}) copy-start(bf16[64,576]{1,0:T(8,128)(2,1)} %copy-done.11) | copy-start | bytes 221188
  224.3 16.5 %all-to-all-start.11 = ((bf16[4,64,576]{2,1,0:T(8,128)(2,1)}), bf16[4,64,576]{2,1,0:T(8,128)(2,1)S(1)}, u32[]{:S(2)}, u32[]{:S(2)}) async-start(bf16[4,64,576]{2,1,0:T(8,128)(2,1)} %leave.3), calls=%async_computation.11 | async-start | bytes 655360 | tf_op jit(solution)/shard_map/all_to_all | solution.py:26
  241.6 21.3 %all-to-all-start.12 = ((bf16[4,64,576]{2,1,0:T(8,128)(2,1)}), bf16[4,64,576]{2,1,0:T(8,128)(2,1)S(1)}, u32[]{:S(2)}, u32[]{:S(2)}) async-start(bf16[4,64,576]{2,1,0:T(8,128)(2,1)} %fold.7), calls=%async_computation.12 | async-start | bytes 655360 | tf_op jit(solution)/shard_map/all_to_all | solution.py:26
  263.9 16.1 %all-to-all-start.13 = ((f32[32,1,136]{2,1,0:T(1,128)}), f32[32,1,136]{2,1,0:T(1,128)S(1)}, u32[]{:S(2)}, u32[]{:S(2)}) async-start(f32[32,1,136]{2,1,0:T(1,128)} %broadcast_in_dim.22), calls=%async_computation.13 | async-start | bytes 65536 | tf_op jit(solution)/shard_map/all_to_all | solution.py:26
  (8 other events, 6.4 us)
Sparse Core Ops, SparseCore 0:
  11.1 81.2 all-gather.2
  94.5 70.1 all-gather.4

commit v8 on v1

--- a/solution.py
+++ b/solution.py
@@ -9,6 +9,9 @@
 BF = jnp.bfloat16
 F32 = jnp.float32
 SEG = ("y", "c")
+FAR = "a"
+NEAR = ("h", "l", "x")
+DEEP = ("h", "l", FAR)
 EPS = 1e-06
 
 
@@ -47,15 +50,16 @@
 
 
 def local(block, w_in, w_out, gains, fac_left, right_perturb_factors, assign):
-    nz, nx = lax.axis_size("z"), lax.axis_size("x")
+    nf, nn = lax.axis_size(FAR), lax.axis_size(NEAR)
+    nx, nz = lax.axis_size("x"), lax.axis_size(DEEP)
     ns = lax.axis_size("y") * lax.axis_size("c")
     width = block.shape[1]
     hid = w_in.shape[1]
     layers = w_in.shape[0]
     members, _, rank, _ = fac_left.shape
-    tok = nz * nx
+    tok = nf * nn
     rows = tok * members
-    z, x = lax.axis_index("z"), lax.axis_index("x")
+    far, near = lax.axis_index(FAR), lax.axis_index(NEAR)
     seg = lax.axis_index("y") * lax.axis_size("c") + lax.axis_index("c")
 
     lefts = [
@@ -66,12 +70,12 @@
         for i in range(layers)
     ]
 
-    base = share(block[0], ("x", "z"), tok)
-    natural = jnp.swapaxes(base.reshape(nx, nz, width), 0, 1).reshape(tok, width)
+    base = share(block[0], (*NEAR, FAR), tok)
+    natural = jnp.swapaxes(base.reshape(nn, nf, width), 0, 1).reshape(tok, width)
     after = jnp.concatenate([natural[1:], jnp.zeros((1, width), BF)], axis=0)
-    after = jnp.swapaxes(after.reshape(nz, nx, width), 0, 1).reshape(tok, width)
+    after = jnp.swapaxes(after.reshape(nf, nn, width), 0, 1).reshape(tok, width)
     place = jnp.arange(tok)
-    token = (place % nz) * nx + place // nz
+    token = (place % nf) * nn + place // nf
     weighting = jnp.where(token < tok - 1, 1.0 + 2.0 * token.astype(F32) / (tok - 2), 0.0)
     target = jnp.repeat(after, members, axis=0).astype(F32)
     row_weight = jnp.repeat(weighting, members)
@@ -82,10 +86,10 @@
     own_weight = lax.dynamic_slice(row_weight, (seg * chunk,), (chunk,))
     to_member = (own_member[None] == jnp.arange(members)[:, None]).astype(F32)
 
-    my_row = x * nz + z
-    mine = jnp.broadcast_to(block, (members, width))
+    group = nf * members
+    my_row = near * nf + far
     scores = []
-    stream = None
+    stream = jnp.repeat(base, members, axis=0)
     for layer in range(layers):
         gain = gains[layer]
         if layer == 0:
@@ -129,17 +133,24 @@
             gated = jax.nn.silu(scale * (hidden + low)).astype(BF)
             gated = share(gated, SEG, ns).reshape(rows, hid)
         update = jnp.dot(gated, w_out[layer], preferred_element_type=F32).astype(BF)
-        part = swap(update.reshape(nx, rows // nx, width), "x")
-        part = jnp.sum(part.astype(F32), axis=0).astype(BF)
-        part = swap(part.reshape(nz, members, width), "z")
-        mine = (mine.astype(F32) + jnp.sum(part.astype(F32), axis=0)).astype(BF)
         if layer < layers - 1:
-            stream = share(mine, "z", nz).reshape(nz * members, width)
-            stream = share(stream, "x", nx).reshape(rows, width)
+            part = swap(update.reshape(nn, group, width), NEAR)
+            part = jnp.sum(part.astype(F32), axis=0).astype(BF)
+            parts = share(part, FAR, nf).reshape(nf, group, width)
+            held = lax.dynamic_slice(stream, (near * group, 0), (group, width))
+            fresh = (held.astype(F32) + jnp.sum(parts.astype(F32), axis=0)).astype(BF)
+            stream = share(fresh, NEAR, nn).reshape(rows, width)
+        else:
+            part = jnp.swapaxes(update.reshape(nn // nx, nx, group, width), 0, 1)
+            part = swap(part.reshape(nx, rows // nx, width), "x")
+            part = jnp.sum(part.astype(F32), axis=0).astype(BF)
+            part = swap(part.reshape(nz, members, width), DEEP)
+            held = lax.dynamic_slice(stream, (my_row * members, 0), (members, width))
+            mine = (held.astype(F32) + jnp.sum(part.astype(F32), axis=0)).astype(BF)
 
     wide = mine.astype(F32)
     my_target = lax.dynamic_slice(after, (my_row, 0), (1, width)).astype(F32)
-    first = jnp.where((z == 0) & (x == 0), 1.0, 0.0)
+    first = jnp.where(my_row == 0, 1.0, 0.0)
     sums = jnp.concatenate(
         [
             jnp.sum(wide * wide, axis=1),
@@ -150,18 +161,20 @@
     count = nx * ns
     got = share(sums, ("x", *SEG), count).reshape(nx, ns, -1)
     got = jnp.sum(got, axis=1)
-    weights_x = lax.dynamic_slice(weighting.reshape(nx, nz), (0, z), (nx, 1))
+    tokens = far * nn + (near // nx) * nx + jnp.arange(nx)
+    weights_x = jnp.where(tokens < tok - 1, 1.0 + 2.0 * tokens.astype(F32) / (tok - 2), 0.0)
+    weights_x = weights_x[:, None]
     square, along = got[:, :members], got[:, members : 2 * members]
     last = jnp.sum(along * lax.rsqrt(square / D + EPS) * weights_x, axis=0)
     earlier = jnp.sum(got[:, 2 * members :], axis=0)
     both = jnp.concatenate([earlier, last])
-    both = jnp.sum(share(both, "z", nz).reshape(nz, -1), axis=0)
+    both = jnp.sum(share(both, DEEP, nz).reshape(nz, -1), axis=0)
     return both.reshape(layers, members) / math.sqrt((tok - 1) * D), mine[None]
 
 
 def solution(mesh):
-    split = Mesh(mesh.devices.reshape(16, 4, 4, 2), ("z", "x", "y", "c"))
-    pop = ("z", "x")
+    split = Mesh(mesh.devices.reshape(4, 2, 2, 4, 4, 2), (FAR, *NEAR, *SEG))
+    pop = (FAR, *NEAR)
     return jax.shard_map(
         local,
         mesh=split,

time: 289 us -> 272 us (0.941)
  waiting for transfers between devices: 95.6 us -> 80.6 us
  starting transfers between devices: 75.7 us -> 66.7 us
  blocking collectives: 75.8 us -> 84.2 us
    all_to_all x12 -> x10, waiting for transfers between devices: 95.6 us -> 80.6 us  [swap(): return lax.all_to_all(chunks, axes, 0, 0, tiled=True)]
    all_to_all x12 -> x10, starting transfers between devices: 75.7 us -> 66.7 us  [swap(): return lax.all_to_all(chunks, axes, 0, 0, tiled=True)]
    all_to_all x6, blocking collectives: 75.8 us -> 84.2 us  [swap(): return lax.all_to_all(chunks, axes, 0, 0, tiled=True)]
  transfers between devices with their start and end apart: 12 -> 10, of which waited for: 12 -> 10; matrix products, arithmetic and copies ran while one was open for 2% -> 2% of each run, Pallas kernels for 0% -> 0%
where the time goes in v8:
time: 272 us; the launch traced here: 271 us
  blocking collectives  84.2 us (31%)
  waiting for transfers between devices  80.6 us (30%)
  starting transfers between devices  66.7 us (25%)
  local copies, waits for them, and re-layouts  13.9 us (5%)
  matrix products  11.5 us (4%)
  other arithmetic  7.04 us (3%)
  between operations  6.66 us (2%)
    all_to_all x6, blocking collectives, swap(): return lax.all_to_all(chunks, axes, 0, 0, tiled=True)  84.2 us
    all_to_all x10, waiting for transfers between devices, swap(): return lax.all_to_all(chunks, axes, 0, 0, tiled=True)  80.6 us
    all_to_all x10, starting transfers between devices, swap(): return lax.all_to_all(chunks, axes, 0, 0, tiled=True)  66.7 us
  transfers between devices with their start and end apart: 10, of which 10 were waited for; matrix products, arithmetic and copies ran while one was open for 2% of the time, Pallas kernels for 0%

profile of v8, /device:TPU:1, one launch (start us, length us, event | category | flops | bytes accessed | tf_op | source)
XLA Modules:
  0.0 270.5 jit_solution(10346030156699583127)
XLA Ops:
  3.8 19.1 %all-to-all-start = ((bf16[64,2,288]{2,1,0:T(2,128)(2,1)}), bf16[64,2,288]{2,1,0:T(2,128)(2,1)S(1)}, u32[]{:S(2)}, u32[]{:S(2)}) async-start(bf16[64,2,288]{2,1,0:T(2,128)(2,1)} %reshape.379), calls=%async_computation | async-start | bytes 196608 | tf_op jit(solution)/shard_map/all_to_all | solution.py:19
  31.7 5.3 %all-to-all-done = bf16[64,2,288]{2,1,0:T(2,128)(2,1)S(1)} async-done(((bf16[64,2,288]{2,1,0:T(2,128)(2,1)}), bf16[64,2,288]{2,1,0:T(2,128)(2,1)S(1)}, u32[]{:S(2)}, u32[]{:S(2)}) %all-to-all-start) | async-done | bytes 73760 | tf_op jit(solution)/shard_map/all_to_all | solution.py:19
  39.3 18.0 %all_to_all.94 = bf16[8,64,640]{2,1,0:T(8,128)(2,1)S(1)} all-to-all(bf16[8,64,640]{2,1,0:T(8,128)(2,1)S(1)} %broadcast_in_dim.60), channel_id=1, replica_groups=mesh['a'=4,'h'=2,'l'=2,'x'=4,'y'=4,'c'=2] {'y','c'}, dimensions={0} | all-to-all | bytes 1310720 | tf_op jit(solution)/shard_map/all_to_all | solution.py:19
  61.3 13.4 %all_to_all.95 = bf16[16,16,576]{2,1,0:T(8,128)(2,1)S(1)} all-to-all(bf16[16,16,576]{2,1,0:T(8,128)(2,1)S(1)} %bitcast.95), channel_id=1, replica_groups=mesh['a'=4,'h'=2,'l'=2,'x'=4,'y'=4,'c'=2] {'h','l','x'}, dimensions={0} | all-to-all | bytes 589824 | tf_op jit(solution)/shard_map/all_to_all | solution.py:19
  75.4 5.2 %all-to-all-start.3 = ((bf16[4,16,576]{2,1,0:T(8,128)(2,1)}), bf16[4,16,576]{2,1,0:T(8,128)(2,1)S(1)}, u32[]{:S(2)}, u32[]{:S(2)}) async-start(bf16[4,16,576]{2,1,0:T(8,128)(2,1)} %broadcast_in_dim.61), calls=%async_computation.3 | async-start | bytes 163840 | tf_op jit(solution)/shard_map/all_to_all | solution.py:19
  80.9 11.8 %all-to-all-done.3 = bf16[4,16,576]{2,1,0:T(8,128)(2,1)S(1)} async-done(((bf16[4,16,576]{2,1,0:T(8,128)(2,1)}), bf16[4,16,576]{2,1,0:T(8,128)(2,1)S(1)}, u32[]{:S(2)}, u32[]{:S(2)}) %all-to-all-start.3) | async-done | bytes 73760 | tf_op jit(solution)/shard_map/all_to_all | solution.py:19
  93.5 4.1 %all-to-all-start.4 = ((bf16[16,16,576]{2,1,0:T(8,128)(2,1)}), bf16[16,16,576]{2,1,0:T(8,128)(2,1)S(1)}, u32[]{:S(2)}, u32[]{:S(2)}) async-start(bf16[16,16,576]{2,1,0:T(8,128)(2,1)} %broadcast_in_dim.63), calls=%async_computation.4 | async-start | bytes 655360 | tf_op jit(solution)/shard_map/all_to_all | solution.py:19
  98.8 8.4 %all-to-all-done.4 = bf16[16,16,576]{2,1,0:T(8,128)(2,1)S(1)} async-done(((bf16[16,16,576]{2,1,0:T(8,128)(2,1)}), bf16[16,16,576]{2,1,0:T(8,128)(2,1)S(1)}, u32[]{:S(2)}, u32[]{:S(2)}) %all-to-all-start.4) | async-done | bytes 294944 | tf_op jit(solution)/shard_map/all_to_all | solution.py:19
  110.5 7.8 %all-to-all-start.5 = ((bf16[8,32,640]{2,1,0:T(8,128)(2,1)}), bf16[8,32,640]{2,1,0:T(8,128)(2,1)S(1)}, u32[]{:S(2)}, u32[]{:S(2)}) async-start(bf16[8,32,640]{2,1,0:T(8,128)(2,1)} %bitcast.19), calls=%async_computation.5 | async-start | bytes 655360 | tf_op jit(solution)/shard_map/all_to_all | solution.py:19
  118.3 7.1 %all-to-all-done.5 = bf16[8,32,640]{2,1,0:T(8,128)(2,1)S(1)} async-done(((bf16[8,32,640]{2,1,0:T(8,128)(2,1)}), bf16[8,32,640]{2,1,0:T(8,128)(2,1)S(1)}, u32[]{:S(2)}, u32[]{:S(2)}) %all-to-all-start.5) | async-done | bytes 327712 | tf_op jit(solution)/shard_map/all_to_all | solution.py:19
  126.0 11.0 %all_to_all.96 = bf16[8,32,576]{2,1,0:T(8,128)(2,1)S(1)} all-to-all(bf16[8,32,576]{2,1,0:T(8,128)(2,1)S(1)} %broadcast_in_dim.67), channel_id=1, replica_groups=mesh['a'=4,'h'=2,'l'=2,'x'=4,'y'=4,'c'=2] {'y','c'}, dimensions={0} | all-to-all | bytes 589824 | tf_op jit(solution)/shard_map/all_to_all | solution.py:19
  138.8 13.2 %all_to_all.97 = bf16[16,16,576]{2,1,0:T(8,128)(2,1)S(1)} all-to-all(bf16[16,16,576]{2,1,0:T(8,128)(2,1)S(1)} %bitcast.96), channel_id=1, replica_groups=mesh['a'=4,'h'=2,'l'=2,'x'=4,'y'=4,'c'=2] {'h','l','x'}, dimensions={0} | all-to-all | bytes 589824 | tf_op jit(solution)/shard_map/all_to_all | solution.py:19
  152.1 14.4 %all_to_all.98 = bf16[4,16,576]{2,1,0:T(8,128)(2,1)S(1)} all-to-all(bf16[4,16,576]{2,1,0:T(8,128)(2,1)S(1)} %broadcast_in_dim.68), channel_id=1, replica_groups=mesh['a'=4,'h'=2,'l'=2,'x'=4,'y'=4,'c'=2] {'a'}, dimensions={0} | all-to-all | bytes 147456 | tf_op jit(solution)/shard_map/all_to_all | solution.py:19
  167.4 4.1 %all-to-all-start.9 = ((bf16[16,16,576]{2,1,0:T(8,128)(2,1)}), bf16[16,16,576]{2,1,0:T(8,128)(2,1)S(1)}, u32[]{:S(2)}, u32[]{:S(2)}) async-start(bf16[16,16,576]{2,1,0:T(8,128)(2,1)} %broadcast_in_dim.128), calls=%async_computation.9 | async-start | bytes 655360 | tf_op jit(solution)/shard_map/all_to_all | solution.py:19
  171.5 9.5 %all-to-all-done.9 = bf16[16,16,576]{2,1,0:T(8,128)(2,1)S(1)} async-done(((bf16[16,16,576]{2,1,0:T(8,128)(2,1)}), bf16[16,16,576]{2,1,0:T(8,128)(2,1)S(1)}, u32[]{:S(2)}, u32[]{:S(2)}) %all-to-all-start.9) | async-done | bytes 294944 | tf_op jit(solution)/shard_map/all_to_all | solution.py:19
  184.2 8.0 %all-to-all-start.10 = ((bf16[8,32,640]{2,1,0:T(8,128)(2,1)}), bf16[8,32,640]{2,1,0:T(8,128)(2,1)S(1)}, u32[]{:S(2)}, u32[]{:S(2)}) async-start(bf16[8,32,640]{2,1,0:T(8,128)(2,1)} %bitcast.29), calls=%async_computation.10 | async-start | bytes 655360 | tf_op jit(solution)/shard_map/all_to_all | solution.py:19
  192.2 7.1 %all-to-all-done.10 = bf16[8,32,640]{2,1,0:T(8,128)(2,1)S(1)} async-done(((bf16[8,32,640]{2,1,0:T(8,128)(2,1)}), bf16[8,32,640]{2,1,0:T(8,128)(2,1)S(1)}, u32[]{:S(2)}, u32[]{:S(2)}) %all-to-all-start.10) | async-done | bytes 327712 | tf_op jit(solution)/shard_map/all_to_all | solution.py:19
  200.5 4.5 %all-to-all-start.11 = ((bf16[8,32,576]{2,1,0:T(8,128)(2,1)}), bf16[8,32,576]{2,1,0:T(8,128)(2,1)S(1)}, u32[]{:S(2)}, u32[]{:S(2)}) async-start(bf16[8,32,576]{2,1,0:T(8,128)(2,1)} %broadcast_in_dim.131), calls=%async_computation.11 | async-start | bytes 655360 | tf_op jit(solution)/shard_map/all_to_all | solution.py:19
  205.3 6.9 %all-to-all-done.11 = bf16[8,32,576]{2,1,0:T(8,128)(2,1)S(1)} async-done(((bf16[8,32,576]{2,1,0:T(8,128)(2,1)}), bf16[8,32,576]{2,1,0:T(8,128)(2,1)S(1)}, u32[]{:S(2)}, u32[]{:S(2)}) %all-to-all-start.11) | async-done | bytes 294944 | tf_op jit(solution)/shard_map/all_to_all | solution.py:19
  218.4 5.7 %all-to-all-done.12 = bf16[4,64,576]{2,1,0:T(8,128)(2,1)S(1)} async-done(((bf16[4,64,576]{2,1,0:T(8,128)(2,1)}), bf16[4,64,576]{2,1,0:T(8,128)(2,1)S(1)}, u32[]{:S(2)}, u32[]{:S(2)}) %all-to-all-start.12) | async-done | bytes 294944 | tf_op jit(solution)/shard_map/all_to_all | solution.py:19
  228.3 11.7 %all-to-all-done.13 = bf16[16,4,576]{2,1,0:T(4,128)(2,1)S(1)} async-done(((bf16[16,4,576]{2,1,0:T(4,128)(2,1)}), bf16[16,4,576]{2,1,0:T(4,128)(2,1)S(1)}, u32[]{:S(2)}, u32[]{:S(2)}) %all-to-all-start.13) | async-done | bytes 73760 | tf_op jit(solution)/shard_map/all_to_all | solution.py:19
  241.5 6.9 %all-to-all-start.14 = ((f32[32,1,16]{2,1,0:T(1,128)}), f32[32,1,16]{2,1,0:T(1,128)S(1)}, u32[]{:S(2)}, u32[]{:S(2)}) async-start(f32[32,1,16]{2,1,0:T(1,128)} %broadcast_in_dim.134), calls=%async_computation.14 | async-start | bytes 32768 | tf_op jit(solution)/shard_map/all_to_all | solution.py:19
  248.5 7.0 %all-to-all-done.14 = f32[32,1,16]{2,1,0:T(1,128)S(1)} async-done(((f32[32,1,16]{2,1,0:T(1,128)}), f32[32,1,16]{2,1,0:T(1,128)S(1)}, u32[]{:S(2)}, u32[]{:S(2)}) %all-to-all-start.14) | async-done | bytes 2080 | tf_op jit(solution)/shard_map/all_to_all | solution.py:19
  255.8 14.0 %all_to_all.99 = f32[16,1,12]{2,1,0:T(1,128)S(1)} all-to-all(f32[16,1,12]{2,1,0:T(1,128)S(1)} %broadcast_in_dim.136), channel_id=1, replica_groups=mesh['a'=4,'h'=2,'l'=2,'x'=4,'y'=4,'c'=2] {'h','l','a'}, dimensions={0} | all-to-all | bytes 1536 | tf_op jit(solution)/shard_map/all_to_all | solution.py:19
  (118 shorter events, 39.4 us)
Async XLA Ops:
  3.8 33.2 %all-to-all-start = ((bf16[64,2,288]{2,1,0:T(2,128)(2,1)}), bf16[64,2,288]{2,1,0:T(2,128)(2,1)S(1)}, u32[]{:S(2)}, u32[]{:S(2)}) async-start(bf16[64,2,288]{2,1,0:T(2,128)(2,1)} %reshape.379), calls=%async_computation | async-start | bytes 196608 | tf_op jit(solution)/shard_map/all_to_all | solution.py:19
  75.4 17.3 %all-to-all-start.3 = ((bf16[4,16,576]{2,1,0:T(8,128)(2,1)}), bf16[4,16,576]{2,1,0:T(8,128)(2,1)S(1)}, u32[]{:S(2)}, u32[]{:S(2)}) async-start(bf16[4,16,576]{2,1,0:T(8,128)(2,1)} %broadcast_in_dim.61), calls=%async_computation.3 | async-start | bytes 163840 | tf_op jit(solution)/shard_map/all_to_all | solution.py:19
  93.5 13.7 %all-to-all-start.4 = ((bf16[16,16,576]{2,1,0:T(8,128)(2,1)}), bf16[16,16,576]{2,1,0:T(8,128)(2,1)S(1)}, u32[]{:S(2)}, u32[]{:S(2)}) async-start(bf16[16,16,576]{2,1,0:T(8,128)(2,1)} %broadcast_in_dim.63), calls=%async_computation.4 | async-start | bytes 655360 | tf_op jit(solution)/shard_map/all_to_all | solution.py:19
  110.5 15.0 %all-to-all-start.5 = ((bf16[8,32,640]{2,1,0:T(8,128)(2,1)}), bf16[8,32,640]{2,1,0:T(8,128)(2,1)S(1)}, u32[]{:S(2)}, u32[]{:S(2)}) async-start(bf16[8,32,640]{2,1,0:T(8,128)(2,1)} %bitcast.19), calls=%async_computation.5 | async-start | bytes 655360 | tf_op jit(solution)/shard_map/all_to_all | solution.py:19
  167.4 13.6 %all-to-all-start.9 = ((bf16[16,16,576]{2,1,0:T(8,128)(2,1)}), bf16[16,16,576]{2,1,0:T(8,128)(2,1)S(1)}, u32[]{:S(2)}, u32[]{:S(2)}) async-start(bf16[16,16,576]{2,1,0:T(8,128)(2,1)} %broadcast_in_dim.128), calls=%async_computation.9 | async-start | bytes 655360 | tf_op jit(solution)/shard_map/all_to_all | solution.py:19
  184.2 15.1 %all-to-all-start.10 = ((bf16[8,32,640]{2,1,0:T(8,128)(2,1)}), bf16[8,32,640]{2,1,0:T(8,128)(2,1)S(1)}, u32[]{:S(2)}, u32[]{:S(2)}) async-start(bf16[8,32,640]{2,1,0:T(8,128)(2,1)} %bitcast.29), calls=%async_computation.10 | async-start | bytes 655360 | tf_op jit(solution)/shard_map/all_to_all | solution.py:19
  200.5 11.6 %all-to-all-start.11 = ((bf16[8,32,576]{2,1,0:T(8,128)(2,1)}), bf16[8,32,576]{2,1,0:T(8,128)(2,1)S(1)}, u32[]{:S(2)}, u32[]{:S(2)}) async-start(bf16[8,32,576]{2,1,0:T(8,128)(2,1)} %broadcast_in_dim.131), calls=%async_computation.11 | async-start | bytes 655360 | tf_op jit(solution)/shard_map/all_to_all | solution.py:19
  214.7 9.4 %all-to-all-start.12 = ((bf16[4,64,576]{2,1,0:T(8,128)(2,1)}), bf16[4,64,576]{2,1,0:T(8,128)(2,1)S(1)}, u32[]{:S(2)}, u32[]{:S(2)}) async-start(bf16[4,64,576]{2,1,0:T(8,128)(2,1)} %bitcast.35), calls=%async_computation.12 | async-start | bytes 655360 | tf_op jit(solution)/shard_map/all_to_all | solution.py:19
  224.8 15.2 %all-to-all-start.13 = ((bf16[16,4,576]{2,1,0:T(4,128)(2,1)}), bf16[16,4,576]{2,1,0:T(4,128)(2,1)S(1)}, u32[]{:S(2)}, u32[]{:S(2)}) async-start(bf16[16,4,576]{2,1,0:T(4,128)(2,1)} %reshape.229), calls=%async_computation.13 | async-start | bytes 163840 | tf_op jit(solution)/shard_map/all_to_all | solution.py:19
  241.5 14.0 %all-to-all-start.14 = ((f32[32,1,16]{2,1,0:T(1,128)}), f32[32,1,16]{2,1,0:T(1,128)S(1)}, u32[]{:S(2)}, u32[]{:S(2)}) async-start(f32[32,1,16]{2,1,0:T(1,128)} %broadcast_in_dim.134), calls=%async_computation.14 | async-start | bytes 32768 | tf_op jit(solution)/shard_map/all_to_all | solution.py:19

commit v9 on v8

v9 whole, which is shorter than its diff:
```python
import functools
import math

import jax
import jax.numpy as jnp
from jax import lax
from jax.experimental import pallas as pl
from jax.experimental.pallas import tpu as pltpu
from jax.sharding import Mesh, PartitionSpec as P

D = 4608
BF = jnp.bfloat16
F32 = jnp.float32
SEG = ("y", "c")
FAR = "a"
NEAR = ("h", "l", "x")
EPS = 1e-06
HALF = 32
SIDE = 2 * HALF
TILE = 128
MIB = 1 << 20


def swap(chunks, axes):
    return lax.all_to_all(chunks, axes, 0, 0, tiled=True)


def share(value, axes, count):
    return swap(jnp.broadcast_to(value[None], (count, *value.shape)), axes)


def dot_t(a, b):
    return lax.dot_general(a, b, (((1,), (1,)), ((), ())), preferred_element_type=F32)


def kernel_call(body, out_shape, name, *given):
    vmem = pl.BlockSpec(memory_space=pltpu.VMEM)
    return pl.pallas_call(
        body,
        out_shape=out_shape,
        in_specs=[vmem] * len(given),
        out_specs=jax.tree.map(lambda _: vmem, out_shape),
        compiler_params=pltpu.CompilerParams(vmem_limit_bytes=12 * MIB),
        name=name,
    )(*given)


def with_sides(full, square, along, pick, low_lanes):
    tile = full[:, :TILE]
    lane = lax.broadcasted_iota(jnp.int32, tile.shape, 1)
    place = lane % HALF
    sides = tile if pick is None else tile * pick
    sides = jnp.where(place == low_lanes, square, sides)
    if along is not None:
        sides = jnp.where(place == low_lanes + 1, along, sides)
    high = sides.astype(BF).astype(F32)
    sides = jnp.where(lane < HALF, high, sides - high)
    return jnp.where(lane < SIDE, sides, tile).astype(BF)


def first_kernel(low_lanes, stream, gain, weight, out):
    wide = stream[...].astype(F32)
    full = dot_t((wide * gain[...]).astype(BF), weight[...])
    square = jnp.sum(wide * wide, axis=1, keepdims=True)
    tile = with_sides(full, square, None, None, low_lanes)
    rest = full[:, TILE:].astype(BF)
    for i in range(out.shape[0]):
        out[i, :, :TILE] = tile
        out[i, :, TILE:] = rest


def first(stream, gain, weight, low_lanes, count):
    shape = jax.ShapeDtypeStruct((count, stream.shape[0], weight.shape[0]), BF)
    return kernel_call(
        functools.partial(first_kernel, low_lanes), shape, "first", stream, gain, weight
    )


def enter_kernel(low_lanes, stream, gain, target, pick, weight, out):
    wide = stream[...].astype(F32)
    full = dot_t((wide * gain[...]).astype(BF), weight[...])
    square = jnp.sum(wide * wide, axis=1, keepdims=True)
    along = jnp.sum(wide * target[...].astype(F32), axis=1, keepdims=True)
    out[:, :TILE] = with_sides(full, square, along, pick[...], low_lanes)
    out[:, TILE:] = full[:, TILE:].astype(BF)


def enter(stream, gain, target, pick, weight, low_lanes):
    shape = jax.ShapeDtypeStruct((stream.shape[0], weight.shape[0]), BF)
    return kernel_call(
        functools.partial(enter_kernel, low_lanes),
        shape,
        "enter",
        stream,
        gain,
        target,
        pick,
        weight,
    )


def middle_kernel(low_lanes, got, right, out, side):
    total = got[0].astype(F32)
    for i in range(1, got.shape[0]):
        total += got[i].astype(F32)
    extras = total[:, :TILE]
    lane = lax.broadcasted_iota(jnp.int32, extras.shape, 1)
    extras = jnp.where(lane < SIDE, extras, 0.0)
    place = lane % HALF
    square = jnp.sum(jnp.where(place == low_lanes, extras, 0.0), axis=1, keepdims=True)
    along = jnp.sum(jnp.where(place == low_lanes + 1, extras, 0.0), axis=1, keepdims=True)
    scale = lax.rsqrt(square / D + EPS)
    side[...] = jnp.broadcast_to(along * scale, side.shape)
    low = jnp.zeros(total.shape, F32)
    left = extras
    for _ in range(3):
        piece = left.astype(BF)
        low += jnp.dot(piece, right[...], preferred_element_type=F32)
        left = left - piece.astype(F32)
    mixed = scale * (total + low)
    gated = mixed / (1.0 + jnp.exp(-mixed))
    tile = jnp.where(lane < SIDE, 0.0, gated[:, :TILE]).astype(BF)
    rest = gated[:, TILE:].astype(BF)
    for i in range(out.shape[0]):
        out[i, :, :TILE] = tile
        out[i, :, TILE:] = rest


def middle(got, right, low_lanes):
    shapes = (
        jax.ShapeDtypeStruct(got.shape, BF),
        jax.ShapeDtypeStruct((got.shape[1], TILE), F32),
    )
    return kernel_call(functools.partial(middle_kernel, low_lanes), shapes, "middle", got, right)


def leave_kernel(gated, weight, out):
    out[...] = jnp.dot(gated[...], weight[...], preferred_element_type=F32).astype(BF)


def leave(gated, weight):
    shape = jax.ShapeDtypeStruct((gated.shape[0], weight.shape[1]), BF)
    return kernel_call(leave_kernel, shape, "leave", gated, weight)


def twice(factors):
    return jnp.pad(
        jnp.concatenate([jnp.pad(factors, ((0, HALF - factors.shape[0]), (0, 0))), factors]),
        ((0, HALF - factors.shape[0]), (0, 0)),
    )


def local(block, w_in, w_out, gains, fac_left, right_perturb_factors, assign):
    nf, nn = lax.axis_size(FAR), lax.axis_size(NEAR)
    nx = lax.axis_size("x")
    ns = lax.axis_size("y") * lax.axis_size("c")
    width = block.shape[1]
    hid = w_in.shape[1]
    layers = w_in.shape[0]
    members, _, rank, _ = fac_left.shape
    tok = nf * nn
    rows = tok * members
    far, near = lax.axis_index(FAR), lax.axis_index(NEAR)
    seg = lax.axis_index("y") * lax.axis_size("c") + lax.axis_index("c")

    low_lanes = members * rank
    chosen = (jnp.arange(fac_left.shape[1])[None] == assign[:, None]).astype(F32)

    def section(factors, layer):
        picked = jnp.sum(factors.astype(F32) * chosen[layer][None, :, None, None], axis=1)
        return picked.astype(BF).reshape(low_lanes, factors.shape[-1])

    stacked_in = [
        jnp.concatenate([twice(section(fac_left, i)), w_in[i]], axis=0) for i in range(layers)
    ]
    stacked_out = [jnp.pad(w_out[i], ((SIDE, 0), (0, 0))) for i in range(layers)]
    rights = [section(right_perturb_factors, i) for i in range(layers)]
    padded_right = [
        jnp.pad(twice(r), ((0, TILE - SIDE), (SIDE, 0))) for r in rights
    ]

    base = share(block[0], (*NEAR, FAR), tok)
    natural = jnp.swapaxes(base.reshape(nn, nf, width), 0, 1).reshape(tok, width)
    after = jnp.concatenate([natural[1:], jnp.zeros((1, width), BF)], axis=0)
    after = jnp.swapaxes(after.reshape(nf, nn, width), 0, 1).reshape(tok, width)
    place = jnp.arange(tok)
    token = (place % nf) * nn + place // nf
    weighting = jnp.where(token < tok - 1, 1.0 + 2.0 * token.astype(F32) / (tok - 2), 0.0)
    target = jnp.repeat(after, members, axis=0)
    row_weight = jnp.repeat(weighting, members)
    row_member = jnp.arange(rows) % members
    lane = jnp.arange(TILE)
    pick = (row_member[:, None] == (lane % HALF // rank)[None]) & (lane % HALF < low_lanes)[None]
    pick = pick.astype(F32)
    chunk = rows // ns
    own_member = jnp.arange(chunk) % members
    own_weight = lax.dynamic_slice(row_weight, (seg * chunk,), (chunk,))
    to_member = (own_member[None] == jnp.arange(members)[:, None]).astype(F32)

    group = nf * members
    scores = []
    stream = jnp.repeat(base, members, axis=0)
    for layer in range(layers):
        gain = gains[layer]
        if layer == 0:
            parts = swap(first(base, gain[None], stacked_in[0], low_lanes, ns), SEG)
            total = jnp.sum(parts.astype(F32), axis=0)
            extras = total[:, :HALF] + total[:, HALF:SIDE]
            hidden = total[:, SIDE:]
            scale = lax.rsqrt(extras[:, low_lanes : low_lanes + 1] / D + EPS)
            low = extras[:, :low_lanes].reshape(tok, members, rank)
            mixed = scale[:, None] * (
                hidden[:, None]
                + jnp.einsum(
                    "tmr,mrf->tmf",
                    low,
                    rights[0].reshape(members, rank, hid).astype(F32),
                    precision=lax.Precision.HIGHEST,
                )
            )
            gated = jax.nn.silu(mixed).astype(BF).reshape(rows, hid)
            update = jnp.dot(gated, w_out[layer], preferred_element_type=F32).astype(BF)
        else:
            part = enter(stream, gain[None], target, pick, stacked_in[layer], low_lanes)
            part = swap(part.reshape(ns, chunk, -1), SEG)
            gated, side = middle(part, padded_right[layer], low_lanes)
            scores.append(jnp.sum(to_member * (side[:, 0] * own_weight), axis=1))
            update = leave(swap(gated, SEG).reshape(rows, -1), stacked_out[layer])
        part = swap(update.reshape(nn, group, width), NEAR)
        part = jnp.sum(part.astype(F32), axis=0).astype(BF)
        parts = share(part, FAR, nf).reshape(nf, group, width)
        held = lax.dynamic_slice(stream, (near * group, 0), (group, width))
        fresh = (held.astype(F32) + jnp.sum(parts.astype(F32), axis=0)).astype(BF)
        if layer < layers - 1:
            stream = share(fresh, NEAR, nn).reshape(rows, width)

    wide = fresh.astype(F32)
    own_target = lax.dynamic_slice(target, (near * group, 0), (group, width)).astype(F32)
    once = jnp.where(near == 0, 1.0, 0.0)
    sums = jnp.concatenate(
        [
            jnp.sum(wide * wide, axis=1),
            jnp.sum(wide * own_target, axis=1),
            *[once * s for s in scores],
        ]
    )
    got = share(sums, ("x", *SEG), nx * ns).reshape(nx, ns, -1)
    got = jnp.sum(got, axis=1)
    square, along = got[:, :group], got[:, group : 2 * group]
    near_here = near // nx * nx + jnp.arange(nx)
    tokens = (jnp.arange(group) // members)[None] * nn + near_here[:, None]
    weights = jnp.where(tokens < tok - 1, 1.0 + 2.0 * tokens.astype(F32) / (tok - 2), 0.0)
    each = along * lax.rsqrt(square / D + EPS) * weights
    latest = jnp.sum(each.reshape(nx * nf, members), axis=0)
    both = jnp.concatenate([jnp.sum(got[:, 2 * group :], axis=0), latest])
    both = jnp.sum(share(both, ("h", "l"), nn // nx).reshape(nn // nx, -1), axis=0)
    mine = lax.dynamic_slice(fresh.reshape(nf, members, width), (far, 0, 0), (1, members, width))
    return both.reshape(layers, members) / math.sqrt((tok - 1) * D), mine


def solution(mesh):
    split = Mesh(mesh.devices.reshape(4, 2, 2, 4, 4, 2), (FAR, *NEAR, *SEG))
    pop = (FAR, *NEAR)
    return jax.shard_map(
        local,
        mesh=split,
        in_specs=(
            P(pop, SEG),
            P(None, pop, SEG),
            P(None, pop, SEG),
            P(None, SEG),
            P(None, None, None, SEG),
            P(None, None, None, pop),
            P(),
        ),
        out_specs=(P(), P(pop, None, SEG)),
        check_vma=False,
    )
```

time: 272 us -> 260 us (0.956)
  blocking collectives: 84.2 us -> 58.8 us
  waiting for transfers between devices: 80.6 us -> 98.7 us
  matrix products: 11.5 us -> 2.19 us
  Pallas kernels: 0 us -> 6.28 us
  starting transfers between devices: 66.7 us -> 72.8 us
  between operations: 6.66 us -> 1.1 us
    all_to_all x6 -> x4, blocking collectives: 84.2 us -> 58.8 us  [swap(): return lax.all_to_all(chunks, axes, 0, 0, tiled=True)]
    all_to_all x10 -> x12, waiting for transfers between devices: 80.6 us -> 98.7 us  [swap(): return lax.all_to_all(chunks, axes, 0, 0, tiled=True)]
    pallas_call x0 -> x7, Pallas kernels: none -> 6.28 us  [kernel_call(): pl.pallas_call(body, out_shape=out_shape, in_specs=[vmem] * len(given), o...]
    all_to_all x10 -> x12, starting transfers between devices: 66.7 us -> 72.8 us  [swap(): return lax.all_to_all(chunks, axes, 0, 0, tiled=True)]
    dot_general x9 -> x1, matrix products: 6.73 us -> 0.6 us  [local(): jnp.einsum('tmr,mrf->tmf', low, rights[0].reshape(members, rank, hid).ast...]
    squeeze x0 -> x2, local copies, waits for them, and re-layouts: none -> 3.22 us  [the longest x1 1.76 us: local(): w_in[i]]
    dot_general x3 -> x1, matrix products: 4.79 us -> 1.59 us  [local(): update = jnp.dot(gated, w_out[layer], preferred_element_type=F32).astype(BF)]
  transfers between devices with their start and end apart: 10 -> 12, of which waited for: 10 -> 12; matrix products, arithmetic and copies ran while one was open for 2% -> 3% of each run, Pallas kernels for 0% -> 0%
where the time goes in v9:
time: 260 us; the launch traced here: 258 us
  waiting for transfers between devices  98.7 us (38%)
  starting transfers between devices  72.8 us (28%)
  blocking collectives  58.8 us (23%)
  local copies, waits for them, and re-layouts  12.3 us (5%)
  Pallas kernels  6.28 us (2%)
  other arithmetic  6.13 us (2%)
    all_to_all x12, waiting for transfers between devices, swap(): return lax.all_to_all(chunks, axes, 0, 0, tiled=True)  98.7 us
    all_to_all x12, starting transfers between devices, swap(): return lax.all_to_all(chunks, axes, 0, 0, tiled=True)  72.8 us
    all_to_all x4, blocking collectives, swap(): return lax.all_to_all(chunks, axes, 0, 0, tiled=True)  58.8 us
    pallas_call x7, Pallas kernels, kernel_call(): pl.pallas_call(body, out_shape=out_shape, in_specs=[vmem] * len(given), o...  6.28 us
  transfers between devices with their start and end apart: 12, of which 12 were waited for; matrix products, arithmetic and copies ran while one was open for 3% of the time, Pallas kernels for 0%

profile of v9, /device:TPU:1, one launch (start us, length us, event | category | flops | bytes accessed | tf_op | source)
XLA Modules:
  0.0 258.4 jit_solution(5302439755310071726)
XLA Ops:
  3.8 19.1 %all-to-all-start = ((bf16[64,2,288]{2,1,0:T(2,128)(2,1)}), bf16[64,2,288]{2,1,0:T(2,128)(2,1)S(1)}, u32[]{:S(2)}, u32[]{:S(2)}) async-start(bf16[64,2,288]{2,1,0:T(2,128)(2,1)} %reshape.208), calls=%async_computation | async-start | bytes 196608 | tf_op jit(solution)/shard_map/all_to_all | solution.py:25
  26.9 10.1 %all-to-all-done = bf16[64,2,288]{2,1,0:T(2,128)(2,1)S(1)} async-done(((bf16[64,2,288]{2,1,0:T(2,128)(2,1)}), bf16[64,2,288]{2,1,0:T(2,128)(2,1)S(1)}, u32[]{:S(2)}, u32[]{:S(2)}) %all-to-all-start) | async-done | bytes 73760 | tf_op jit(solution)/shard_map/all_to_all | solution.py:25
  37.6 18.0 %all_to_all.85 = bf16[8,64,640]{2,1,0:T(8,128)(2,1)S(1)} all-to-all(bf16[8,64,640]{2,1,0:T(8,128)(2,1)S(1)} %first.1), channel_id=1, replica_groups=mesh['a'=4,'h'=2,'l'=2,'x'=4,'y'=4,'c'=2] {'y','c'}, dimensions={0} | all-to-all | bytes 1310720 | tf_op jit(solution)/shard_map/all_to_all | solution.py:25
  59.0 13.5 %all_to_all.86 = bf16[16,16,576]{2,1,0:T(8,128)(2,1)S(1)} all-to-all(bf16[16,16,576]{2,1,0:T(8,128)(2,1)S(1)} %bitcast.62), channel_id=1, replica_groups=mesh['a'=4,'h'=2,'l'=2,'x'=4,'y'=4,'c'=2] {'h','l','x'}, dimensions={0} | all-to-all | bytes 589824 | tf_op jit(solution)/shard_map/all_to_all | solution.py:25
  73.1 4.1 %all-to-all-start.3 = ((bf16[4,16,576]{2,1,0:T(8,128)(2,1)}), bf16[4,16,576]{2,1,0:T(8,128)(2,1)S(1)}, u32[]{:S(2)}, u32[]{:S(2)}) async-start(bf16[4,16,576]{2,1,0:T(8,128)(2,1)} %broadcast_in_dim.31), calls=%async_computation.3 | async-start | bytes 163840 | tf_op jit(solution)/shard_map/all_to_all | solution.py:25
  77.4 11.8 %all-to-all-done.3 = bf16[4,16,576]{2,1,0:T(8,128)(2,1)S(1)} async-done(((bf16[4,16,576]{2,1,0:T(8,128)(2,1)}), bf16[4,16,576]{2,1,0:T(8,128)(2,1)S(1)}, u32[]{:S(2)}, u32[]{:S(2)}) %all-to-all-start.3) | async-done | bytes 73760 | tf_op jit(solution)/shard_map/all_to_all | solution.py:25
  90.0 4.1 %all-to-all-start.4 = ((bf16[16,16,576]{2,1,0:T(8,128)(2,1)}), bf16[16,16,576]{2,1,0:T(8,128)(2,1)S(1)}, u32[]{:S(2)}, u32[]{:S(2)}) async-start(bf16[16,16,576]{2,1,0:T(8,128)(2,1)} %broadcast_in_dim.32), calls=%async_computation.4 | async-start | bytes 655360 | tf_op jit(solution)/shard_map/all_to_all | solution.py:25
  95.4 8.4 %all-to-all-done.4 = bf16[16,16,576]{2,1,0:T(8,128)(2,1)S(1)} async-done(((bf16[16,16,576]{2,1,0:T(8,128)(2,1)}), bf16[16,16,576]{2,1,0:T(8,128)(2,1)S(1)}, u32[]{:S(2)}, u32[]{:S(2)}) %all-to-all-start.4) | async-done | bytes 294944 | tf_op jit(solution)/shard_map/all_to_all | solution.py:25
  104.9 7.8 %all-to-all-start.5 = ((bf16[8,32,640]{2,1,0:T(8,128)(2,1)}), bf16[8,32,640]{2,1,0:T(8,128)(2,1)S(1)}, u32[]{:S(2)}, u32[]{:S(2)}) async-start(bf16[8,32,640]{2,1,0:T(8,128)(2,1)} %bitcast.13), calls=%async_computation.5 | async-start | bytes 655360 | tf_op jit(solution)/shard_map/all_to_all | solution.py:25
  112.9 7.0 %all-to-all-done.5.got = bf16[8,32,640]{2,1,0:T(8,128)(2,1)S(1)} async-done(((bf16[8,32,640]{2,1,0:T(8,128)(2,1)}), bf16[8,32,640]{2,1,0:T(8,128)(2,1)S(1)}, u32[]{:S(2)}, u32[]{:S(2)}) %all-to-all-start.5) | async-done | bytes 327712 | tf_op jit(solution)/shard_map/all_to_all | solution.py:25
  120.8 4.5 %all-to-all-start.6 = ((bf16[8,32,640]{2,1,0:T(8,128)(2,1)}), bf16[8,32,640]{2,1,0:T(8,128)(2,1)S(1)}, u32[]{:S(2)}, u32[]{:S(2)}) async-start(bf16[8,32,640]{2,1,0:T(8,128)(2,1)} %get-tuple-element.6), calls=%async_computation.6 | async-start | bytes 655360 | tf_op jit(solution)/shard_map/all_to_all | solution.py:25
  126.8 5.6 %all-to-all-done.6 = bf16[8,32,640]{2,1,0:T(8,128)(2,1)S(1)} async-done(((bf16[8,32,640]{2,1,0:T(8,128)(2,1)}), bf16[8,32,640]{2,1,0:T(8,128)(2,1)S(1)}, u32[]{:S(2)}, u32[]{:S(2)}) %all-to-all-start.6) | async-done | bytes 327712 | tf_op jit(solution)/shard_map/all_to_all | solution.py:25
  132.9 12.8 %all_to_all.87 = bf16[16,16,576]{2,1,0:T(8,128)(2,1)S(1)} all-to-all(bf16[16,16,576]{2,1,0:T(8,128)(2,1)S(1)} %bitcast.59), channel_id=1, replica_groups=mesh['a'=4,'h'=2,'l'=2,'x'=4,'y'=4,'c'=2] {'h','l','x'}, dimensions={0} | all-to-all | bytes 589824 | tf_op jit(solution)/shard_map/all_to_all | solution.py:25
  145.7 14.6 %all_to_all.88 = bf16[4,16,576]{2,1,0:T(8,128)(2,1)S(1)} all-to-all(bf16[4,16,576]{2,1,0:T(8,128)(2,1)S(1)} %broadcast_in_dim.34), channel_id=1, replica_groups=mesh['a'=4,'h'=2,'l'=2,'x'=4,'y'=4,'c'=2] {'a'}, dimensions={0} | all-to-all | bytes 147456 | tf_op jit(solution)/shard_map/all_to_all | solution.py:25
  161.1 4.3 %all-to-all-start.9 = ((bf16[16,16,576]{2,1,0:T(8,128)(2,1)}), bf16[16,16,576]{2,1,0:T(8,128)(2,1)S(1)}, u32[]{:S(2)}, u32[]{:S(2)}) async-start(bf16[16,16,576]{2,1,0:T(8,128)(2,1)} %broadcast_in_dim.35), calls=%async_computation.9 | async-start | bytes 655360 | tf_op jit(solution)/shard_map/all_to_all | solution.py:25
  165.6 9.3 %all-to-all-done.9 = bf16[16,16,576]{2,1,0:T(8,128)(2,1)S(1)} async-done(((bf16[16,16,576]{2,1,0:T(8,128)(2,1)}), bf16[16,16,576]{2,1,0:T(8,128)(2,1)S(1)}, u32[]{:S(2)}, u32[]{:S(2)}) %all-to-all-start.9) | async-done | bytes 294944 | tf_op jit(solution)/shard_map/all_to_all | solution.py:25
  176.1 7.5 %all-to-all-start.10 = ((bf16[8,32,640]{2,1,0:T(8,128)(2,1)}), bf16[8,32,640]{2,1,0:T(8,128)(2,1)S(1)}, u32[]{:S(2)}, u32[]{:S(2)}) async-start(bf16[8,32,640]{2,1,0:T(8,128)(2,1)} %bitcast.20), calls=%async_computation.10 | async-start | bytes 655360 | tf_op jit(solution)/shard_map/all_to_all | solution.py:25
  183.7 7.0 %all-to-all-done.10.got = bf16[8,32,640]{2,1,0:T(8,128)(2,1)S(1)} async-done(((bf16[8,32,640]{2,1,0:T(8,128)(2,1)}), bf16[8,32,640]{2,1,0:T(8,128)(2,1)S(1)}, u32[]{:S(2)}, u32[]{:S(2)}) %all-to-all-start.10) | async-done | bytes 327712 | tf_op jit(solution)/shard_map/all_to_all | solution.py:25
  191.6 4.5 %all-to-all-start.11 = ((bf16[8,32,640]{2,1,0:T(8,128)(2,1)}), bf16[8,32,640]{2,1,0:T(8,128)(2,1)S(1)}, u32[]{:S(2)}, u32[]{:S(2)}) async-start(bf16[8,32,640]{2,1,0:T(8,128)(2,1)} %get-tuple-element.7), calls=%async_computation.11 | async-start | bytes 655360 | tf_op jit(solution)/shard_map/all_to_all | solution.py:25
  196.2 7.1 %all-to-all-done.11 = bf16[8,32,640]{2,1,0:T(8,128)(2,1)S(1)} async-done(((bf16[8,32,640]{2,1,0:T(8,128)(2,1)}), bf16[8,32,640]{2,1,0:T(8,128)(2,1)S(1)}, u32[]{:S(2)}, u32[]{:S(2)}) %all-to-all-start.11) | async-done | bytes 327712 | tf_op jit(solution)/shard_map/all_to_all | solution.py:25
  208.7 9.7 %all-to-all-done.12 = bf16[16,16,576]{2,1,0:T(8,128)(2,1)S(1)} async-done(((bf16[16,16,576]{2,1,0:T(8,128)(2,1)}), bf16[16,16,576]{2,1,0:T(8,128)(2,1)S(1)}, u32[]{:S(2)}, u32[]{:S(2)}) %all-to-all-start.12) | async-done | bytes 294944 | tf_op jit(solution)/shard_map/all_to_all | solution.py:25
  222.4 12.0 %all-to-all-done.13 = bf16[4,16,576]{2,1,0:T(8,128)(2,1)S(1)} async-done(((bf16[4,16,576]{2,1,0:T(8,128)(2,1)}), bf16[4,16,576]{2,1,0:T(8,128)(2,1)S(1)}, u32[]{:S(2)}, u32[]{:S(2)}) %all-to-all-start.13) | async-done | bytes 73760 | tf_op jit(solution)/shard_map/all_to_all | solution.py:25
  235.2 6.9 %all-to-all-start.14 = ((f32[32,1,40]{2,1,0:T(1,128)}), f32[32,1,40]{2,1,0:T(1,128)S(1)}, u32[]{:S(2)}, u32[]{:S(2)}) async-start(f32[32,1,40]{2,1,0:T(1,128)} %broadcast_in_dim.39), calls=%async_computation.14 | async-start | bytes 32768 | tf_op jit(solution)/shard_map/all_to_all | solution.py:25
  242.2 7.0 %all-to-all-done.14 = f32[32,1,40]{2,1,0:T(1,128)S(1)} async-done(((f32[32,1,40]{2,1,0:T(1,128)}), f32[32,1,40]{2,1,0:T(1,128)S(1)}, u32[]{:S(2)}, u32[]{:S(2)}) %all-to-all-start.14) | async-done | bytes 5152 | tf_op jit(solution)/shard_map/all_to_all | solution.py:25
  (107 shorter events, 40.6 us)
Async XLA Ops:
  3.8 33.2 %all-to-all-start = ((bf16[64,2,288]{2,1,0:T(2,128)(2,1)}), bf16[64,2,288]{2,1,0:T(2,128)(2,1)S(1)}, u32[]{:S(2)}, u32[]{:S(2)}) async-start(bf16[64,2,288]{2,1,0:T(2,128)(2,1)} %reshape.208), calls=%async_computation | async-start | bytes 196608 | tf_op jit(solution)/shard_map/all_to_all | solution.py:25
  25.0 1.9 copy-start
  73.1 16.2 %all-to-all-start.3 = ((bf16[4,16,576]{2,1,0:T(8,128)(2,1)}), bf16[4,16,576]{2,1,0:T(8,128)(2,1)S(1)}, u32[]{:S(2)}, u32[]{:S(2)}) async-start(bf16[4,16,576]{2,1,0:T(8,128)(2,1)} %broadcast_in_dim.31), calls=%async_computation.3 | async-start | bytes 163840 | tf_op jit(solution)/shard_map/all_to_all | solution.py:25
  90.0 13.7 %all-to-all-start.4 = ((bf16[16,16,576]{2,1,0:T(8,128)(2,1)}), bf16[16,16,576]{2,1,0:T(8,128)(2,1)S(1)}, u32[]{:S(2)}, u32[]{:S(2)}) async-start(bf16[16,16,576]{2,1,0:T(8,128)(2,1)} %broadcast_in_dim.32), calls=%async_computation.4 | async-start | bytes 655360 | tf_op jit(solution)/shard_map/all_to_all | solution.py:25
  104.9 15.0 %all-to-all-start.5 = ((bf16[8,32,640]{2,1,0:T(8,128)(2,1)}), bf16[8,32,640]{2,1,0:T(8,128)(2,1)S(1)}, u32[]{:S(2)}, u32[]{:S(2)}) async-start(bf16[8,32,640]{2,1,0:T(8,128)(2,1)} %bitcast.13), calls=%async_computation.5 | async-start | bytes 655360 | tf_op jit(solution)/shard_map/all_to_all | solution.py:25
  120.8 11.6 %all-to-all-start.6 = ((bf16[8,32,640]{2,1,0:T(8,128)(2,1)}), bf16[8,32,640]{2,1,0:T(8,128)(2,1)S(1)}, u32[]{:S(2)}, u32[]{:S(2)}) async-start(bf16[8,32,640]{2,1,0:T(8,128)(2,1)} %get-tuple-element.6), calls=%async_computation.6 | async-start | bytes 655360 | tf_op jit(solution)/shard_map/all_to_all | solution.py:25
  161.1 13.8 %all-to-all-start.9 = ((bf16[16,16,576]{2,1,0:T(8,128)(2,1)}), bf16[16,16,576]{2,1,0:T(8,128)(2,1)S(1)}, u32[]{:S(2)}, u32[]{:S(2)}) async-start(bf16[16,16,576]{2,1,0:T(8,128)(2,1)} %broadcast_in_dim.35), calls=%async_computation.9 | async-start | bytes 655360 | tf_op jit(solution)/shard_map/all_to_all | solution.py:25
  176.1 14.6 %all-to-all-start.10 = ((bf16[8,32,640]{2,1,0:T(8,128)(2,1)}), bf16[8,32,640]{2,1,0:T(8,128)(2,1)S(1)}, u32[]{:S(2)}, u32[]{:S(2)}) async-start(bf16[8,32,640]{2,1,0:T(8,128)(2,1)} %bitcast.20), calls=%async_computation.10 | async-start | bytes 655360 | tf_op jit(solution)/shard_map/all_to_all | solution.py:25
  191.6 11.6 %all-to-all-start.11 = ((bf16[8,32,640]{2,1,0:T(8,128)(2,1)}), bf16[8,32,640]{2,1,0:T(8,128)(2,1)S(1)}, u32[]{:S(2)}, u32[]{:S(2)}) async-start(bf16[8,32,640]{2,1,0:T(8,128)(2,1)} %get-tuple-element.7), calls=%async_computation.11 | async-start | bytes 655360 | tf_op jit(solution)/shard_map/all_to_all | solution.py:25
  204.4 13.9 %all-to-all-start.12 = ((bf16[16,16,576]{2,1,0:T(8,128)(2,1)}), bf16[16,16,576]{2,1,0:T(8,128)(2,1)S(1)}, u32[]{:S(2)}, u32[]{:S(2)}) async-start(bf16[16,16,576]{2,1,0:T(8,128)(2,1)} %bitcast.23), calls=%async_computation.12 | async-start | bytes 655360 | tf_op jit(solution)/shard_map/all_to_all | solution.py:25
  219.0 15.4 %all-to-all-start.13 = ((bf16[4,16,576]{2,1,0:T(8,128)(2,1)}), bf16[4,16,576]{2,1,0:T(8,128)(2,1)S(1)}, u32[]{:S(2)}, u32[]{:S(2)}) async-start(bf16[4,16,576]{2,1,0:T(8,128)(2,1)} %broadcast_in_dim.36), calls=%async_computation.13 | async-start | bytes 163840 | tf_op jit(solution)/shard_map/all_to_all | solution.py:25
  235.2 14.0 %all-to-all-start.14 = ((f32[32,1,40]{2,1,0:T(1,128)}), f32[32,1,40]{2,1,0:T(1,128)S(1)}, u32[]{:S(2)}, u32[]{:S(2)}) async-start(f32[32,1,40]{2,1,0:T(1,128)} %broadcast_in_dim.39), calls=%async_computation.14 | async-start | bytes 32768 | tf_op jit(solution)/shard_map/all_to_all | solution.py:25
  250.2 7.5 %all-to-all-start.15 = ((f32[4,1,12]{2,1,0:T(1,128)}), f32[4,1,12]{2,1,0:T(1,128)S(1)}, u32[]{:S(2)}, u32[]{:S(2)}) async-start(f32[4,1,12]{2,1,0:T(1,128)} %broadcast_in_dim.41), calls=%async_computation.15 | async-start | bytes 4096 | tf_op jit(solution)/shard_map/all_to_all | solution.py:25
